TPU v7x, 32 devices: a whole 2x2x4 slice. The times are simulated.
32 devices in a mesh: grp: 2 (over x), had: 16 (over z, y, core).
Axes of the slice: x: 2, y: 2, z: 4, core: 2. Of those that a mesh axis runs over, the one named last changes fastest.
Arguments:
- source_slabs: bfloat16 [512, 128, 128], P(('grp', 'had')), parts along dimension 0, may hold values from -6 to 6
- sink_slabs: bfloat16 [512, 128, 128], P(('grp', 'had')), parts along dimension 0, may hold values from -6 to 6
- perambulators: bfloat16 [4, 2, 128, 128], P('grp'), parts along dimension 0, may hold values from -0.5 to 0.5
- send_pick: int32 [32, 16], P(('grp', 'had')), parts along dimension 0, may hold values from 0 to 15
- graph_slot: int32 [32, 512, 2], P(('grp', 'had')), parts along dimension 0, may hold values from 0 to 15
- graph_sink: int32 [32, 512, 2], P(('grp', 'had')), parts along dimension 0, may hold values from 0 to 15
- graph_count: int32 [32], P(('grp', 'had')), parts along dimension 0, may hold values from 64 to 512, as said below
- pair_list: int32 [256, 2], P(('grp', 'had')), parts along dimension 0, may hold values from 0 to 15
Outputs:
- edge_matrices: bfloat16 [32, 128, 128], P(('grp', 'had')), parts along dimension 0
- pair_products: bfloat16 [256, 128, 128], P(('grp', 'had')), parts along dimension 0
There are 2 independent parts, one for each index of `grp`. A program takes and returns all parts, laid end to end along the dimension named above; each array names one. Nothing has to cross between parts.
Inputs may be any that keep to these rules, and one draw needn't show every extreme that they name: Some reader uses all 512 graph slots; slots from graph_count on are unused.
All inputs are finite; a program needn't handle non-finite values.
Results may differ from a plain program's by a relative error of at most 0.012.
Values may be sent and summed in bfloat16 or wider, within the bound.
No kernel may reach another device: no remote copies, remote signals or barrier semaphores. Data moves between devices by JAX's collectives and lax.ppermute only.
A program may use at most 64 MiB of HBM per device.

v0:
```python
import math

import jax
import jax.numpy as jnp
from jax import lax
from jax.sharding import PartitionSpec as P


def shards(
    source_slabs,
    sink_slabs,
    perambulators,
    send_pick,
    graph_slot,
    graph_sink,
    graph_count,
    pair_list,
):
    my_index = lax.axis_index("had")
    evecs = source_slabs.shape[1]
    per_device = source_slabs.shape[0]
    root_scale = 1.0 / math.sqrt(evecs)
    edge_scale = 1.0 / math.sqrt(evecs * graph_slot.shape[1])
    timeslice = my_index * per_device // evecs
    local_peram = lax.dynamic_index_in_dim(perambulators, timeslice, 0, keepdims=False)
    first_turn = jnp.einsum(
        "xa,jab->xjb", local_peram[0], source_slabs, preferred_element_type=jnp.float32
    ).astype(jnp.bfloat16)
    pick_row = send_pick[0]
    second_turn = jnp.einsum(
        "xjb,yb->xjy", first_turn, local_peram[1], preferred_element_type=jnp.float32
    ).astype(jnp.bfloat16)
    outgoing = jnp.take(second_turn, pick_row, axis=1)
    received = lax.all_to_all(outgoing, "had", split_axis=1, concat_axis=1, tiled=True)
    graph_rows = graph_slot.shape[1]
    block_width = min(64, graph_rows)
    slot_table = graph_slot[0]
    sink_table = graph_sink[0]
    graph_total = graph_count[0]

    def factor(slots, sinks):
        gathered = jnp.take(received, slots, axis=1)
        resident = jnp.take(sink_slabs, sinks, axis=0)
        product = jnp.einsum("gxb,agb->gxa", resident, gathered, preferred_element_type=jnp.float32)
        return (product * root_scale).astype(jnp.bfloat16)

    def accumulate(block_index, running_sum):
        offset = block_index * block_width
        slots = lax.dynamic_slice_in_dim(slot_table, offset, block_width, 0)
        sinks = lax.dynamic_slice_in_dim(sink_table, offset, block_width, 0)
        is_valid = (offset + jnp.arange(block_width, dtype=jnp.int32) < graph_total).astype(
            jnp.bfloat16
        )
        left_side = factor(slots[:, 0], sinks[:, 0]) * is_valid[:, None, None]
        right_side = factor(slots[:, 1], sinks[:, 1])
        return running_sum + jnp.einsum(
            "gxa,gay->xy", left_side, right_side, preferred_element_type=jnp.float32
        )

    block_count = (graph_total + block_width - 1) // block_width
    summed = lax.fori_loop(0, block_count, accumulate, jnp.zeros((evecs, evecs), jnp.float32))
    edge_local = (summed * edge_scale).astype(jnp.bfloat16)[None]
    left_ids = pair_list[:, 0]
    right_ids = pair_list[:, 1]
    shard_rows = lax.all_gather(edge_local, "had", axis=0, tiled=True)
    row_ids = jnp.arange(shard_rows.shape[0], dtype=jnp.int32)
    left_select = (left_ids[:, None] == row_ids[None, :]).astype(jnp.bfloat16)
    right_select = (right_ids[:, None] == row_ids[None, :]).astype(jnp.bfloat16)
    left_part = jnp.einsum(
        "pn,nxy->pxy", left_select, shard_rows, preferred_element_type=jnp.float32
    )
    right_part = jnp.einsum(
        "pn,nxy->pxy", right_select, shard_rows, preferred_element_type=jnp.float32
    )
    left_edges = left_part.astype(jnp.bfloat16)
    right_edges = right_part.astype(jnp.bfloat16)
    product = jnp.einsum(
        "pxa,pay->pxy", left_edges, right_edges, preferred_element_type=jnp.float32
    )
    pair_products = (product * root_scale).astype(jnp.bfloat16)
    return (edge_local, pair_products)


def solution(mesh):
    return jax.shard_map(
        shards,
        mesh=mesh,
        in_specs=(
            P(("grp", "had"), None, None),
            P(("grp", "had"), None, None),
            P("grp", None, None, None),
            P(("grp", "had"), None),
            P(("grp", "had"), None, None),
            P(("grp", "had"), None, None),
            P(("grp", "had")),
            P(("grp", "had"), None),
        ),
        out_specs=(P(("grp", "had"), None, None), P(("grp", "had"), None, None)),
        check_vma=False,
    )
```

profile of v0, /device:TPU:0, one launch (start us, length us, event | category | flops | bytes accessed | tf_op | source)
XLA Modules:
  0.0 210.8 jit_solution(10187311681063074676)
XLA Ops:
  5.0 7.4 %all-to-all-start = ((bf16[128,16,128]{2,0,1:T(8,128)(2,1)}), bf16[128,16,128]{2,0,1:T(8,128)(2,1)S(1)}, u32[]{:S(2)}, u32[]{:S(2)}) async-start(bf16[128,16,128]{2,0,1:T(8,128)(2,1)} %select_bitcast_fusion), calls=%async_computation | async-start | bytes 1048576 | tf_op jit(solution)/shard_map/all_to_all | solution.py:34
  13.1 13.8 %all-to-all-done = bf16[128,16,128]{2,0,1:T(8,128)(2,1)S(1)} async-done(((bf16[128,16,128]{2,0,1:T(8,128)(2,1)}), bf16[128,16,128]{2,0,1:T(8,128)(2,1)S(1)}, u32[]{:S(2)}, u32[]{:S(2)}) %all-to-all-start) | async-done | bytes 524320 | tf_op jit(solution)/shard_map/all_to_all | solution.py:34
  26.8 162.8 %while.10 = (s32[]{:T(128)}, f32[128,128]{1,0:T(8,128)S(1)}, s32[]{:T(128)}, s32[512,2]{0,1:T(2,128)}, bf16[16,128,128]{2,1,0:T(8,128)(2,1)S(1)}, /*index=5*/s32...) while((s32[]{:T(128)}, f32[128,128]{1,0:T(8,128)S(1)}, ...), condition=%wide.region_1.4_spmd, body=%wide.region_0.3_spmd.sunk | while | flops 814765760 | bytes 29514672 | solution.py:61
  29.8 2.1 %gather_fusion.1 = bf16[64,128,128]{2,1,0:T(8,128)(2,1)} fusion(bf16[16,128,128]{2,1,0:T(8,128)(2,1)S(1)} %get-tuple-element.186, s32[1024]{0:T(1024)S(1)} %pad_clamp_fusion.10), kind=kCustom, calls=%fused_computation.2.clone.clone.1 | custom fusion | bytes 4194560 | tf_op jit(solution)/shard_map/while/body/jit(_take)/gather | solution.py:43
  32.0 5.2 %multiply_convert_fusion.4 = bf16[64,128,128]{2,1,0:T(8,128)(2,1)} fusion(bf16[64,128,128]{2,1,0:T(8,128)(2,1)} %gather_fusion, bf16[64,128,128]{2,1,0:T(8,128)(2,1)} %gather_fusion.1, pred[64]{0:T(512)(128)(4,1)S(1)} %get-tuple-element.152, pred[64]{0:T(512)(128)(4,1)S(1)} %get-tuple-element.153), kind=kOutput, calls=%fused_computation.5.clone.1 | convolution fusion | flops 272629760 | bytes 6291584 | tf_op jit(solution)/shard_map/while/body/gxb,agb->gxa/dot_general | solution.py:44
  42.1 5.1 %fusion.64 = f32[128,128]{1,0:T(8,128)S(1)} fusion(f32[128,128]{1,0:T(8,128)S(1)} %get-tuple-element.171, bf16[64,128,128]{2,1,0:T(8,128)(2,1)} %multiply_convert_fusion.4, bf16[64,128,128]{2,1,0:T(8,128)(2,1)} %gather_fusion.2, bf16[64,128,128]{2,1,0:T(8,128)(2,1)} %gather_fusion.3, pred[64]{0:T(512)(128)(4,1)S(1)} %get-tuple-element.156, ...), kind=kOutput, calls=%fused_computation.20.clone.1 | convolution fusion | flops 542130176 | bytes 6422784 | tf_op jit(solution)/shard_map/while/body/gxa,gay->xy/dot_general | solution.py:56
  50.2 2.1 %gather_fusion.1 = bf16[64,128,128]{2,1,0:T(8,128)(2,1)} fusion(bf16[16,128,128]{2,1,0:T(8,128)(2,1)S(1)} %get-tuple-element.186, s32[1024]{0:T(1024)S(1)} %pad_clamp_fusion.10), kind=kCustom, calls=%fused_computation.2.clone.clone.1 | custom fusion | bytes 4194560 | tf_op jit(solution)/shard_map/while/body/jit(_take)/gather | solution.py:43
  52.3 5.2 %multiply_convert_fusion.4 = bf16[64,128,128]{2,1,0:T(8,128)(2,1)} fusion(bf16[64,128,128]{2,1,0:T(8,128)(2,1)} %gather_fusion, bf16[64,128,128]{2,1,0:T(8,128)(2,1)} %gather_fusion.1, pred[64]{0:T(512)(128)(4,1)S(1)} %get-tuple-element.152, pred[64]{0:T(512)(128)(4,1)S(1)} %get-tuple-element.153), kind=kOutput, calls=%fused_computation.5.clone.1 | convolution fusion | flops 272629760 | bytes 6291584 | tf_op jit(solution)/shard_map/while/body/gxb,agb->gxa/dot_general | solution.py:44
  62.5 5.1 %fusion.64 = f32[128,128]{1,0:T(8,128)S(1)} fusion(f32[128,128]{1,0:T(8,128)S(1)} %get-tuple-element.171, bf16[64,128,128]{2,1,0:T(8,128)(2,1)} %multiply_convert_fusion.4, bf16[64,128,128]{2,1,0:T(8,128)(2,1)} %gather_fusion.2, bf16[64,128,128]{2,1,0:T(8,128)(2,1)} %gather_fusion.3, pred[64]{0:T(512)(128)(4,1)S(1)} %get-tuple-element.156, ...), kind=kOutput, calls=%fused_computation.20.clone.1 | convolution fusion | flops 542130176 | bytes 6422784 | tf_op jit(solution)/shard_map/while/body/gxa,gay->xy/dot_general | solution.py:56
  70.5 2.1 %gather_fusion.1 = bf16[64,128,128]{2,1,0:T(8,128)(2,1)} fusion(bf16[16,128,128]{2,1,0:T(8,128)(2,1)S(1)} %get-tuple-element.186, s32[1024]{0:T(1024)S(1)} %pad_clamp_fusion.10), kind=kCustom, calls=%fused_computation.2.clone.clone.1 | custom fusion | bytes 4194560 | tf_op jit(solution)/shard_map/while/body/jit(_take)/gather | solution.py:43
  72.7 5.2 %multiply_convert_fusion.4 = bf16[64,128,128]{2,1,0:T(8,128)(2,1)} fusion(bf16[64,128,128]{2,1,0:T(8,128)(2,1)} %gather_fusion, bf16[64,128,128]{2,1,0:T(8,128)(2,1)} %gather_fusion.1, pred[64]{0:T(512)(128)(4,1)S(1)} %get-tuple-element.152, pred[64]{0:T(512)(128)(4,1)S(1)} %get-tuple-element.153), kind=kOutput, calls=%fused_computation.5.clone.1 | convolution fusion | flops 272629760 | bytes 6291584 | tf_op jit(solution)/shard_map/while/body/gxb,agb->gxa/dot_general | solution.py:44
  82.8 5.1 %fusion.64 = f32[128,128]{1,0:T(8,128)S(1)} fusion(f32[128,128]{1,0:T(8,128)S(1)} %get-tuple-element.171, bf16[64,128,128]{2,1,0:T(8,128)(2,1)} %multiply_convert_fusion.4, bf16[64,128,128]{2,1,0:T(8,128)(2,1)} %gather_fusion.2, bf16[64,128,128]{2,1,0:T(8,128)(2,1)} %gather_fusion.3, pred[64]{0:T(512)(128)(4,1)S(1)} %get-tuple-element.156, ...), kind=kOutput, calls=%fused_computation.20.clone.1 | convolution fusion | flops 542130176 | bytes 6422784 | tf_op jit(solution)/shard_map/while/body/gxa,gay->xy/dot_general | solution.py:56
  90.9 2.1 %gather_fusion.1 = bf16[64,128,128]{2,1,0:T(8,128)(2,1)} fusion(bf16[16,128,128]{2,1,0:T(8,128)(2,1)S(1)} %get-tuple-element.186, s32[1024]{0:T(1024)S(1)} %pad_clamp_fusion.10), kind=kCustom, calls=%fused_computation.2.clone.clone.1 | custom fusion | bytes 4194560 | tf_op jit(solution)/shard_map/while/body/jit(_take)/gather | solution.py:43
  93.0 5.2 %multiply_convert_fusion.4 = bf16[64,128,128]{2,1,0:T(8,128)(2,1)} fusion(bf16[64,128,128]{2,1,0:T(8,128)(2,1)} %gather_fusion, bf16[64,128,128]{2,1,0:T(8,128)(2,1)} %gather_fusion.1, pred[64]{0:T(512)(128)(4,1)S(1)} %get-tuple-element.152, pred[64]{0:T(512)(128)(4,1)S(1)} %get-tuple-element.153), kind=kOutput, calls=%fused_computation.5.clone.1 | convolution fusion | flops 272629760 | bytes 6291584 | tf_op jit(solution)/shard_map/while/body/gxb,agb->gxa/dot_general | solution.py:44
  103.2 5.1 %fusion.64 = f32[128,128]{1,0:T(8,128)S(1)} fusion(f32[128,128]{1,0:T(8,128)S(1)} %get-tuple-element.171, bf16[64,128,128]{2,1,0:T(8,128)(2,1)} %multiply_convert_fusion.4, bf16[64,128,128]{2,1,0:T(8,128)(2,1)} %gather_fusion.2, bf16[64,128,128]{2,1,0:T(8,128)(2,1)} %gather_fusion.3, pred[64]{0:T(512)(128)(4,1)S(1)} %get-tuple-element.156, ...), kind=kOutput, calls=%fused_computation.20.clone.1 | convolution fusion | flops 542130176 | bytes 6422784 | tf_op jit(solution)/shard_map/while/body/gxa,gay->xy/dot_general | solution.py:56
  113.4 5.2 %multiply_convert_fusion.4 = bf16[64,128,128]{2,1,0:T(8,128)(2,1)} fusion(bf16[64,128,128]{2,1,0:T(8,128)(2,1)} %gather_fusion, bf16[64,128,128]{2,1,0:T(8,128)(2,1)} %gather_fusion.1, pred[64]{0:T(512)(128)(4,1)S(1)} %get-tuple-element.152, pred[64]{0:T(512)(128)(4,1)S(1)} %get-tuple-element.153), kind=kOutput, calls=%fused_computation.5.clone.1 | convolution fusion | flops 272629760 | bytes 6291584 | tf_op jit(solution)/shard_map/while/body/gxb,agb->gxa/dot_general | solution.py:44
  123.5 5.1 %fusion.64 = f32[128,128]{1,0:T(8,128)S(1)} fusion(f32[128,128]{1,0:T(8,128)S(1)} %get-tuple-element.171, bf16[64,128,128]{2,1,0:T(8,128)(2,1)} %multiply_convert_fusion.4, bf16[64,128,128]{2,1,0:T(8,128)(2,1)} %gather_fusion.2, bf16[64,128,128]{2,1,0:T(8,128)(2,1)} %gather_fusion.3, pred[64]{0:T(512)(128)(4,1)S(1)} %get-tuple-element.156, ...), kind=kOutput, calls=%fused_computation.20.clone.1 | convolution fusion | flops 542130176 | bytes 6422784 | tf_op jit(solution)/shard_map/while/body/gxa,gay->xy/dot_general | solution.py:56
  133.7 5.2 %multiply_convert_fusion.4 = bf16[64,128,128]{2,1,0:T(8,128)(2,1)} fusion(bf16[64,128,128]{2,1,0:T(8,128)(2,1)} %gather_fusion, bf16[64,128,128]{2,1,0:T(8,128)(2,1)} %gather_fusion.1, pred[64]{0:T(512)(128)(4,1)S(1)} %get-tuple-element.152, pred[64]{0:T(512)(128)(4,1)S(1)} %get-tuple-element.153), kind=kOutput, calls=%fused_computation.5.clone.1 | convolution fusion | flops 272629760 | bytes 6291584 | tf_op jit(solution)/shard_map/while/body/gxb,agb->gxa/dot_general | solution.py:44
  143.9 5.1 %fusion.64 = f32[128,128]{1,0:T(8,128)S(1)} fusion(f32[128,128]{1,0:T(8,128)S(1)} %get-tuple-element.171, bf16[64,128,128]{2,1,0:T(8,128)(2,1)} %multiply_convert_fusion.4, bf16[64,128,128]{2,1,0:T(8,128)(2,1)} %gather_fusion.2, bf16[64,128,128]{2,1,0:T(8,128)(2,1)} %gather_fusion.3, pred[64]{0:T(512)(128)(4,1)S(1)} %get-tuple-element.156, ...), kind=kOutput, calls=%fused_computation.20.clone.1 | convolution fusion | flops 542130176 | bytes 6422784 | tf_op jit(solution)/shard_map/while/body/gxa,gay->xy/dot_general | solution.py:56
  154.1 5.2 %multiply_convert_fusion.4 = bf16[64,128,128]{2,1,0:T(8,128)(2,1)} fusion(bf16[64,128,128]{2,1,0:T(8,128)(2,1)} %gather_fusion, bf16[64,128,128]{2,1,0:T(8,128)(2,1)} %gather_fusion.1, pred[64]{0:T(512)(128)(4,1)S(1)} %get-tuple-element.152, pred[64]{0:T(512)(128)(4,1)S(1)} %get-tuple-element.153), kind=kOutput, calls=%fused_computation.5.clone.1 | convolution fusion | flops 272629760 | bytes 6291584 | tf_op jit(solution)/shard_map/while/body/gxb,agb->gxa/dot_general | solution.py:44
  164.2 5.1 %fusion.64 = f32[128,128]{1,0:T(8,128)S(1)} fusion(f32[128,128]{1,0:T(8,128)S(1)} %get-tuple-element.171, bf16[64,128,128]{2,1,0:T(8,128)(2,1)} %multiply_convert_fusion.4, bf16[64,128,128]{2,1,0:T(8,128)(2,1)} %gather_fusion.2, bf16[64,128,128]{2,1,0:T(8,128)(2,1)} %gather_fusion.3, pred[64]{0:T(512)(128)(4,1)S(1)} %get-tuple-element.156, ...), kind=kOutput, calls=%fused_computation.20.clone.1 | convolution fusion | flops 542130176 | bytes 6422784 | tf_op jit(solution)/shard_map/while/body/gxa,gay->xy/dot_general | solution.py:56
  174.4 5.2 %multiply_convert_fusion.4 = bf16[64,128,128]{2,1,0:T(8,128)(2,1)} fusion(bf16[64,128,128]{2,1,0:T(8,128)(2,1)} %gather_fusion, bf16[64,128,128]{2,1,0:T(8,128)(2,1)} %gather_fusion.1, pred[64]{0:T(512)(128)(4,1)S(1)} %get-tuple-element.152, pred[64]{0:T(512)(128)(4,1)S(1)} %get-tuple-element.153), kind=kOutput, calls=%fused_computation.5.clone.1 | convolution fusion | flops 272629760 | bytes 6291584 | tf_op jit(solution)/shard_map/while/body/gxb,agb->gxa/dot_general | solution.py:44
  184.6 5.1 %fusion.64 = f32[128,128]{1,0:T(8,128)S(1)} fusion(f32[128,128]{1,0:T(8,128)S(1)} %get-tuple-element.171, bf16[64,128,128]{2,1,0:T(8,128)(2,1)} %multiply_convert_fusion.4, bf16[64,128,128]{2,1,0:T(8,128)(2,1)} %gather_fusion.2, bf16[64,128,128]{2,1,0:T(8,128)(2,1)} %gather_fusion.3, pred[64]{0:T(512)(128)(4,1)S(1)} %get-tuple-element.156, ...), kind=kOutput, calls=%fused_computation.20.clone.1 | convolution fusion | flops 542130176 | bytes 6422784 | tf_op jit(solution)/shard_map/while/body/gxa,gay->xy/dot_general | solution.py:56
  190.3 18.8 %all-gather = bf16[2048,128]{1,0:T(8,128)(2,1)S(1)} all-gather(bf16[128,128]{1,0:T(8,128)(2,1)S(1)} %multiply_convert_fusion.2), channel_id=2, replica_groups=mesh['grp'=2,'had'=16] {'had'}, dimensions={0}, use_global_device_ids=true | all-gather | bytes 557056 | tf_op jit(solution)/shard_map/all_gather | solution.py:65
  (111 shorter events, 78.0 us)
Async XLA Ops:
  0.6 1.4 copy-start
  2.1 11.0 %copy-start.2 = (s32[8,2]{0,1:T(2,128)S(1)}, s32[8,2]{0,1:T(2,128)}, u32[]{:S(2)}) copy-start(s32[8,2]{0,1:T(2,128)} %param.21) | copy-start | bytes 196
  2.1 24.8 %copy-start.1 = (bf16[16,128,128]{2,1,0:T(8,128)(2,1)S(1)}, bf16[16,128,128]{2,1,0:T(8,128)(2,1)}, u32[]{:S(2)}) copy-start(bf16[16,128,128]{2,1,0:T(8,128)(2,1)} %param.15) | copy-start | bytes 1572868
  5.0 21.9 %all-to-all-start = ((bf16[128,16,128]{2,0,1:T(8,128)(2,1)}), bf16[128,16,128]{2,0,1:T(8,128)(2,1)S(1)}, u32[]{:S(2)}, u32[]{:S(2)}) async-start(bf16[128,16,128]{2,0,1:T(8,128)(2,1)} %select_bitcast_fusion), calls=%async_computation | async-start | bytes 1048576 | tf_op jit(solution)/shard_map/all_to_all | solution.py:34
where the time goes:
time: 212 us; the launch traced here: 211 us
  matrix products  85.4 us (40%)
  local copies, waits for them, and re-layouts  75.1 us (35%)
  blocking collectives  18.8 us (9%)
  waiting for transfers between devices  13.8 us (7%)
  other arithmetic  8.44 us (4%)
  starting transfers between devices  7.38 us (3%)
    dot_general x8, matrix products, factor(): jnp.einsum('gxb,agb->gxa', resident, gathered, preferred_element_type=jnp...  41.7 us
    dot_general x8, matrix products, accumulate(): jnp.einsum('gxa,gay->xy', left_side, right_side, preferred_element_type=j...  40.7 us
    gather x16, local copies, waits for them, and re-layouts, factor(): resident = jnp.take(sink_slabs, sinks, axis=0)  34.1 us
    gather x16, local copies, waits for them, and re-layouts, factor(): gathered = jnp.take(received, slots, axis=1)  34.1 us
    all_gather x1, blocking collectives, shards(): shard_rows = lax.all_gather(edge_local, 'had', axis=0, tiled=True)  18.8 us
    all_to_all x1, waiting for transfers between devices, shards(): lax.all_to_all(outgoing, 'had', split_axis=1, concat_axis=1, tiled=True)  13.8 us
    all_to_all x1, starting transfers between devices, shards(): lax.all_to_all(outgoing, 'had', split_axis=1, concat_axis=1, tiled=True)  7.38 us
    dynamic_slice x8, local copies, waits for them, and re-layouts, accumulate(): slots = lax.dynamic_slice_in_dim(slot_table, offset, block_width, 0)  6.18 us
  transfers between devices with their start and end apart: 1, of which 1 were waited for; matrix products, arithmetic and copies ran while one was open for 0% of the time, Pallas kernels for 0%

commit v1 on v0

v1 whole, which is shorter than its diff:
```python
import functools
import math

import jax
import jax.numpy as jnp
from jax import lax
from jax.experimental import pallas as pl
from jax.experimental.pallas import tpu as pltpu
from jax.sharding import PartitionSpec as P

BF16 = jnp.bfloat16
F32 = jnp.float32
VMEM = pl.BlockSpec(memory_space=pltpu.VMEM)
SMEM = pl.BlockSpec(memory_space=pltpu.SMEM)
HBM = pl.BlockSpec(memory_space=pltpu.HBM)


def times_transposed(left, right):
    return lax.dot_general(left, right, (((1,), (1,)), ((), ())), preferred_element_type=F32)


def rotate_kernel(pick_hbm, source_hbm, peram_hbm, out_ref, pick_ref, source_ref, peram_ref, rotated_ref, sems):
    per_device, evecs, _ = source_ref.shape
    readers = out_ref.shape[0]
    timeslice = lax.axis_index("had") * per_device // evecs
    copies = [
        pltpu.make_async_copy(peram_hbm.at[timeslice], peram_ref, sems.at[0]),
        pltpu.make_async_copy(source_hbm, source_ref, sems.at[1]),
        pltpu.make_async_copy(pick_hbm, pick_ref, sems.at[2]),
    ]
    for copy in copies:
        copy.start()
    for copy in copies:
        copy.wait()
    group = math.gcd(4, per_device)
    for j in range(0, per_device, group):
        side_by_side = jnp.concatenate([source_ref[j + i] for i in range(group)], axis=1)
        half = jnp.dot(peram_ref[0], side_by_side, preferred_element_type=F32).astype(BF16)
        stacked = jnp.concatenate(
            [half[:, i * evecs : (i + 1) * evecs] for i in range(group)], axis=0
        )
        rotated = times_transposed(stacked, peram_ref[1]).astype(BF16)
        rotated_ref[j : j + group] = rotated.reshape(group, evecs, evecs)

    def place(r, carry):
        out_ref[r] = rotated_ref[pick_ref[0, r]]
        return carry

    lax.fori_loop(0, readers, place, 0, unroll=min(readers, 16))


def edge_kernel(block, root_scale, edge_scale, count_ref, slot_ref, sink_ref, received_ref, resident_ref, out_ref, *factors):
    slots, evecs, _ = received_ref.shape
    sinks = resident_ref.shape[0]
    total = count_ref[0]

    if factors:
        (factor_ref,) = factors
        wide, tall = math.gcd(2, slots), math.gcd(4, sinks)
        for s in range(0, slots, wide):
            weights = received_ref[s : s + wide].reshape(wide * evecs, evecs)
            for k in range(0, sinks, tall):
                rows = resident_ref[k : k + tall].reshape(tall * evecs, evecs)
                product = (times_transposed(rows, weights) * root_scale).astype(BF16)
                for i in range(wide):
                    first = (s + i) * sinks + k
                    factor_ref[first : first + tall] = product[
                        :, i * evecs : (i + 1) * evecs
                    ].reshape(tall, evecs, evecs)
        factor_ref[slots * sinks] = jnp.zeros((evecs, evecs), BF16)

        def factor(side, g):
            row = slot_ref[side, g] * sinks + sink_ref[side, g]
            if side == 0:
                row = jnp.where(g < total, row, slots * sinks)
            return factor_ref[row]
    else:

        def factor(side, g):
            product = times_transposed(
                resident_ref[sink_ref[side, g]], received_ref[slot_ref[side, g]]
            ) * root_scale
            if side == 0:
                product = jnp.where(g < total, product, 0.0)
            return product.astype(BF16)

    def step(b, total_sum):
        base = b * block
        left = jnp.concatenate([factor(0, base + i) for i in range(block)], axis=1)
        right = jnp.concatenate([factor(1, base + i) for i in range(block)], axis=0)
        return total_sum + jnp.dot(left, right, preferred_element_type=F32)

    summed = lax.fori_loop(
        0, (total + block - 1) // block, step, jnp.zeros((evecs, evecs), F32)
    )
    out_ref[0] = (summed * edge_scale).astype(BF16)


def pair_kernel(scale, place, pair_ref, *refs):
    *parts, out_ref, edge_ref = refs
    first = 0
    for part in parts:
        edge_ref[first : first + part.shape[0]] = part[...]
        first += part.shape[0]
    for i in range(out_ref.shape[0]):
        product = jnp.dot(
            edge_ref[place(pair_ref[0, i])],
            edge_ref[place(pair_ref[1, i])],
            preferred_element_type=F32,
        )
        out_ref[i] = (product * scale).astype(BF16)


def xor_phases(readers):
    bits = readers.bit_length() - 1
    near = [[1 << b] for b in range(min(2, bits))]
    step = 1 << len(near)
    far = [[step * i for i in range(readers // step - 1, 0, -1)]]
    return [phase for phase in far + near[::-1] if phase]


def gather_edges(edge, readers):
    if readers & (readers - 1) or readers > 16:
        return [lax.all_gather(edge, "had", axis=0, tiled=True)], lambda r: r
    held, masks = edge, [0]
    for number, phase in enumerate(phases := xor_phases(readers)):
        arrived = [
            lax.ppermute(held, "had", [(d, d ^ mask) for d in range(readers)]) for mask in phase
        ]
        masks = masks + [m ^ mask for mask in phase for m in masks]
        parts = [held] + arrived
        if number < len(phases) - 1:
            held = jnp.concatenate(parts, axis=0)

    def place(reader):
        wanted = reader ^ lax.axis_index("had")
        found = jnp.int32(0)
        for position, mask in enumerate(masks):
            found = jnp.where(wanted == mask, position, found)
        return found

    return parts, place


def shards(
    readers,
    source_slabs,
    sink_slabs,
    perambulators,
    send_pick,
    graph_slot,
    graph_sink,
    graph_count,
    pair_list,
):
    per_device, evecs, _ = source_slabs.shape
    sinks = sink_slabs.shape[0]
    graphs = graph_slot.shape[1]
    pairs = pair_list.shape[0]
    slab = (evecs, evecs)

    outgoing = pl.pallas_call(
        rotate_kernel,
        out_shape=jax.ShapeDtypeStruct((readers,) + slab, BF16),
        in_specs=[HBM, HBM, HBM],
        out_specs=VMEM,
        scratch_shapes=[
            pltpu.SMEM((1, readers), jnp.int32),
            pltpu.VMEM((per_device,) + slab, BF16),
            pltpu.VMEM((2,) + slab, BF16),
            pltpu.VMEM((per_device,) + slab, BF16),
            pltpu.SemaphoreType.DMA((3,)),
        ],
        compiler_params=pltpu.CompilerParams(vmem_limit_bytes=24 << 20),
        name="rotate",
    )(send_pick, source_slabs, perambulators)
    received = lax.all_to_all(outgoing, "had", split_axis=0, concat_axis=0, tiled=True)

    root_scale = 1.0 / math.sqrt(evecs)
    edge_scale = 1.0 / math.sqrt(evecs * graphs)
    dense = readers * sinks <= graphs
    block = math.gcd(128 if dense else 8, graphs)
    edge = pl.pallas_call(
        functools.partial(edge_kernel, block, root_scale, edge_scale),
        out_shape=jax.ShapeDtypeStruct((1,) + slab, BF16),
        in_specs=[SMEM, SMEM, SMEM, VMEM, VMEM],
        out_specs=VMEM,
        scratch_shapes=[pltpu.VMEM((readers * sinks + 1,) + slab, BF16)] if dense else [],
        compiler_params=pltpu.CompilerParams(vmem_limit_bytes=32 << 20),
        name="edge",
    )(graph_count, graph_slot[0].T, graph_sink[0].T, received, sink_slabs)

    parts, place = gather_edges(edge, readers)
    pair_products = pl.pallas_call(
        functools.partial(pair_kernel, root_scale, place),
        out_shape=jax.ShapeDtypeStruct((pairs,) + slab, BF16),
        in_specs=[SMEM] + [VMEM] * len(parts),
        out_specs=VMEM,
        scratch_shapes=[pltpu.VMEM((readers,) + slab, BF16)],
        compiler_params=pltpu.CompilerParams(vmem_limit_bytes=24 << 20),
        name="pairs",
    )(pair_list.T, *parts)
    return edge, pair_products


def solution(mesh):
    return jax.shard_map(
        functools.partial(shards, mesh.shape["had"]),
        mesh=mesh,
        in_specs=(
            P(("grp", "had"), None, None),
            P(("grp", "had"), None, None),
            P("grp", None, None, None),
            P(("grp", "had"), None),
            P(("grp", "had"), None, None),
            P(("grp", "had"), None, None),
            P(("grp", "had")),
            P(("grp", "had"), None),
        ),
        out_specs=(P(("grp", "had"), None, None), P(("grp", "had"), None, None)),
        check_vma=False,
    )
```

time: 212 us -> 51.9 us (0.24)
  matrix products: 85.4 us -> 0 us
  local copies, waits for them, and re-layouts: 75.1 us -> 3.46 us
  blocking collectives: 18.8 us -> 0 us
  Pallas kernels: 0 us -> 12.5 us
  other arithmetic: 8.44 us -> 0.02 us
  waiting for transfers between devices: 13.8 us -> 20.5 us
  starting transfers between devices: 7.38 us -> 13.5 us
    dot_general x20 -> x0, matrix products: 85.4 us -> none  [the longest x8 41.7 us: factor(): jnp.einsum('gxb,agb->gxa', resident, gathered, preferred_element_type=jnp...]
    gather x33 -> x0, local copies, waits for them, and re-layouts: 68.9 us -> none  [the longest x16 34.1 us: factor(): resident = jnp.take(sink_slabs, sinks, axis=0)]
    all_gather x1 -> x0, blocking collectives: 18.8 us -> none  [shards(): shard_rows = lax.all_gather(edge_local, 'had', axis=0, tiled=True)]
    pallas_call x0 -> x3, Pallas kernels: none -> 12.5 us  [the longest x1 8.8 us: shards(): pl.pallas_call(functools.partial(edge_kernel, block, root_scale, edge_sca...]
    ppermute x0 -> x5, waiting for transfers between devices: none -> 6.72 us  [gather_edges(): lax.ppermute(held, 'had', [(d, d ^ mask) for d in range(readers)])]
    dynamic_slice x8 -> x0, local copies, waits for them, and re-layouts: 6.18 us -> none  [accumulate(): slots = lax.dynamic_slice_in_dim(slot_table, offset, block_width, 0)]
    ppermute x0 -> x5, starting transfers between devices: none -> 5.95 us  [gather_edges(): lax.ppermute(held, 'had', [(d, d ^ mask) for d in range(readers)])]
    convert_element_type x9 -> x0, other arithmetic: 5.2 us -> none  [the longest x8 5.19 us: accumulate(): (offset + jnp.arange(block_width, dtype=jnp.int32) < graph_total).astype(...]
  transfers between devices with their start and end apart: 1 -> 6, of which waited for: 1 -> 6; matrix products, arithmetic and copies ran while one was open for 0% -> 2% of each run, Pallas kernels for 0% -> 0%
where the time goes in v1:
time: 51.9 us; the launch traced here: 51.4 us
  waiting for transfers between devices  20.5 us (39%)
  starting transfers between devices  13.5 us (26%)
  Pallas kernels  12.5 us (24%)
  local copies, waits for them, and re-layouts  3.46 us (7%)
  between operations  1.38 us (3%)
    all_to_all x1, waiting for transfers between devices, shards(): lax.all_to_all(outgoing, 'had', split_axis=0, concat_axis=0, tiled=True)  13.8 us
    pallas_call x1, Pallas kernels, shards(): pl.pallas_call(functools.partial(edge_kernel, block, root_scale, edge_sca...  8.8 us
    all_to_all x1, starting transfers between devices, shards(): lax.all_to_all(outgoing, 'had', split_axis=0, concat_axis=0, tiled=True)  7.53 us
    ppermute x5, waiting for transfers between devices, gather_edges(): lax.ppermute(held, 'had', [(d, d ^ mask) for d in range(readers)])  6.72 us
    ppermute x5, starting transfers between devices, gather_edges(): lax.ppermute(held, 'had', [(d, d ^ mask) for d in range(readers)])  5.95 us
    unnamed x20, local copies, waits for them, and re-layouts  3.44 us
    pallas_call x1, Pallas kernels, shards(): pl.pallas_call(rotate_kernel, out_shape=jax.ShapeDtypeStruct((readers,) +...  2.14 us
    pallas_call x1, Pallas kernels, shards(): pl.pallas_call(functools.partial(pair_kernel, root_scale, place), out_sha...  1.59 us
  transfers between devices with their start and end apart: 6, of which 6 were waited for; matrix products, arithmetic and copies ran while one was open for 2% of the time, Pallas kernels for 0%

profile of v1, /device:TPU:0, one launch (start us, length us, event | category | flops | bytes accessed | tf_op | source)
XLA Modules:
  0.0 51.4 jit_solution(4908085140628144422)
XLA Ops:
  0.6 0.0 copy-start
  0.6 1.0 %copy-done = bf16[16,128,128]{2,1,0:T(8,128)(2,1)S(1)} copy-done((bf16[16,128,128]{2,1,0:T(8,128)(2,1)S(1)}, bf16[16,128,128]{2,1,0:T(8,128)(2,1)}, u32[]{:S(2)}) %copy-start) | copy-done | bytes 524312
  1.7 0.9 %copy-done.2 = bf16[2,2,128,128]{3,2,1,0:T(8,128)(2,1)S(1)} copy-done((bf16[2,2,128,128]{3,2,1,0:T(8,128)(2,1)S(1)}, bf16[2,2,128,128]{3,2,1,0:T(8,128)(2,1)}, u32[]{:S(2)}) %copy-start.2) | copy-done | bytes 131096
  2.6 0.7 %copy-done.6 = s32[1,16]{1,0:T(1,128)S(1)} copy-done((s32[1,16]{1,0:T(1,128)S(1)}, s32[1,16]{1,0:T(1,128)}, u32[]{:S(2)}) %copy-start.6) | copy-done | bytes 88
  3.2 2.1 %rotate.1 = bf16[16,128,128]{2,1,0:T(8,128)(2,1)} custom-call(s32[1,16]{1,0:T(1,128)S(1)} %copy-done.6, bf16[16,128,128]{2,1,0:T(8,128)(2,1)S(1)} %copy-done, bf16[2,2,128,128]{3,2,1,0:T(8,128)(2,1)S(1)} %copy-done.2), custom_call_target="tpu_custom_call" | custom-call | tf_op jit(solution)/shard_map/rotate/pallas_call | solution.py:162
  5.4 0.0 copy-start.1
  5.4 0.0 copy-start.4
  5.4 7.5 %all-to-all-start = ((bf16[16,128,128]{2,1,0:T(8,128)(2,1)}), bf16[16,128,128]{2,1,0:T(8,128)(2,1)S(1)}, u32[]{:S(2)}, u32[]{:S(2)}) async-start(bf16[16,128,128]{2,1,0:T(8,128)(2,1)} %rotate.1), calls=%async_computation | async-start | bytes 1048576 | tf_op jit(solution)/shard_map/all_to_all | solution.py:177
  12.9 0.0 copy-start.3
  13.6 13.8 %all-to-all-done.received_ref = bf16[16,128,128]{2,1,0:T(8,128)(2,1)S(1)} async-done(((bf16[16,128,128]{2,1,0:T(8,128)(2,1)}), bf16[16,128,128]{2,1,0:T(8,128)(2,1)S(1)}, u32[]{:S(2)}, u32[]{:S(2)}) %all-to-all-start) | async-done | bytes 524320 | tf_op jit(solution)/shard_map/all_to_all | solution.py:177
  27.4 8.8 %edge.1 = bf16[1,128,128]{2,1,0:T(8,128)(2,1)} custom-call(s32[1]{0:T(128)S(6)} %copy.14.count_ref, s32[2,512]{1,0:T(2,128)S(1)} %bitcast.7, s32[2,512]{1,0:T(2,128)S(1)} %bitcast.8, bf16[16,128,128]{2,1,0:T(8,128)(2,1)S(1)} %all-to-all-done.received_ref, bf16[16,128,128]{2,1,0:T(8,128)(2,1)S(1)} %copy-done.1), custom_call_target="tpu_custom_call" | custom-call | tf_op jit(solution)/shard_map/edge/pallas_call | solution.py:183
  36.2 1.4 %collective-permute-start = (bf16[1,128,128]{2,1,0:T(8,128)(2,1)}, bf16[1,128,128]{2,1,0:T(8,128)(2,1)S(1)}, u32[]{:S(2)}, u32[]{:S(2)}) collective-permute-start(bf16[1,128,128]{2,1,0:T(8,128)(2,1)} %edge.1), channel_id=1, source_target_pairs={{0,12},{1,13},{2,14},{3,15},{4,8},{5,9},{6,10},{7,11},{8,4},{9,5},... | collective-permute-start | bytes 98312 | tf_op jit(solution)/shard_map/ppermute | solution.py:128
  37.6 0.9 %collective-permute-start.1 = (bf16[1,128,128]{2,1,0:T(8,128)(2,1)}, bf16[1,128,128]{2,1,0:T(8,128)(2,1)S(1)}, u32[]{:S(2)}, u32[]{:S(2)}) collective-permute-start(bf16[1,128,128]{2,1,0:T(8,128)(2,1)} %edge.1), channel_id=1, source_target_pairs={{0,8},{1,9},{2,10},{3,11},{4,12},{5,13},{6,14},{7,15},{8,0},{9,1},... | collective-permute-start | bytes 98312 | tf_op jit(solution)/shard_map/ppermute | solution.py:128
  38.5 2.1 %collective-permute-start.2 = (bf16[1,128,128]{2,1,0:T(8,128)(2,1)}, bf16[1,128,128]{2,1,0:T(8,128)(2,1)S(1)}, u32[]{:S(2)}, u32[]{:S(2)}) collective-permute-start(bf16[1,128,128]{2,1,0:T(8,128)(2,1)} %edge.1), channel_id=1, source_target_pairs={{0,4},{1,5},{2,6},{3,7},{4,0},{5,1},{6,2},{7,3},{8,12},{9,13},{10,... | collective-permute-start | bytes 98312 | tf_op jit(solution)/shard_map/ppermute | solution.py:128
  40.6 0.8 %constant_dynamic-update-slice_fusion.4 = bf16[8,128,128]{2,1,0:T(8,128)(2,1)S(1)} fusion(bf16[1,128,128]{2,1,0:T(8,128)(2,1)} %edge.1), kind=kLoop, calls=%fused_computation.5 | loop fusion | bytes 65536
  41.4 0.7 %collective-permute-done = bf16[1,128,128]{2,1,0:T(8,128)(2,1)S(1)} collective-permute-done((bf16[1,128,128]{2,1,0:T(8,128)(2,1)}, bf16[1,128,128]{2,1,0:T(8,128)(2,1)S(1)}, u32[]{:S(2)}, u32[]{:S(2)}) %collective-permute-start) | collective-permute-done | bytes 32800 | tf_op jit(solution)/shard_map/ppermute | solution.py:128
  42.2 0.6 %collective-permute-done.1 = bf16[1,128,128]{2,1,0:T(8,128)(2,1)S(1)} collective-permute-done((bf16[1,128,128]{2,1,0:T(8,128)(2,1)}, bf16[1,128,128]{2,1,0:T(8,128)(2,1)S(1)}, u32[]{:S(2)}, u32[]{:S(2)}) %collective-permute-start.1) | collective-permute-done | bytes 32800 | tf_op jit(solution)/shard_map/ppermute | solution.py:128
  42.8 0.3 collective-permute-done.2
  43.1 1.5 %collective-permute-start.3 = (bf16[4,128,128]{2,1,0:T(8,128)(2,1)S(1)}, bf16[4,128,128]{2,1,0:T(8,128)(2,1)S(1)}, u32[]{:S(2)}, u32[]{:S(2)}) collective-permute-start(bf16[4,128,128]{2,1,0:T(8,128)(2,1)S(1)} %pad_maximum_fusion), channel_id=1, source_target_pairs={{0,2},{1,3},{2,0},{3,1},{4,6},{5,7},{6,4},{7,5},{8,10},{9,11},{10,... | collective-permute-start | bytes 393224 | tf_op jit(solution)/shard_map/ppermute | solution.py:128
  44.7 3.5 %collective-permute-done.3 = bf16[4,128,128]{2,1,0:T(8,128)(2,1)S(1)} collective-permute-done((bf16[4,128,128]{2,1,0:T(8,128)(2,1)S(1)}, bf16[4,128,128]{2,1,0:T(8,128)(2,1)S(1)}, u32[]{:S(2)}, u32[]{:S(2)}) %collective-permute-start.3) | collective-permute-done | bytes 131104 | tf_op jit(solution)/shard_map/ppermute | solution.py:128
  48.2 0.0 copy-start.5
  48.2 0.1 collective-permute-start.4
  48.3 1.5 %collective-permute-done.4.refs_1_ = bf16[8,128,128]{2,1,0:T(8,128)(2,1)S(1)} collective-permute-done((bf16[8,128,128]{2,1,0:T(8,128)(2,1)S(1)}, bf16[8,128,128]{2,1,0:T(8,128)(2,1)S(1)}, u32[]{:S(2)}, u32[]{:S(2)}) %collective-permute-start.4) | collective-permute-done | bytes 262176 | tf_op jit(solution)/shard_map/ppermute | solution.py:128
  49.8 1.6 %pairs.1 = bf16[8,128,128]{2,1,0:T(8,128)(2,1)} custom-call(s32[2,8]{1,0:T(2,128)S(1)} %bitcast.9, bf16[8,128,128]{2,1,0:T(8,128)(2,1)S(1)} %constant_dynamic-update-slice_fusion.refs_0_, bf16[8,128,128]{2,1,0:T(8,128)(2,1)S(1)} %collective-permute-done.4.refs_1_), custom_call_target="tpu_custom_call" | custom-call | tf_op jit(solution)/shard_map/pairs/pallas_call | solution.py:194
  (13 shorter events, 0.1 us)
Async XLA Ops:
  0.6 1.0 %copy-start = (bf16[16,128,128]{2,1,0:T(8,128)(2,1)S(1)}, bf16[16,128,128]{2,1,0:T(8,128)(2,1)}, u32[]{:S(2)}) copy-start(bf16[16,128,128]{2,1,0:T(8,128)(2,1)} %source_hbm.1) | copy-start | bytes 1572868
  1.7 0.9 %copy-start.2 = (bf16[2,2,128,128]{3,2,1,0:T(8,128)(2,1)S(1)}, bf16[2,2,128,128]{3,2,1,0:T(8,128)(2,1)}, u32[]{:S(2)}) copy-start(bf16[2,2,128,128]{3,2,1,0:T(8,128)(2,1)} %peram_hbm.1) | copy-start | bytes 393220
  2.6 0.7 %copy-start.6 = (s32[1,16]{1,0:T(1,128)S(1)}, s32[1,16]{1,0:T(1,128)}, u32[]{:S(2)}) copy-start(s32[1,16]{1,0:T(1,128)} %pick_hbm.1) | copy-start | bytes 196
  5.4 22.0 %copy-start.1 = (bf16[16,128,128]{2,1,0:T(8,128)(2,1)S(1)}, bf16[16,128,128]{2,1,0:T(8,128)(2,1)}, u32[]{:S(2)}) copy-start(bf16[16,128,128]{2,1,0:T(8,128)(2,1)} %resident_ref.1) | copy-start | bytes 1572868
  5.4 22.0 %copy-start.4 = (s32[1,512,2]{1,2,0:T(2,128)S(1)}, s32[1,512,2]{1,2,0:T(2,128)}, u32[]{:S(2)}) copy-start(s32[1,512,2]{1,2,0:T(2,128)} %param.13) | copy-start | bytes 12292
  5.4 22.0 %all-to-all-start = ((bf16[16,128,128]{2,1,0:T(8,128)(2,1)}), bf16[16,128,128]{2,1,0:T(8,128)(2,1)S(1)}, u32[]{:S(2)}, u32[]{:S(2)}) async-start(bf16[16,128,128]{2,1,0:T(8,128)(2,1)} %rotate.1), calls=%async_computation | async-start | bytes 1048576 | tf_op jit(solution)/shard_map/all_to_all | solution.py:177
  12.9 14.5 %copy-start.3 = (s32[1,512,2]{1,2,0:T(2,128)S(1)}, s32[1,512,2]{1,2,0:T(2,128)}, u32[]{:S(2)}) copy-start(s32[1,512,2]{1,2,0:T(2,128)} %param.12) | copy-start | bytes 12292
  36.2 6.9 %copy-start.7 = (bf16[1,128,128]{2,1,0:T(8,128)(2,1)S(1)}, bf16[1,128,128]{2,1,0:T(8,128)(2,1)}, u32[]{:S(2)}) copy-start(bf16[1,128,128]{2,1,0:T(8,128)(2,1)} %edge.1) | copy-start | bytes 98308
  36.2 5.9 %collective-permute-start = (bf16[1,128,128]{2,1,0:T(8,128)(2,1)}, bf16[1,128,128]{2,1,0:T(8,128)(2,1)S(1)}, u32[]{:S(2)}, u32[]{:S(2)}) collective-permute-start(bf16[1,128,128]{2,1,0:T(8,128)(2,1)} %edge.1), channel_id=1, source_target_pairs={{0,12},{1,13},{2,14},{3,15},{4,8},{5,9},{6,10},{7,11},{8,4},{9,5},... | collective-permute-start | bytes 98312 | tf_op jit(solution)/shard_map/ppermute | solution.py:128
  37.6 5.2 %collective-permute-start.1 = (bf16[1,128,128]{2,1,0:T(8,128)(2,1)}, bf16[1,128,128]{2,1,0:T(8,128)(2,1)S(1)}, u32[]{:S(2)}, u32[]{:S(2)}) collective-permute-start(bf16[1,128,128]{2,1,0:T(8,128)(2,1)} %edge.1), channel_id=1, source_target_pairs={{0,8},{1,9},{2,10},{3,11},{4,12},{5,13},{6,14},{7,15},{8,0},{9,1},... | collective-permute-start | bytes 98312 | tf_op jit(solution)/shard_map/ppermute | solution.py:128
  38.5 4.6 %collective-permute-start.2 = (bf16[1,128,128]{2,1,0:T(8,128)(2,1)}, bf16[1,128,128]{2,1,0:T(8,128)(2,1)S(1)}, u32[]{:S(2)}, u32[]{:S(2)}) collective-permute-start(bf16[1,128,128]{2,1,0:T(8,128)(2,1)} %edge.1), channel_id=1, source_target_pairs={{0,4},{1,5},{2,6},{3,7},{4,0},{5,1},{6,2},{7,3},{8,12},{9,13},{10,... | collective-permute-start | bytes 98312 | tf_op jit(solution)/shard_map/ppermute | solution.py:128
  43.1 5.0 %collective-permute-start.3 = (bf16[4,128,128]{2,1,0:T(8,128)(2,1)S(1)}, bf16[4,128,128]{2,1,0:T(8,128)(2,1)S(1)}, u32[]{:S(2)}, u32[]{:S(2)}) collective-permute-start(bf16[4,128,128]{2,1,0:T(8,128)(2,1)S(1)} %pad_maximum_fusion), channel_id=1, source_target_pairs={{0,2},{1,3},{2,0},{3,1},{4,6},{5,7},{6,4},{7,5},{8,10},{9,11},{10,... | collective-permute-start | bytes 393224 | tf_op jit(solution)/shard_map/ppermute | solution.py:128
  48.2 1.6 %copy-start.5 = (s32[8,2]{0,1:T(2,128)S(1)}, s32[8,2]{0,1:T(2,128)}, u32[]{:S(2)}) copy-start(s32[8,2]{0,1:T(2,128)} %param.15) | copy-start | bytes 196
  48.2 1.6 %collective-permute-start.4 = (bf16[8,128,128]{2,1,0:T(8,128)(2,1)S(1)}, bf16[8,128,128]{2,1,0:T(8,128)(2,1)S(1)}, u32[]{:S(2)}, u32[]{:S(2)}) collective-permute-start(bf16[8,128,128]{2,1,0:T(8,128)(2,1)S(1)} %constant_dynamic-update-slice_fusion.refs_0_), channel_id=1, source_target_pairs={{0,1},{1,0},{2,3},{3,2},{4,5},{5,4},{6,7},{7,6},{8,9},{9,8},{10,11... | collective-permute-start | bytes 786440 | tf_op jit(solution)/shard_map/ppermute | solution.py:128

commit v2 on v1

v2 whole, which is shorter than its diff:
```python
import functools
import math

import jax
import jax.numpy as jnp
from jax import lax
from jax.experimental import pallas as pl
from jax.experimental.pallas import tpu as pltpu
from jax.sharding import PartitionSpec as P

BF16 = jnp.bfloat16
F32 = jnp.float32
VMEM = pl.BlockSpec(memory_space=pltpu.VMEM)
SMEM = pl.BlockSpec(memory_space=pltpu.SMEM)
HBM = pl.BlockSpec(memory_space=pltpu.HBM)
ORDER = (1, 4, 6, 2, 5, 7, 3)
EARLY = 4


def params(mebibytes):
    return pltpu.CompilerParams(vmem_limit_bytes=mebibytes << 20)


def times_transposed(left, right):
    return lax.dot_general(left, right, (((1,), (1,)), ((), ())), preferred_element_type=F32)


def rotate_slabs(pick_hbm, source_hbm, peram_hbm, pick_ref, source_ref, peram_ref, rotated_ref, sems):
    per_device, evecs, _ = source_ref.shape
    timeslice = lax.axis_index("had") * per_device // evecs
    copies = [
        pltpu.make_async_copy(peram_hbm.at[timeslice], peram_ref, sems.at[0]),
        pltpu.make_async_copy(source_hbm, source_ref, sems.at[1]),
        pltpu.make_async_copy(pick_hbm, pick_ref, sems.at[2]),
    ]
    for copy in copies:
        copy.start()
    for copy in copies:
        copy.wait()
    group = math.gcd(4, per_device)
    for j in range(0, per_device, group):
        side_by_side = jnp.concatenate([source_ref[j + i] for i in range(group)], axis=1)
        half = jnp.dot(peram_ref[0], side_by_side, preferred_element_type=F32).astype(BF16)
        stacked = jnp.concatenate(
            [half[:, i * evecs : (i + 1) * evecs] for i in range(group)], axis=0
        )
        rotated = times_transposed(stacked, peram_ref[1]).astype(BF16)
        rotated_ref[j : j + group] = rotated.reshape(group, evecs, evecs)


def rotate_kernel(pick_hbm, source_hbm, peram_hbm, out_ref, *scratch):
    pick_ref, _, _, rotated_ref, _ = scratch
    rotate_slabs(pick_hbm, source_hbm, peram_hbm, *scratch)

    def place(r, carry):
        out_ref[r] = rotated_ref[pick_ref[0, r]]
        return carry

    lax.fori_loop(0, out_ref.shape[0], place, 0)


def rotate_pairs_kernel(
    pick_hbm, source_hbm, peram_hbm, sink_hbm, mine_ref, other_ref, resident_ref, *scratch
):
    *scratch, sink_sem = scratch
    pick_ref, _, _, rotated_ref, _ = scratch
    sinks_in = pltpu.make_async_copy(sink_hbm, resident_ref, sink_sem)
    sinks_in.start()
    rotate_slabs(pick_hbm, source_hbm, peram_hbm, *scratch)
    me = lax.axis_index("had")
    for i in range(mine_ref.shape[0]):
        other_ref[i] = rotated_ref[pick_ref[0, me ^ (2 * i + 1)]]
        mine_ref[i] = rotated_ref[pick_ref[0, me ^ (2 * i)]]
    sinks_in.wait()


def zip_kernel(mine_ref, got_ref, *out_refs):
    for i, out_ref in enumerate(out_refs):
        out_ref[0] = mine_ref[i]
        out_ref[1] = got_ref[i]


def fill_factors(factor_ref, resident_ref, weights, first_slot, root_scale):
    sinks, evecs, _ = resident_ref.shape
    wide, tall = weights.shape[0] // evecs, math.gcd(4, sinks)
    for k in range(0, sinks, tall):
        rows = resident_ref[k : k + tall].reshape(tall * evecs, evecs)
        product = (times_transposed(rows, weights) * root_scale).astype(BF16)
        for i in range(wide):
            first = (first_slot + i) * sinks + k
            factor_ref[first : first + tall] = product[
                :, i * evecs : (i + 1) * evecs
            ].reshape(tall, evecs, evecs)


def factor_kernel(root_scale, first_slots, resident_ref, *refs):
    *arrived, factor_ref = refs
    _, evecs, _ = resident_ref.shape
    for first_slot, ref in zip(first_slots, arrived):
        fill_factors(factor_ref, resident_ref, ref[...].reshape(-1, evecs), first_slot, root_scale)


def graph_sum(block, total, factor, evecs):
    def step(b, total_sum):
        base = b * block
        left = jnp.concatenate([factor(0, base + i) for i in range(block)], axis=1)
        right = jnp.concatenate([factor(1, base + i) for i in range(block)], axis=0)
        return total_sum + jnp.dot(left, right, preferred_element_type=F32)

    return lax.fori_loop(
        0, (total + block - 1) // block, step, jnp.zeros((evecs, evecs), F32)
    )


def masked_edge_kernel(
    block, root_scale, edge_scale, first_slots, count_ref, slot_hbm, sink_hbm, resident_ref, *refs
):
    *arrived, _, out_ref, factor_ref, slot_ref, sink_ref, sems = refs
    sinks, evecs, _ = resident_ref.shape
    copies = [
        pltpu.make_async_copy(slot_hbm, slot_ref, sems.at[0]),
        pltpu.make_async_copy(sink_hbm, sink_ref, sems.at[1]),
    ]
    for copy in copies:
        copy.start()
    for first_slot, ref in zip(first_slots, arrived):
        fill_factors(factor_ref, resident_ref, ref[...].reshape(-1, evecs), first_slot, root_scale)
    nothing = factor_ref.shape[0] - 1
    factor_ref[nothing] = jnp.zeros((evecs, evecs), BF16)
    for copy in copies:
        copy.wait()
    me = lax.axis_index("had")
    total = count_ref[0]

    def factor(side, g):
        row = (slot_ref[side, g] ^ me) * sinks + sink_ref[side, g]
        if side == 0:
            row = jnp.where(g < total, row, nothing)
        return factor_ref[row]

    out_ref[0] = (graph_sum(block, total, factor, evecs) * edge_scale).astype(BF16)


def edge_kernel(block, root_scale, edge_scale, count_ref, slot_ref, sink_ref, received_ref, resident_ref, out_ref, *factors):
    slots, evecs, _ = received_ref.shape
    sinks = resident_ref.shape[0]
    total = count_ref[0]

    if factors:
        (factor_ref,) = factors
        wide = math.gcd(2, slots)
        for s in range(0, slots, wide):
            weights = received_ref[s : s + wide].reshape(wide * evecs, evecs)
            fill_factors(factor_ref, resident_ref, weights, s, root_scale)
        factor_ref[slots * sinks] = jnp.zeros((evecs, evecs), BF16)

        def factor(side, g):
            row = slot_ref[side, g] * sinks + sink_ref[side, g]
            if side == 0:
                row = jnp.where(g < total, row, slots * sinks)
            return factor_ref[row]
    else:

        def factor(side, g):
            product = times_transposed(
                resident_ref[sink_ref[side, g]], received_ref[slot_ref[side, g]]
            ) * root_scale
            if side == 0:
                product = jnp.where(g < total, product, 0.0)
            return product.astype(BF16)

    out_ref[0] = (graph_sum(block, total, factor, evecs) * edge_scale).astype(BF16)


def pair_kernel(scale, place, pair_ref, *refs):
    *parts, out_hbm, edge_ref, product_ref, sems = refs
    first = 0
    for part in parts:
        edge_ref[first : first + part.shape[0]] = part[...]
        first += part.shape[0]
    copies = []
    for i in range(out_hbm.shape[0]):
        product = jnp.dot(
            edge_ref[place(pair_ref[0, i])],
            edge_ref[place(pair_ref[1, i])],
            preferred_element_type=F32,
        )
        product_ref[i] = (product * scale).astype(BF16)
        copies.append(pltpu.make_async_copy(product_ref.at[i], out_hbm.at[i], sems.at[i]))
        copies[-1].start()
    for copy in copies:
        copy.wait()


def xor_phases(readers):
    far = list(range(readers - 4, 0, -4))
    return [phase for phase in ([2] if readers > 2 else [], far, [1]) if phase]


def by_xor(readers):
    return 2 <= readers <= 16 and readers & (readers - 1) == 0


def xor_permute(array, readers, mask):
    return lax.ppermute(array, "had", [(d, d ^ mask) for d in range(readers)])


def gather_edges(edge, readers):
    if not by_xor(readers):
        return [lax.all_gather(edge, "had", axis=0, tiled=True)], lambda r: r
    held = edge
    for phase in xor_phases(readers):
        arrived = [xor_permute(held, readers, mask) for mask in phase]
        parts = [held] + arrived[::-1]
        if phase != [1]:
            held = jnp.concatenate(parts, axis=0)

    def place(reader):
        mask = reader ^ lax.axis_index("had")
        return (mask >> 1) + (mask & 1) * (readers // 2)

    return parts, place


def shards(
    readers,
    source_slabs,
    sink_slabs,
    perambulators,
    send_pick,
    graph_slot,
    graph_sink,
    graph_count,
    pair_list,
):
    per_device, evecs, _ = source_slabs.shape
    sinks = sink_slabs.shape[0]
    graphs = graph_slot.shape[1]
    pairs = pair_list.shape[0]
    slab = (evecs, evecs)

    root_scale = 1.0 / math.sqrt(evecs)
    edge_scale = 1.0 / math.sqrt(evecs * graphs)
    dense = readers * sinks <= graphs
    block = math.gcd(128 if dense else 8, graphs)
    rotate_args = [
        pltpu.with_memory_space_constraint(array, pltpu.HBM)
        for array in (send_pick, source_slabs, perambulators)
    ]
    rotate_scratch = [
        pltpu.SMEM((1, readers), jnp.int32),
        pltpu.VMEM((per_device,) + slab, BF16),
        pltpu.VMEM((2,) + slab, BF16),
        pltpu.VMEM((per_device,) + slab, BF16),
        pltpu.SemaphoreType.DMA((3,)),
    ]
    counts = (graph_count, graph_slot[0].T, graph_sink[0].T)

    if dense and by_xor(readers):
        half = readers // 2
        mine, other, resident = pl.pallas_call(
            rotate_pairs_kernel,
            out_shape=[
                pltpu.VMEM((half,) + slab, BF16),
                pltpu.VMEM((half,) + slab, BF16),
                pltpu.VMEM((sinks,) + slab, BF16),
            ],
            in_specs=[HBM] * 4,
            out_specs=[VMEM] * 3,
            scratch_shapes=rotate_scratch + [pltpu.SemaphoreType.DMA],
            compiler_params=params(16),
            name="rotate",
        )(*rotate_args, pltpu.with_memory_space_constraint(sink_slabs, pltpu.HBM))
        got = xor_permute(other, readers, 1)
        pairs_for = pl.pallas_call(
            zip_kernel,
            out_shape=[pltpu.VMEM((2,) + slab, BF16)] * half,
            in_specs=[VMEM] * 2,
            out_specs=[VMEM] * half,
            compiler_params=params(16),
            name="zip",
        )(mine, got)
        order = [i for i in ORDER if i < half]
        arrived = {0: pairs_for[0]}
        for i in order:
            arrived[i] = xor_permute(pairs_for[i], readers, 2 * i)
        early = [0] + order[:EARLY]
        late = order[EARLY:]
        rows = readers * sinks + 1
        factors = pl.pallas_call(
            functools.partial(factor_kernel, root_scale, [2 * i for i in early]),
            out_shape=pltpu.VMEM((rows,) + slab, BF16),
            in_specs=[VMEM] * (1 + len(early)),
            out_specs=VMEM,
            compiler_params=params(16),
            cost_estimate=pl.CostEstimate(
                flops=8 * len(early) * sinks * evecs**3, bytes_accessed=0, transcendentals=0
            ),
            name="factors",
        )(resident, *[arrived[i] for i in early])
        edge, _ = pl.pallas_call(
            functools.partial(
                masked_edge_kernel, block, root_scale, edge_scale, [2 * i for i in late]
            ),
            out_shape=[
                pltpu.VMEM((1,) + slab, BF16),
                pltpu.VMEM((rows,) + slab, BF16),
            ],
            in_specs=[SMEM, HBM, HBM] + [VMEM] * (2 + len(late)),
            out_specs=[VMEM] * 2,
            scratch_shapes=[
                pltpu.SMEM((2, graphs), jnp.int32),
                pltpu.SMEM((2, graphs), jnp.int32),
                pltpu.SemaphoreType.DMA((2,)),
            ],
            input_output_aliases={4 + len(late): 1},
            compiler_params=params(16),
            name="edge",
        )(*counts, resident, *[arrived[i] for i in late], factors)
    else:
        outgoing = pl.pallas_call(
            rotate_kernel,
            out_shape=jax.ShapeDtypeStruct((readers,) + slab, BF16),
            in_specs=[HBM] * 3,
            out_specs=VMEM,
            scratch_shapes=rotate_scratch,
            compiler_params=params(24),
            name="rotate",
        )(*rotate_args)
        received = lax.all_to_all(outgoing, "had", split_axis=0, concat_axis=0, tiled=True)
        edge = pl.pallas_call(
            functools.partial(edge_kernel, block, root_scale, edge_scale),
            out_shape=jax.ShapeDtypeStruct((1,) + slab, BF16),
            in_specs=[SMEM, SMEM, SMEM, VMEM, VMEM],
            out_specs=VMEM,
            scratch_shapes=[pltpu.VMEM((readers * sinks + 1,) + slab, BF16)] if dense else [],
            compiler_params=params(32),
            name="edge",
        )(*counts, received, sink_slabs)

    parts, place = gather_edges(edge, readers)
    pair_products = pl.pallas_call(
        functools.partial(pair_kernel, root_scale, place),
        out_shape=jax.ShapeDtypeStruct((pairs,) + slab, BF16),
        in_specs=[SMEM] + [VMEM] * len(parts),
        out_specs=HBM,
        scratch_shapes=[
            pltpu.VMEM((readers,) + slab, BF16),
            pltpu.VMEM((pairs,) + slab, BF16),
            pltpu.SemaphoreType.DMA((pairs,)),
        ],
        compiler_params=params(24),
        name="pairs",
    )(pair_list.T, *parts)
    return edge, pair_products


def solution(mesh):
    return jax.shard_map(
        functools.partial(shards, mesh.shape["had"]),
        mesh=mesh,
        in_specs=(
            P(("grp", "had"), None, None),
            P(("grp", "had"), None, None),
            P("grp", None, None, None),
            P(("grp", "had"), None),
            P(("grp", "had"), None, None),
            P(("grp", "had"), None, None),
            P(("grp", "had")),
            P(("grp", "had"), None),
        ),
        out_specs=(P(("grp", "had"), None, None), P(("grp", "had"), None, None)),
        check_vma=False,
    )
```

time: 51.9 us -> 44.2 us (0.85)
  waiting for transfers between devices: 20.5 us -> 13.9 us
  starting transfers between devices: 13.5 us -> 19.5 us
  Pallas kernels: 12.5 us -> 8.66 us
  local copies, waits for them, and re-layouts: 3.46 us -> 0.69 us
    all_to_all x1 -> x0, waiting for transfers between devices: 13.8 us -> none  [shards(): lax.all_to_all(outgoing, 'had', split_axis=0, concat_axis=0, tiled=True)]
    ppermute x5 -> x13, starting transfers between devices: 5.95 us -> 19.5 us  [xor_permute(): return lax.ppermute(array, 'had', [(d, d ^ mask) for d in range(readers)])]
    all_to_all x1 -> x0, starting transfers between devices: 7.53 us -> none  [shards(): lax.all_to_all(outgoing, 'had', split_axis=0, concat_axis=0, tiled=True)]
    ppermute x5 -> x13, waiting for transfers between devices: 6.72 us -> 13.9 us  [xor_permute(): return lax.ppermute(array, 'had', [(d, d ^ mask) for d in range(readers)])]
    pallas_call x2 -> x4, Pallas kernels: 10.9 us -> 7.15 us  [the longest x1 3.62 us: shards(): pl.pallas_call(functools.partial(masked_edge_kernel, block, root_scale, e...]
    unnamed x20 -> x10, local copies, waits for them, and re-layouts: 3.44 us -> 0.66 us
  transfers between devices with their start and end apart: 6 -> 13, of which waited for: 6 -> 7; matrix products, arithmetic and copies ran while one was open for 2% -> 1% of each run, Pallas kernels for 0% -> 3%
where the time goes in v2:
time: 44.2 us; the launch traced here: 44.1 us
  starting transfers between devices  19.5 us (44%)
  waiting for transfers between devices  13.9 us (31%)
  Pallas kernels  8.66 us (20%)
  between operations  1.38 us (3%)
  local copies, waits for them, and re-layouts  0.69 us (2%)
    ppermute x13, starting transfers between devices, xor_permute(): return lax.ppermute(array, 'had', [(d, d ^ mask) for d in range(readers)])  19.5 us
    ppermute x13, waiting for transfers between devices, xor_permute(): return lax.ppermute(array, 'had', [(d, d ^ mask) for d in range(readers)])  13.9 us
    pallas_call x1, Pallas kernels, shards(): pl.pallas_call(functools.partial(masked_edge_kernel, block, root_scale, e...  3.62 us
    pallas_call x1, Pallas kernels, shards(): pl.pallas_call(rotate_pairs_kernel, out_shape=[pltpu.VMEM((half,) + slab,...  1.97 us
    pallas_call x1, Pallas kernels, shards(): pl.pallas_call(functools.partial(factor_kernel, root_scale, [2 * i for i...  1.53 us
    pallas_call x1, Pallas kernels, shards(): pl.pallas_call(functools.partial(pair_kernel, root_scale, place), out_sha...  1.51 us
  transfers between devices with their start and end apart: 13, of which 7 were waited for; matrix products, arithmetic and copies ran while one was open for 1% of the time, Pallas kernels for 3%

profile of v2, /device:TPU:0, one launch (start us, length us, event | category | flops | bytes accessed | tf_op | source)
XLA Modules:
  0.0 44.1 jit_solution(9875609184129140528)
XLA Ops:
  0.7 2.0 %rotate.1 = (bf16[8,128,128]{2,1,0:T(8,128)(2,1)S(1)}, bf16[8,128,128]{2,1,0:T(8,128)(2,1)S(1)}, bf16[16,128,128]{2,1,0:T(8,128)(2,1)S(1)}) custom-call(s32[1,16]{1,0:T(1,128)} %pick_hbm.1, bf16[16,128,128]{2,1,0:T(8,128)(2,1)} %source_hbm.1, bf16[2,2,128,128]{3,2,1,0:T(8,128)(2,1)} %peram_hbm.1, bf16[16,128,128]{2,1,0:T(8,128)(2,1)} %sink_hbm.1), custom_call_target="tpu_custom_call" | custom-call | tf_op jit(solution)/shard_map/rotate/pallas_call | solution.py:261
  2.6 0.5 %collective-permute-start = (bf16[8,128,128]{2,1,0:T(8,128)(2,1)S(1)}, bf16[8,128,128]{2,1,0:T(8,128)(2,1)S(1)}, u32[]{:S(2)}, u32[]{:S(2)}) collective-permute-start(bf16[8,128,128]{2,1,0:T(8,128)(2,1)S(1)} %get-tuple-element.16), channel_id=1, source_target_pairs={{0,1},{1,0},{2,3},{3,2},{4,5},{5,4},{6,7},{7,6},{8,9},{9,8},{10,11... | collective-permute-start | bytes 786440 | tf_op jit(solution)/shard_map/ppermute | solution.py:205
  3.2 1.2 %collective-permute-done.got_ref = bf16[8,128,128]{2,1,0:T(8,128)(2,1)S(1)} collective-permute-done((bf16[8,128,128]{2,1,0:T(8,128)(2,1)S(1)}, bf16[8,128,128]{2,1,0:T(8,128)(2,1)S(1)}, u32[]{:S(2)}, u32[]{:S(2)}) %collective-permute-start) | collective-permute-done | bytes 262176 | tf_op jit(solution)/shard_map/ppermute | solution.py:205
  4.4 3.0 %collective-permute-start.4 = (bf16[2,128,128]{2,1,0:T(8,128)(2,1)S(1)}, bf16[2,128,128]{2,1,0:T(8,128)(2,1)S(1)}, u32[]{:S(2)}, u32[]{:S(2)}) collective-permute-start(bf16[2,128,128]{2,1,0:T(8,128)(2,1)S(1)} %get-tuple-element.21), channel_id=1, source_target_pairs={{0,2},{1,3},{2,0},{3,1},{4,6},{5,7},{6,4},{7,5},{8,10},{9,11},{10,... | collective-permute-start | bytes 196616 | tf_op jit(solution)/shard_map/ppermute | solution.py:205
  7.3 2.6 %collective-permute-start.5 = (bf16[2,128,128]{2,1,0:T(8,128)(2,1)S(1)}, bf16[2,128,128]{2,1,0:T(8,128)(2,1)S(1)}, u32[]{:S(2)}, u32[]{:S(2)}) collective-permute-start(bf16[2,128,128]{2,1,0:T(8,128)(2,1)S(1)} %get-tuple-element.22), channel_id=1, source_target_pairs={{0,8},{1,9},{2,10},{3,11},{4,12},{5,13},{6,14},{7,15},{8,0},{9,1},... | collective-permute-start | bytes 196616 | tf_op jit(solution)/shard_map/ppermute | solution.py:205
  9.9 1.3 %collective-permute-start.6 = (bf16[2,128,128]{2,1,0:T(8,128)(2,1)S(1)}, bf16[2,128,128]{2,1,0:T(8,128)(2,1)S(1)}, u32[]{:S(2)}, u32[]{:S(2)}) collective-permute-start(bf16[2,128,128]{2,1,0:T(8,128)(2,1)S(1)} %get-tuple-element.23), channel_id=1, source_target_pairs={{0,12},{1,13},{2,14},{3,15},{4,8},{5,9},{6,10},{7,11},{8,4},{9,5},... | collective-permute-start | bytes 196616 | tf_op jit(solution)/shard_map/ppermute | solution.py:205
  11.2 0.2 collective-permute-start.7
  12.1 2.8 %collective-permute-start.1 = (bf16[2,128,128]{2,1,0:T(8,128)(2,1)S(1)}, bf16[2,128,128]{2,1,0:T(8,128)(2,1)S(1)}, u32[]{:S(2)}, u32[]{:S(2)}) collective-permute-start(bf16[2,128,128]{2,1,0:T(8,128)(2,1)S(1)} %get-tuple-element.17), channel_id=1, source_target_pairs={{0,10},{1,11},{2,8},{3,9},{4,14},{5,15},{6,12},{7,13},{8,2},{9,3},... | collective-permute-start | bytes 196616 | tf_op jit(solution)/shard_map/ppermute | solution.py:205
  14.9 2.3 %collective-permute-start.2 = (bf16[2,128,128]{2,1,0:T(8,128)(2,1)S(1)}, bf16[2,128,128]{2,1,0:T(8,128)(2,1)S(1)}, u32[]{:S(2)}, u32[]{:S(2)}) collective-permute-start(bf16[2,128,128]{2,1,0:T(8,128)(2,1)S(1)} %get-tuple-element.18), channel_id=1, source_target_pairs={{0,14},{1,15},{2,12},{3,13},{4,10},{5,11},{6,8},{7,9},{8,6},{9,7},... | collective-permute-start | bytes 196616 | tf_op jit(solution)/shard_map/ppermute | solution.py:205
  17.3 0.0 copy-start.2
  17.3 1.5 %factors.1.refs_3_ = bf16[257,128,128]{2,1,0:T(8,128)(2,1)S(1)} custom-call(bf16[16,128,128]{2,1,0:T(8,128)(2,1)S(1)} %get-tuple-element.14.resident_ref, bf16[2,128,128]{2,1,0:T(8,128)(2,1)S(1)} %get-tuple-element.20.refs_0_, bf16[2,128,128]{2,1,0:T(8,128)(2,1)S(1)} %collective-permute-done.4.refs_1_, ...), custom_call_target="tpu_custom_call" | custom-call | flops 1342177280 | tf_op jit(solution)/shard_map/factors/pallas_call | solution.py:290
  18.8 1.7 %collective-permute-done.1.refs_0_ = bf16[2,128,128]{2,1,0:T(8,128)(2,1)S(1)} collective-permute-done((bf16[2,128,128]{2,1,0:T(8,128)(2,1)S(1)}, bf16[2,128,128]{2,1,0:T(8,128)(2,1)S(1)}, u32[]{:S(2)}, u32[]{:S(2)}) %collective-permute-start.1) | collective-permute-done | bytes 65568 | tf_op jit(solution)/shard_map/ppermute | solution.py:205
  20.5 1.4 %collective-permute-done.2.refs_1_ = bf16[2,128,128]{2,1,0:T(8,128)(2,1)S(1)} collective-permute-done((bf16[2,128,128]{2,1,0:T(8,128)(2,1)S(1)}, bf16[2,128,128]{2,1,0:T(8,128)(2,1)S(1)}, u32[]{:S(2)}, u32[]{:S(2)}) %collective-permute-start.2) | collective-permute-done | bytes 65568 | tf_op jit(solution)/shard_map/ppermute | solution.py:205
  21.9 0.7 %collective-permute-done.3.refs_2_ = bf16[2,128,128]{2,1,0:T(8,128)(2,1)S(1)} collective-permute-done((bf16[2,128,128]{2,1,0:T(8,128)(2,1)S(1)}, bf16[2,128,128]{2,1,0:T(8,128)(2,1)S(1)}, u32[]{:S(2)}, u32[]{:S(2)}) %collective-permute-start.3) | collective-permute-done | bytes 65568 | tf_op jit(solution)/shard_map/ppermute | solution.py:205
  22.6 3.6 %edge.1 = (bf16[1,128,128]{2,1,0:T(8,128)(2,1)S(1)}, bf16[257,128,128]{2,1,0:T(8,128)(2,1)S(1)}) custom-call(s32[1]{0:T(128)S(6)} %copy.18.count_ref, s32[2,512]{1,0:T(2,128)S(1)} %bitcast.7, s32[2,512]{1,0:T(2,128)S(1)} %bitcast.8, bf16[16,128,128]{2,1,0:T(8,128)(2,1)S(1)} %get-tuple-element.14.resident_ref, ...), custom_call_target="tpu_custom_call", output_to_operand_aliasing={{1}: (7, {})} | custom-call | tf_op jit(solution)/shard_map/edge/pallas_call | solution.py:301
  26.2 1.1 %collective-permute-start.8 = (bf16[1,128,128]{2,1,0:T(8,128)(2,1)S(1)}, bf16[1,128,128]{2,1,0:T(8,128)(2,1)S(1)}, u32[]{:S(2)}, u32[]{:S(2)}) collective-permute-start(bf16[1,128,128]{2,1,0:T(8,128)(2,1)S(1)} %get-tuple-element.30), channel_id=1, source_target_pairs={{0,2},{1,3},{2,0},{3,1},{4,6},{5,7},{6,4},{7,5},{8,10},{9,11},{10,... | collective-permute-start | bytes 98312 | tf_op jit(solution)/shard_map/ppermute | solution.py:205
  27.3 2.9 %collective-permute-done.8 = bf16[1,128,128]{2,1,0:T(8,128)(2,1)S(1)} collective-permute-done((bf16[1,128,128]{2,1,0:T(8,128)(2,1)S(1)}, bf16[1,128,128]{2,1,0:T(8,128)(2,1)S(1)}, u32[]{:S(2)}, u32[]{:S(2)}) %collective-permute-start.8) | collective-permute-done | bytes 32800 | tf_op jit(solution)/shard_map/ppermute | solution.py:205
  30.2 2.3 %collective-permute-start.9 = (bf16[2,128,128]{2,1,0:T(8,128)(2,1)S(1)}, bf16[2,128,128]{2,1,0:T(8,128)(2,1)S(1)}, u32[]{:S(2)}, u32[]{:S(2)}) collective-permute-start(bf16[2,128,128]{2,1,0:T(8,128)(2,1)S(1)} %get-tuple-element.26), channel_id=1, source_target_pairs={{0,4},{1,5},{2,6},{3,7},{4,0},{5,1},{6,2},{7,3},{8,12},{9,13},{10,... | collective-permute-start | bytes 196616 | tf_op jit(solution)/shard_map/ppermute | solution.py:205
  32.5 3.3 %collective-permute-start.11 = (bf16[2,128,128]{2,1,0:T(8,128)(2,1)S(1)}, bf16[2,128,128]{2,1,0:T(8,128)(2,1)S(1)}, u32[]{:S(2)}, u32[]{:S(2)}) collective-permute-start(bf16[2,128,128]{2,1,0:T(8,128)(2,1)S(1)} %get-tuple-element.26), channel_id=1, source_target_pairs={{0,12},{1,13},{2,14},{3,15},{4,8},{5,9},{6,10},{7,11},{8,4},{9,5},... | collective-permute-start | bytes 196616 | tf_op jit(solution)/shard_map/ppermute | solution.py:205
  35.8 5.1 %collective-permute-done.10 = bf16[2,128,128]{2,1,0:T(8,128)(2,1)S(1)} collective-permute-done((bf16[2,128,128]{2,1,0:T(8,128)(2,1)S(1)}, bf16[2,128,128]{2,1,0:T(8,128)(2,1)S(1)}, u32[]{:S(2)}, u32[]{:S(2)}) %collective-permute-start.10) | collective-permute-done | bytes 65568 | tf_op jit(solution)/shard_map/ppermute | solution.py:205
  41.0 0.1 collective-permute-start.12
  41.1 0.6 %copy.17 = bf16[1,128,128]{2,1,0:T(8,128)(2,1)} copy(bf16[1,128,128]{2,1,0:T(8,128)(2,1)S(1)} %get-tuple-element.30) | data formatting | bytes 65536
  41.7 0.9 %collective-permute-done.12.refs_1_ = bf16[8,128,128]{2,1,0:T(8,128)(2,1)S(1)} collective-permute-done((bf16[8,128,128]{2,1,0:T(8,128)(2,1)S(1)}, bf16[8,128,128]{2,1,0:T(8,128)(2,1)S(1)}, u32[]{:S(2)}, u32[]{:S(2)}) %collective-permute-start.12) | collective-permute-done | bytes 262176 | tf_op jit(solution)/shard_map/ppermute | solution.py:205
  42.6 1.5 %pairs.1 = bf16[8,128,128]{2,1,0:T(8,128)(2,1)} custom-call(s32[2,8]{1,0:T(2,128)S(1)} %bitcast.9, bf16[8,128,128]{2,1,0:T(8,128)(2,1)S(1)} %constant_dynamic-update-slice_fusion.2.refs_0_, bf16[8,128,128]{2,1,0:T(8,128)(2,1)S(1)} %collective-permute-done.12.refs_1_), custom_call_target="tpu_custom_call" | custom-call | tf_op jit(solution)/shard_map/pairs/pallas_call | solution.py:342
  (19 shorter events, 0.1 us)
Async XLA Ops:
  0.6 22.0 %copy-start.1 = (s32[1,512,2]{1,2,0:T(2,128)S(1)}, s32[1,512,2]{1,2,0:T(2,128)}, u32[]{:S(2)}) copy-start(s32[1,512,2]{1,2,0:T(2,128)} %param.13) | copy-start | bytes 12292
  0.6 22.0 %copy-start = (s32[1,512,2]{1,2,0:T(2,128)S(1)}, s32[1,512,2]{1,2,0:T(2,128)}, u32[]{:S(2)}) copy-start(s32[1,512,2]{1,2,0:T(2,128)} %param.12) | copy-start | bytes 12292
  2.6 1.7 %collective-permute-start = (bf16[8,128,128]{2,1,0:T(8,128)(2,1)S(1)}, bf16[8,128,128]{2,1,0:T(8,128)(2,1)S(1)}, u32[]{:S(2)}, u32[]{:S(2)}) collective-permute-start(bf16[8,128,128]{2,1,0:T(8,128)(2,1)S(1)} %get-tuple-element.16), channel_id=1, source_target_pairs={{0,1},{1,0},{2,3},{3,2},{4,5},{5,4},{6,7},{7,6},{8,9},{9,8},{10,11... | collective-permute-start | bytes 786440 | tf_op jit(solution)/shard_map/ppermute | solution.py:205
  4.4 10.6 %collective-permute-start.4 = (bf16[2,128,128]{2,1,0:T(8,128)(2,1)S(1)}, bf16[2,128,128]{2,1,0:T(8,128)(2,1)S(1)}, u32[]{:S(2)}, u32[]{:S(2)}) collective-permute-start(bf16[2,128,128]{2,1,0:T(8,128)(2,1)S(1)} %get-tuple-element.21), channel_id=1, source_target_pairs={{0,2},{1,3},{2,0},{3,1},{4,6},{5,7},{6,4},{7,5},{8,10},{9,11},{10,... | collective-permute-start | bytes 196616 | tf_op jit(solution)/shard_map/ppermute | solution.py:205
  7.3 9.9 %collective-permute-start.5 = (bf16[2,128,128]{2,1,0:T(8,128)(2,1)S(1)}, bf16[2,128,128]{2,1,0:T(8,128)(2,1)S(1)}, u32[]{:S(2)}, u32[]{:S(2)}) collective-permute-start(bf16[2,128,128]{2,1,0:T(8,128)(2,1)S(1)} %get-tuple-element.22), channel_id=1, source_target_pairs={{0,8},{1,9},{2,10},{3,11},{4,12},{5,13},{6,14},{7,15},{8,0},{9,1},... | collective-permute-start | bytes 196616 | tf_op jit(solution)/shard_map/ppermute | solution.py:205
  9.9 7.4 %collective-permute-start.6 = (bf16[2,128,128]{2,1,0:T(8,128)(2,1)S(1)}, bf16[2,128,128]{2,1,0:T(8,128)(2,1)S(1)}, u32[]{:S(2)}, u32[]{:S(2)}) collective-permute-start(bf16[2,128,128]{2,1,0:T(8,128)(2,1)S(1)} %get-tuple-element.23), channel_id=1, source_target_pairs={{0,12},{1,13},{2,14},{3,15},{4,8},{5,9},{6,10},{7,11},{8,4},{9,5},... | collective-permute-start | bytes 196616 | tf_op jit(solution)/shard_map/ppermute | solution.py:205
  11.2 6.0 %collective-permute-start.7 = (bf16[2,128,128]{2,1,0:T(8,128)(2,1)S(1)}, bf16[2,128,128]{2,1,0:T(8,128)(2,1)S(1)}, u32[]{:S(2)}, u32[]{:S(2)}) collective-permute-start(bf16[2,128,128]{2,1,0:T(8,128)(2,1)S(1)} %get-tuple-element.24), channel_id=1, source_target_pairs={{0,4},{1,5},{2,6},{3,7},{4,0},{5,1},{6,2},{7,3},{8,12},{9,13},{10,... | collective-permute-start | bytes 196616 | tf_op jit(solution)/shard_map/ppermute | solution.py:205
  12.1 8.4 %collective-permute-start.1 = (bf16[2,128,128]{2,1,0:T(8,128)(2,1)S(1)}, bf16[2,128,128]{2,1,0:T(8,128)(2,1)S(1)}, u32[]{:S(2)}, u32[]{:S(2)}) collective-permute-start(bf16[2,128,128]{2,1,0:T(8,128)(2,1)S(1)} %get-tuple-element.17), channel_id=1, source_target_pairs={{0,10},{1,11},{2,8},{3,9},{4,14},{5,15},{6,12},{7,13},{8,2},{9,3},... | collective-permute-start | bytes 196616 | tf_op jit(solution)/shard_map/ppermute | solution.py:205
  14.9 7.0 %collective-permute-start.2 = (bf16[2,128,128]{2,1,0:T(8,128)(2,1)S(1)}, bf16[2,128,128]{2,1,0:T(8,128)(2,1)S(1)}, u32[]{:S(2)}, u32[]{:S(2)}) collective-permute-start(bf16[2,128,128]{2,1,0:T(8,128)(2,1)S(1)} %get-tuple-element.18), channel_id=1, source_target_pairs={{0,14},{1,15},{2,12},{3,13},{4,10},{5,11},{6,8},{7,9},{8,6},{9,7},... | collective-permute-start | bytes 196616 | tf_op jit(solution)/shard_map/ppermute | solution.py:205
  17.3 5.4 %collective-permute-start.3 = (bf16[2,128,128]{2,1,0:T(8,128)(2,1)S(1)}, bf16[2,128,128]{2,1,0:T(8,128)(2,1)S(1)}, u32[]{:S(2)}, u32[]{:S(2)}) collective-permute-start(bf16[2,128,128]{2,1,0:T(8,128)(2,1)S(1)} %get-tuple-element.19), channel_id=1, source_target_pairs={{0,6},{1,7},{2,4},{3,5},{4,2},{5,3},{6,0},{7,1},{8,14},{9,15},{10,... | collective-permute-start | bytes 196616 | tf_op jit(solution)/shard_map/ppermute | solution.py:205
  17.3 25.4 %copy-start.2 = (s32[8,2]{0,1:T(2,128)S(1)}, s32[8,2]{0,1:T(2,128)}, u32[]{:S(2)}) copy-start(s32[8,2]{0,1:T(2,128)} %param.15) | copy-start | bytes 196
  26.2 4.0 %collective-permute-start.8 = (bf16[1,128,128]{2,1,0:T(8,128)(2,1)S(1)}, bf16[1,128,128]{2,1,0:T(8,128)(2,1)S(1)}, u32[]{:S(2)}, u32[]{:S(2)}) collective-permute-start(bf16[1,128,128]{2,1,0:T(8,128)(2,1)S(1)} %get-tuple-element.30), channel_id=1, source_target_pairs={{0,2},{1,3},{2,0},{3,1},{4,6},{5,7},{6,4},{7,5},{8,10},{9,11},{10,... | collective-permute-start | bytes 98312 | tf_op jit(solution)/shard_map/ppermute | solution.py:205
  30.2 5.6 %collective-permute-start.9 = (bf16[2,128,128]{2,1,0:T(8,128)(2,1)S(1)}, bf16[2,128,128]{2,1,0:T(8,128)(2,1)S(1)}, u32[]{:S(2)}, u32[]{:S(2)}) collective-permute-start(bf16[2,128,128]{2,1,0:T(8,128)(2,1)S(1)} %get-tuple-element.26), channel_id=1, source_target_pairs={{0,4},{1,5},{2,6},{3,7},{4,0},{5,1},{6,2},{7,3},{8,12},{9,13},{10,... | collective-permute-start | bytes 196616 | tf_op jit(solution)/shard_map/ppermute | solution.py:205
  32.5 8.5 %collective-permute-start.11 = (bf16[2,128,128]{2,1,0:T(8,128)(2,1)S(1)}, bf16[2,128,128]{2,1,0:T(8,128)(2,1)S(1)}, u32[]{:S(2)}, u32[]{:S(2)}) collective-permute-start(bf16[2,128,128]{2,1,0:T(8,128)(2,1)S(1)} %get-tuple-element.26), channel_id=1, source_target_pairs={{0,12},{1,13},{2,14},{3,15},{4,8},{5,9},{6,10},{7,11},{8,4},{9,5},... | collective-permute-start | bytes 196616 | tf_op jit(solution)/shard_map/ppermute | solution.py:205
  35.8 5.2 %collective-permute-start.10 = (bf16[2,128,128]{2,1,0:T(8,128)(2,1)S(1)}, bf16[2,128,128]{2,1,0:T(8,128)(2,1)S(1)}, u32[]{:S(2)}, u32[]{:S(2)}) collective-permute-start(bf16[2,128,128]{2,1,0:T(8,128)(2,1)S(1)} %get-tuple-element.26), channel_id=1, source_target_pairs={{0,8},{1,9},{2,10},{3,11},{4,12},{5,13},{6,14},{7,15},{8,0},{9,1},... | collective-permute-start | bytes 196616 | tf_op jit(solution)/shard_map/ppermute | solution.py:205
  41.0 1.6 %collective-permute-start.12 = (bf16[8,128,128]{2,1,0:T(8,128)(2,1)S(1)}, bf16[8,128,128]{2,1,0:T(8,128)(2,1)S(1)}, u32[]{:S(2)}, u32[]{:S(2)}) collective-permute-start(bf16[8,128,128]{2,1,0:T(8,128)(2,1)S(1)} %constant_dynamic-update-slice_fusion.2.refs_0_), channel_id=1, source_target_pairs={{0,1},{1,0},{2,3},{3,2},{4,5},{5,4},{6,7},{7,6},{8,9},{9,8},{10,11... | collective-permute-start | bytes 786440 | tf_op jit(solution)/shard_map/ppermute | solution.py:205

commit v3 on v2

--- a/solution.py
+++ b/solution.py
@@ -15,6 +15,8 @@
 HBM = pl.BlockSpec(memory_space=pltpu.HBM)
 ORDER = (1, 4, 6, 2, 5, 7, 3)
 EARLY = 4
+STEP = 64
+LANES = 128
 
 
 def params(mebibytes):
@@ -60,18 +62,24 @@
 
 
 def rotate_pairs_kernel(
-    pick_hbm, source_hbm, peram_hbm, sink_hbm, mine_ref, other_ref, resident_ref, *scratch
+    pick_hbm, source_hbm, peram_hbm, *refs
 ):
-    *scratch, sink_sem = scratch
+    later_hbm, (mine_ref, other_ref), later_refs = refs[:3], refs[3:5], refs[5:8]
+    *scratch, later_sems = refs[8:]
     pick_ref, _, _, rotated_ref, _ = scratch
-    sinks_in = pltpu.make_async_copy(sink_hbm, resident_ref, sink_sem)
-    sinks_in.start()
+    later = [
+        pltpu.make_async_copy(hbm, ref, later_sems.at[i])
+        for i, (hbm, ref) in enumerate(zip(later_hbm, later_refs))
+    ]
+    for copy in later:
+        copy.start()
     rotate_slabs(pick_hbm, source_hbm, peram_hbm, *scratch)
     me = lax.axis_index("had")
     for i in range(mine_ref.shape[0]):
         other_ref[i] = rotated_ref[pick_ref[0, me ^ (2 * i + 1)]]
         mine_ref[i] = rotated_ref[pick_ref[0, me ^ (2 * i)]]
-    sinks_in.wait()
+    for copy in later:
+        copy.wait()
 
 
 def zip_kernel(mine_ref, got_ref, *out_refs):
@@ -93,11 +101,127 @@
             ].reshape(tall, evecs, evecs)
 
 
-def factor_kernel(root_scale, first_slots, resident_ref, *refs):
-    *arrived, factor_ref = refs
+def down(row):
+    return jnp.transpose(jnp.broadcast_to(row, (LANES, row.shape[1])))
+
+
+def plan_graphs(total, slots, sinks, early, readers, sinks_each, step):
+    graphs = slots.shape[1]
+    nothing = readers * sinks_each
+
+    def is_early(slot):
+        found = [(slot >> 1) == i for i in early]
+        return functools.reduce(jnp.logical_or, found)
+
+    lane = lax.broadcasted_iota(jnp.int32, (1, graphs), 1)
+    valid = lane < total
+    both = is_early(slots[0:1]) & is_early(slots[1:2])
+    kind = jnp.where(valid, jnp.where(both, 0, 1), 2)
+    key = ((kind * readers + slots[0:1]) * sinks_each + sinks[0:1]).astype(F32)
+    key_down = down(key)
+    at = lax.broadcasted_iota(jnp.int32, (graphs, LANES), 0)
+    across = lax.broadcasted_iota(jnp.int32, (graphs, LANES), 1)
+
+    ranks = []
+    for c in range(0, graphs, LANES):
+        same = (key_down == key[:, c : c + LANES]) & (at < across + c)
+        ranks.append(jnp.sum(jnp.where(same, 1.0, 0.0), axis=0, keepdims=True))
+    rank = jnp.concatenate(ranks, axis=1).astype(jnp.int32)
+    second = valid & ((rank & 1) == 1)
+    first = valid & ((rank & 1) == 0)
+    opens = [jnp.where(first & (kind == i), 1.0, 0.0) for i in range(2)]
+    opened = jnp.concatenate(opens + [jnp.zeros((14, graphs), F32)], axis=0).astype(BF16)
+    ahead = []
+    for c in range(0, graphs, LANES):
+        before = jnp.where(at < across + c, 1.0, 0.0).astype(BF16)
+        ahead.append(jnp.dot(opened, before, preferred_element_type=F32))
+    ahead = jnp.concatenate(ahead, axis=1)
+    blocks = [jnp.sum(o, axis=1, keepdims=True).astype(jnp.int32) for o in opens]
+    late_start = ((blocks[0] + step - 1) // step * step).astype(F32)
+    block = jnp.where(
+        first, jnp.where(kind == 0, ahead[0:1], late_start + ahead[1:2]), -1.0
+    )
+    mark = (key * graphs + (rank >> 1).astype(F32) + 1.0) * 2.0 + jnp.where(second, 1.0, 0.0)
+    block_down, mark_down = down(block), down(mark)
+
+    ones = jnp.ones((1, graphs), F32)
+    columns = [slots[1:2].astype(F32), sinks[1:2].astype(F32), ones]
+    columns += [slots[0:1].astype(F32), sinks[0:1].astype(F32)]
+    values = jnp.concatenate(columns + [jnp.zeros((11, graphs), F32)], axis=0).astype(BF16)
+    tables = []
+    for c in range(0, graphs + LANES, LANES):
+        opener = block_down == (across[:1] + c).astype(F32)
+        opener_mark = jnp.sum(jnp.where(opener, mark_down, 0.0), axis=0, keepdims=True)
+        closer = mark_down == opener_mark + 1.0
+        one = jnp.dot(values, jnp.where(opener, 1.0, 0.0).astype(BF16), preferred_element_type=F32)
+        two = jnp.dot(values, jnp.where(closer, 1.0, 0.0).astype(BF16), preferred_element_type=F32)
+        rows = [
+            jnp.where(one[2:3] > 0.5, one[3:4] * sinks_each + one[4:5], nothing),
+            jnp.where(one[2:3] > 0.5, one[0:1] * sinks_each + one[1:2], nothing),
+            jnp.where(two[2:3] > 0.5, two[0:1] * sinks_each + two[1:2], nothing),
+        ]
+        counts = jnp.where(across[:1] == 0, blocks[0], blocks[1])
+        rows = [row.astype(jnp.int32) for row in rows] + [counts]
+        tables.append(jnp.concatenate(rows + [jnp.zeros((4, LANES), jnp.int32)], axis=0))
+    return jnp.concatenate(tables, axis=1)
+
+
+def add_blocks(total_sum, table_ref, factor_ref, start, stop, step):
+    def body(b, total_sum):
+        base = b * step
+        left = jnp.concatenate([factor_ref[table_ref[0, base + i]] for i in range(step)], axis=1)
+        right = jnp.concatenate(
+            [
+                jnp.concatenate(
+                    [factor_ref[table_ref[1, base + i]], factor_ref[table_ref[2, base + i]]], axis=1
+                )
+                for i in range(step)
+            ],
+            axis=0,
+        )
+        return total_sum + jnp.dot(left, right, preferred_element_type=F32)
+
+    return lax.fori_loop(start, stop, body, total_sum)
+
+
+def steps_of(count, step):
+    return (count + step - 1) // step
+
+
+def plan_kernel(step, readers, sinks, early, count_ref, slot_ref, sink_ref, table_ref):
+    me = lax.axis_index("had")
+    table_ref[...] = plan_graphs(
+        count_ref[0], slot_ref[...] ^ me, sink_ref[...], early, readers, sinks, step
+    )
+
+
+def early_kernel(step, root_scale, early, table_ref, resident_ref, *refs):
+    *arrived, factor_ref, sum_ref, smem_ref, sem = refs
     _, evecs, _ = resident_ref.shape
-    for first_slot, ref in zip(first_slots, arrived):
-        fill_factors(factor_ref, resident_ref, ref[...].reshape(-1, evecs), first_slot, root_scale)
+    copy = pltpu.make_async_copy(table_ref, smem_ref, sem)
+    copy.start()
+    for i, ref in zip(early, arrived):
+        fill_factors(factor_ref, resident_ref, ref[...].reshape(-1, evecs), 2 * i, root_scale)
+    factor_ref[factor_ref.shape[0] - 1] = jnp.zeros((evecs, evecs), BF16)
+    copy.wait()
+    stop = steps_of(smem_ref[3, 0], step)
+    sum_ref[...] = add_blocks(
+        jnp.zeros((evecs, 2 * evecs), F32), smem_ref, factor_ref, 0, stop, step
+    )
+
+
+def late_kernel(step, root_scale, edge_scale, late, table_ref, sum_ref, resident_ref, *refs):
+    *arrived, _, out_ref, factor_ref, smem_ref, sem = refs
+    _, evecs, _ = resident_ref.shape
+    copy = pltpu.make_async_copy(table_ref, smem_ref, sem)
+    copy.start()
+    for i, ref in zip(late, arrived):
+        fill_factors(factor_ref, resident_ref, ref[...].reshape(-1, evecs), 2 * i, root_scale)
+    copy.wait()
+    start = steps_of(smem_ref[3, 0], step)
+    stop = start + steps_of(smem_ref[3, 1], step)
+    both = add_blocks(sum_ref[...], smem_ref, factor_ref, start, stop, step)
+    out_ref[0] = ((both[:, :evecs] + both[:, evecs:]) * edge_scale).astype(BF16)
 
 
 def graph_sum(block, total, factor, evecs):
@@ -110,35 +234,6 @@
     return lax.fori_loop(
         0, (total + block - 1) // block, step, jnp.zeros((evecs, evecs), F32)
     )
-
-
-def masked_edge_kernel(
-    block, root_scale, edge_scale, first_slots, count_ref, slot_hbm, sink_hbm, resident_ref, *refs
-):
-    *arrived, _, out_ref, factor_ref, slot_ref, sink_ref, sems = refs
-    sinks, evecs, _ = resident_ref.shape
-    copies = [
-        pltpu.make_async_copy(slot_hbm, slot_ref, sems.at[0]),
-        pltpu.make_async_copy(sink_hbm, sink_ref, sems.at[1]),
-    ]
-    for copy in copies:
-        copy.start()
-    for first_slot, ref in zip(first_slots, arrived):
-        fill_factors(factor_ref, resident_ref, ref[...].reshape(-1, evecs), first_slot, root_scale)
-    nothing = factor_ref.shape[0] - 1
-    factor_ref[nothing] = jnp.zeros((evecs, evecs), BF16)
-    for copy in copies:
-        copy.wait()
-    me = lax.axis_index("had")
-    total = count_ref[0]
-
-    def factor(side, g):
-        row = (slot_ref[side, g] ^ me) * sinks + sink_ref[side, g]
-        if side == 0:
-            row = jnp.where(g < total, row, nothing)
-        return factor_ref[row]
-
-    out_ref[0] = (graph_sum(block, total, factor, evecs) * edge_scale).astype(BF16)
 
 
 def edge_kernel(block, root_scale, edge_scale, count_ref, slot_ref, sink_ref, received_ref, resident_ref, out_ref, *factors):
@@ -256,21 +351,29 @@
     ]
     counts = (graph_count, graph_slot[0].T, graph_sink[0].T)
 
-    if dense and by_xor(readers):
+    if dense and by_xor(readers) and graphs % LANES == 0:
         half = readers // 2
-        mine, other, resident = pl.pallas_call(
+        mine, other, resident, slot_table, sink_table = pl.pallas_call(
             rotate_pairs_kernel,
             out_shape=[
                 pltpu.VMEM((half,) + slab, BF16),
                 pltpu.VMEM((half,) + slab, BF16),
                 pltpu.VMEM((sinks,) + slab, BF16),
-            ],
-            in_specs=[HBM] * 4,
-            out_specs=[VMEM] * 3,
-            scratch_shapes=rotate_scratch + [pltpu.SemaphoreType.DMA],
+                pltpu.VMEM((2, graphs), jnp.int32),
+                pltpu.VMEM((2, graphs), jnp.int32),
+            ],
+            in_specs=[HBM] * 6,
+            out_specs=[VMEM] * 5,
+            scratch_shapes=rotate_scratch + [pltpu.SemaphoreType.DMA((3,))],
             compiler_params=params(16),
             name="rotate",
-        )(*rotate_args, pltpu.with_memory_space_constraint(sink_slabs, pltpu.HBM))
+        )(
+            *rotate_args,
+            *[
+                pltpu.with_memory_space_constraint(array, pltpu.HBM)
+                for array in (sink_slabs, *counts[1:])
+            ],
+        )
         got = xor_permute(other, readers, 1)
         pairs_for = pl.pallas_call(
             zip_kernel,
@@ -287,36 +390,49 @@
         early = [0] + order[:EARLY]
         late = order[EARLY:]
         rows = readers * sinks + 1
-        factors = pl.pallas_call(
-            functools.partial(factor_kernel, root_scale, [2 * i for i in early]),
-            out_shape=pltpu.VMEM((rows,) + slab, BF16),
-            in_specs=[VMEM] * (1 + len(early)),
+        table = pl.pallas_call(
+            functools.partial(plan_kernel, STEP, readers, sinks, early),
+            out_shape=pltpu.VMEM((8, graphs + LANES), jnp.int32),
+            in_specs=[SMEM, VMEM, VMEM],
             out_specs=VMEM,
+            compiler_params=params(16),
+            cost_estimate=pl.CostEstimate(flops=10**8, bytes_accessed=0, transcendentals=0),
+            name="plan",
+        )(graph_count, slot_table, sink_table)
+        factors, early_sum = pl.pallas_call(
+            functools.partial(early_kernel, STEP, root_scale, early),
+            out_shape=[
+                pltpu.VMEM((rows,) + slab, BF16),
+                pltpu.VMEM((evecs, 2 * evecs), F32),
+            ],
+            in_specs=[VMEM] * (2 + len(early)),
+            out_specs=[VMEM] * 2,
+            scratch_shapes=[
+                pltpu.SMEM((8, graphs + LANES), jnp.int32),
+                pltpu.SemaphoreType.DMA,
+            ],
             compiler_params=params(16),
             cost_estimate=pl.CostEstimate(
                 flops=8 * len(early) * sinks * evecs**3, bytes_accessed=0, transcendentals=0
             ),
-            name="factors",
-        )(resident, *[arrived[i] for i in early])
+            name="early",
+        )(table, resident, *[arrived[i] for i in early])
         edge, _ = pl.pallas_call(
-            functools.partial(
-                masked_edge_kernel, block, root_scale, edge_scale, [2 * i for i in late]
-            ),
+            functools.partial(late_kernel, STEP, root_scale, edge_scale, late),
             out_shape=[
                 pltpu.VMEM((1,) + slab, BF16),
                 pltpu.VMEM((rows,) + slab, BF16),
             ],
-            in_specs=[SMEM, HBM, HBM] + [VMEM] * (2 + len(late)),
+            in_specs=[VMEM] * (4 + len(late)),
             out_specs=[VMEM] * 2,
             scratch_shapes=[
-                pltpu.SMEM((2, graphs), jnp.int32),
-                pltpu.SMEM((2, graphs), jnp.int32),
-                pltpu.SemaphoreType.DMA((2,)),
-            ],
-            input_output_aliases={4 + len(late): 1},
+                pltpu.SMEM((8, graphs + LANES), jnp.int32),
+                pltpu.SemaphoreType.DMA,
+            ],
+            input_output_aliases={3 + len(late): 1},
             compiler_params=params(16),
             name="edge",
-        )(*counts, resident, *[arrived[i] for i in late], factors)
+        )(table, early_sum, resident, *[arrived[i] for i in late], factors)
     else:
         outgoing = pl.pallas_call(
             rotate_kernel,

time: 44.2 us -> 42.2 us (0.955)
  Pallas kernels: 8.66 us -> 12 us
  starting transfers between devices: 19.5 us -> 16.4 us
  waiting for transfers between devices: 13.9 us -> 11.9 us
    pallas_call x2 -> x3, Pallas kernels: 5.14 us -> 8.45 us  [the longest x1 3.9 us: shards(): pl.pallas_call(functools.partial(late_kernel, STEP, root_scale, edge_scal...]
    ppermute x13, starting transfers between devices: 19.5 us -> 16.4 us  [xor_permute(): return lax.ppermute(array, 'had', [(d, d ^ mask) for d in range(readers)])]
    ppermute x13, waiting for transfers between devices: 13.9 us -> 11.9 us  [xor_permute(): return lax.ppermute(array, 'had', [(d, d ^ mask) for d in range(readers)])]
  transfers between devices with their start and end apart: 13 -> 13, of which waited for: 7 -> 7; matrix products, arithmetic and copies ran while one was open for 1% -> 2% of each run, Pallas kernels for 3% -> 11%
where the time goes in v3:
time: 42.2 us; the launch traced here: 42.4 us
  starting transfers between devices  16.4 us (39%)
  Pallas kernels  12 us (28%)
  waiting for transfers between devices  11.9 us (28%)
  between operations  1.4 us (3%)
  local copies, waits for them, and re-layouts  0.68 us (2%)
    ppermute x13, starting transfers between devices, xor_permute(): return lax.ppermute(array, 'had', [(d, d ^ mask) for d in range(readers)])  16.4 us
    ppermute x13, waiting for transfers between devices, xor_permute(): return lax.ppermute(array, 'had', [(d, d ^ mask) for d in range(readers)])  11.9 us
    pallas_call x1, Pallas kernels, shards(): pl.pallas_call(functools.partial(late_kernel, STEP, root_scale, edge_scal...  3.9 us
    pallas_call x1, Pallas kernels, shards(): pl.pallas_call(functools.partial(early_kernel, STEP, root_scale, early),...  3.73 us
    pallas_call x1, Pallas kernels, shards(): pl.pallas_call(rotate_pairs_kernel, out_shape=[pltpu.VMEM((half,) + slab,...  2.02 us
    pallas_call x1, Pallas kernels, shards(): pl.pallas_call(functools.partial(pair_kernel, root_scale, place), out_sha...  1.51 us
  transfers between devices with their start and end apart: 13, of which 7 were waited for; matrix products, arithmetic and copies ran while one was open for 2% of the time, Pallas kernels for 11%

profile of v3, /device:TPU:0, one launch (start us, length us, event | category | flops | bytes accessed | tf_op | source)
XLA Modules:
  0.0 42.4 jit_solution(4094403245683694300)
XLA Ops:
  0.6 2.0 %rotate.1 = (bf16[8,128,128]{2,1,0:T(8,128)(2,1)S(1)}, bf16[8,128,128]{2,1,0:T(8,128)(2,1)S(1)}, bf16[16,128,128]{2,1,0:T(8,128)(2,1)S(1)}, s32[2,512]{1,0:T(2,128)S(1)}, s32[2,512]{1,0:T(2,128)S(1)}) custom-call(s32[1,16]{1,0:T(1,128)} %pick_hbm.1, bf16[16,128,128]{2,1,0:T(8,128)(2,1)} %source_hbm.1, bf16[2,2,128,128]{3,2,1,0:T(8,128)(2,1)} %peram_hbm.1, ...), custom_call_target="tpu_custom_call" | custom-call | tf_op jit(solution)/shard_map/rotate/pallas_call | solution.py:356
  2.7 0.5 %collective-permute-start = (bf16[8,128,128]{2,1,0:T(8,128)(2,1)S(1)}, bf16[8,128,128]{2,1,0:T(8,128)(2,1)S(1)}, u32[]{:S(2)}, u32[]{:S(2)}) collective-permute-start(bf16[8,128,128]{2,1,0:T(8,128)(2,1)S(1)} %get-tuple-element.22), channel_id=1, source_target_pairs={{0,1},{1,0},{2,3},{3,2},{4,5},{5,4},{6,7},{7,6},{8,9},{9,8},{10,11... | collective-permute-start | bytes 786440 | tf_op jit(solution)/shard_map/ppermute | solution.py:300
  3.2 1.2 %collective-permute-done.got_ref = bf16[8,128,128]{2,1,0:T(8,128)(2,1)S(1)} collective-permute-done((bf16[8,128,128]{2,1,0:T(8,128)(2,1)S(1)}, bf16[8,128,128]{2,1,0:T(8,128)(2,1)S(1)}, u32[]{:S(2)}, u32[]{:S(2)}) %collective-permute-start) | collective-permute-done | bytes 262176 | tf_op jit(solution)/shard_map/ppermute | solution.py:300
  4.4 3.0 %collective-permute-start.1 = (bf16[2,128,128]{2,1,0:T(8,128)(2,1)S(1)}, bf16[2,128,128]{2,1,0:T(8,128)(2,1)S(1)}, u32[]{:S(2)}, u32[]{:S(2)}) collective-permute-start(bf16[2,128,128]{2,1,0:T(8,128)(2,1)S(1)} %get-tuple-element.24), channel_id=1, source_target_pairs={{0,2},{1,3},{2,0},{3,1},{4,6},{5,7},{6,4},{7,5},{8,10},{9,11},{10,... | collective-permute-start | bytes 196616 | tf_op jit(solution)/shard_map/ppermute | solution.py:300
  7.3 2.6 %collective-permute-start.2 = (bf16[2,128,128]{2,1,0:T(8,128)(2,1)S(1)}, bf16[2,128,128]{2,1,0:T(8,128)(2,1)S(1)}, u32[]{:S(2)}, u32[]{:S(2)}) collective-permute-start(bf16[2,128,128]{2,1,0:T(8,128)(2,1)S(1)} %get-tuple-element.25), channel_id=1, source_target_pairs={{0,8},{1,9},{2,10},{3,11},{4,12},{5,13},{6,14},{7,15},{8,0},{9,1},... | collective-permute-start | bytes 196616 | tf_op jit(solution)/shard_map/ppermute | solution.py:300
  9.9 1.3 %collective-permute-start.3 = (bf16[2,128,128]{2,1,0:T(8,128)(2,1)S(1)}, bf16[2,128,128]{2,1,0:T(8,128)(2,1)S(1)}, u32[]{:S(2)}, u32[]{:S(2)}) collective-permute-start(bf16[2,128,128]{2,1,0:T(8,128)(2,1)S(1)} %get-tuple-element.26), channel_id=1, source_target_pairs={{0,12},{1,13},{2,14},{3,15},{4,8},{5,9},{6,10},{7,11},{8,4},{9,5},... | collective-permute-start | bytes 196616 | tf_op jit(solution)/shard_map/ppermute | solution.py:300
  11.3 0.2 collective-permute-start.4
  12.2 0.8 %plan.1.table_ref = s32[8,640]{1,0:T(8,128)S(1)} custom-call(s32[1]{0:T(128)S(6)} %copy.18.count_ref, s32[2,512]{1,0:T(2,128)S(1)} %get-tuple-element.18.slot_ref, s32[2,512]{1,0:T(2,128)S(1)} %get-tuple-element.19.sink_ref), custom_call_target="tpu_custom_call" | custom-call | flops 100000000 | tf_op jit(solution)/shard_map/plan/pallas_call | solution.py:393
  13.0 2.8 %collective-permute-start.5 = (bf16[2,128,128]{2,1,0:T(8,128)(2,1)S(1)}, bf16[2,128,128]{2,1,0:T(8,128)(2,1)S(1)}, u32[]{:S(2)}, u32[]{:S(2)}) collective-permute-start(bf16[2,128,128]{2,1,0:T(8,128)(2,1)S(1)} %get-tuple-element.29), channel_id=1, source_target_pairs={{0,10},{1,11},{2,8},{3,9},{4,14},{5,15},{6,12},{7,13},{8,2},{9,3},... | collective-permute-start | bytes 196616 | tf_op jit(solution)/shard_map/ppermute | solution.py:300
  15.8 2.3 %collective-permute-start.6 = (bf16[2,128,128]{2,1,0:T(8,128)(2,1)S(1)}, bf16[2,128,128]{2,1,0:T(8,128)(2,1)S(1)}, u32[]{:S(2)}, u32[]{:S(2)}) collective-permute-start(bf16[2,128,128]{2,1,0:T(8,128)(2,1)S(1)} %get-tuple-element.30), channel_id=1, source_target_pairs={{0,14},{1,15},{2,12},{3,13},{4,10},{5,11},{6,8},{7,9},{8,6},{9,7},... | collective-permute-start | bytes 196616 | tf_op jit(solution)/shard_map/ppermute | solution.py:300
  18.1 3.7 %early.1 = (bf16[257,128,128]{2,1,0:T(8,128)(2,1)S(1)}, f32[128,256]{1,0:T(8,128)S(1)}) custom-call(s32[8,640]{1,0:T(8,128)S(1)} %plan.1.table_ref, bf16[16,128,128]{2,1,0:T(8,128)(2,1)S(1)} %get-tuple-element.20.resident_ref, bf16[2,128,128]{2,1,0:T(8,128)(2,1)S(1)} %get-tuple-element.23.refs_0_, bf16[2,128,128]{2,1,0:T(8,128)(2,1)S(1)} %collective-permute-done.1.refs_1_, ...), custom_call_target="tpu_custom_call" | custom-call | flops 1342177280 | tf_op jit(solution)/shard_map/early/pallas_call | solution.py:402
  21.9 0.9 %collective-permute-done.6.refs_1_ = bf16[2,128,128]{2,1,0:T(8,128)(2,1)S(1)} collective-permute-done((bf16[2,128,128]{2,1,0:T(8,128)(2,1)S(1)}, bf16[2,128,128]{2,1,0:T(8,128)(2,1)S(1)}, u32[]{:S(2)}, u32[]{:S(2)}) %collective-permute-start.6) | collective-permute-done | bytes 65568 | tf_op jit(solution)/shard_map/ppermute | solution.py:300
  22.8 0.7 %collective-permute-done.7.refs_2_ = bf16[2,128,128]{2,1,0:T(8,128)(2,1)S(1)} collective-permute-done((bf16[2,128,128]{2,1,0:T(8,128)(2,1)S(1)}, bf16[2,128,128]{2,1,0:T(8,128)(2,1)S(1)}, u32[]{:S(2)}, u32[]{:S(2)}) %collective-permute-start.7) | collective-permute-done | bytes 65568 | tf_op jit(solution)/shard_map/ppermute | solution.py:300
  23.5 3.9 %edge.1 = (bf16[1,128,128]{2,1,0:T(8,128)(2,1)S(1)}, bf16[257,128,128]{2,1,0:T(8,128)(2,1)S(1)}) custom-call(s32[8,640]{1,0:T(8,128)S(1)} %plan.1.table_ref, f32[128,256]{1,0:T(8,128)S(1)} %get-tuple-element.28.sum_ref, bf16[16,128,128]{2,1,0:T(8,128)(2,1)S(1)} %get-tuple-element.20.resident_ref, ...), custom_call_target="tpu_custom_call", output_to_operand_aliasing={{1}: (6, {})} | custom-call | tf_op jit(solution)/shard_map/edge/pallas_call | solution.py:420
  27.4 0.1 collective-permute-start.8
  27.5 3.9 %collective-permute-done.8 = bf16[1,128,128]{2,1,0:T(8,128)(2,1)S(1)} collective-permute-done((bf16[1,128,128]{2,1,0:T(8,128)(2,1)S(1)}, bf16[1,128,128]{2,1,0:T(8,128)(2,1)S(1)}, u32[]{:S(2)}, u32[]{:S(2)}) %collective-permute-start.8) | collective-permute-done | bytes 32800 | tf_op jit(solution)/shard_map/ppermute | solution.py:300
  31.4 0.1 collective-permute-start.9
  31.5 1.5 %collective-permute-start.11 = (bf16[2,128,128]{2,1,0:T(8,128)(2,1)S(1)}, bf16[2,128,128]{2,1,0:T(8,128)(2,1)S(1)}, u32[]{:S(2)}, u32[]{:S(2)}) collective-permute-start(bf16[2,128,128]{2,1,0:T(8,128)(2,1)S(1)} %get-tuple-element.34), channel_id=1, source_target_pairs={{0,12},{1,13},{2,14},{3,15},{4,8},{5,9},{6,10},{7,11},{8,4},{9,5},... | collective-permute-start | bytes 196616 | tf_op jit(solution)/shard_map/ppermute | solution.py:300
  33.0 2.0 %collective-permute-start.10 = (bf16[2,128,128]{2,1,0:T(8,128)(2,1)S(1)}, bf16[2,128,128]{2,1,0:T(8,128)(2,1)S(1)}, u32[]{:S(2)}, u32[]{:S(2)}) collective-permute-start(bf16[2,128,128]{2,1,0:T(8,128)(2,1)S(1)} %get-tuple-element.34), channel_id=1, source_target_pairs={{0,8},{1,9},{2,10},{3,11},{4,12},{5,13},{6,14},{7,15},{8,0},{9,1},... | collective-permute-start | bytes 196616 | tf_op jit(solution)/shard_map/ppermute | solution.py:300
  34.9 1.5 %collective-permute-done.9 = bf16[2,128,128]{2,1,0:T(8,128)(2,1)S(1)} collective-permute-done((bf16[2,128,128]{2,1,0:T(8,128)(2,1)S(1)}, bf16[2,128,128]{2,1,0:T(8,128)(2,1)S(1)}, u32[]{:S(2)}, u32[]{:S(2)}) %collective-permute-start.9) | collective-permute-done | bytes 65568 | tf_op jit(solution)/shard_map/ppermute | solution.py:300
  36.4 2.9 %collective-permute-done.10 = bf16[2,128,128]{2,1,0:T(8,128)(2,1)S(1)} collective-permute-done((bf16[2,128,128]{2,1,0:T(8,128)(2,1)S(1)}, bf16[2,128,128]{2,1,0:T(8,128)(2,1)S(1)}, u32[]{:S(2)}, u32[]{:S(2)}) %collective-permute-start.10) | collective-permute-done | bytes 65568 | tf_op jit(solution)/shard_map/ppermute | solution.py:300
  39.4 0.6 %copy.17 = bf16[1,128,128]{2,1,0:T(8,128)(2,1)} copy(bf16[1,128,128]{2,1,0:T(8,128)(2,1)S(1)} %get-tuple-element.38) | data formatting | bytes 65536
  40.0 0.9 %collective-permute-done.12.refs_1_ = bf16[8,128,128]{2,1,0:T(8,128)(2,1)S(1)} collective-permute-done((bf16[8,128,128]{2,1,0:T(8,128)(2,1)S(1)}, bf16[8,128,128]{2,1,0:T(8,128)(2,1)S(1)}, u32[]{:S(2)}, u32[]{:S(2)}) %collective-permute-start.12) | collective-permute-done | bytes 262176 | tf_op jit(solution)/shard_map/ppermute | solution.py:300
  40.9 1.5 %pairs.1 = bf16[8,128,128]{2,1,0:T(8,128)(2,1)} custom-call(s32[2,8]{1,0:T(2,128)S(1)} %bitcast.7, bf16[8,128,128]{2,1,0:T(8,128)(2,1)S(1)} %constant_dynamic-update-slice_fusion.2.refs_0_, bf16[8,128,128]{2,1,0:T(8,128)(2,1)S(1)} %collective-permute-done.12.refs_1_), custom_call_target="tpu_custom_call" | custom-call | tf_op jit(solution)/shard_map/pairs/pallas_call | solution.py:458
  (16 shorter events, 0.2 us)
Async XLA Ops:
  0.6 40.3 %copy-start = (s32[8,2]{0,1:T(2,128)S(1)}, s32[8,2]{0,1:T(2,128)}, u32[]{:S(2)}) copy-start(s32[8,2]{0,1:T(2,128)} %param.15) | copy-start | bytes 196
  2.7 1.7 %collective-permute-start = (bf16[8,128,128]{2,1,0:T(8,128)(2,1)S(1)}, bf16[8,128,128]{2,1,0:T(8,128)(2,1)S(1)}, u32[]{:S(2)}, u32[]{:S(2)}) collective-permute-start(bf16[8,128,128]{2,1,0:T(8,128)(2,1)S(1)} %get-tuple-element.22), channel_id=1, source_target_pairs={{0,1},{1,0},{2,3},{3,2},{4,5},{5,4},{6,7},{7,6},{8,9},{9,8},{10,11... | collective-permute-start | bytes 786440 | tf_op jit(solution)/shard_map/ppermute | solution.py:300
  4.4 11.4 %collective-permute-start.1 = (bf16[2,128,128]{2,1,0:T(8,128)(2,1)S(1)}, bf16[2,128,128]{2,1,0:T(8,128)(2,1)S(1)}, u32[]{:S(2)}, u32[]{:S(2)}) collective-permute-start(bf16[2,128,128]{2,1,0:T(8,128)(2,1)S(1)} %get-tuple-element.24), channel_id=1, source_target_pairs={{0,2},{1,3},{2,0},{3,1},{4,6},{5,7},{6,4},{7,5},{8,10},{9,11},{10,... | collective-permute-start | bytes 196616 | tf_op jit(solution)/shard_map/ppermute | solution.py:300
  7.3 10.8 %collective-permute-start.2 = (bf16[2,128,128]{2,1,0:T(8,128)(2,1)S(1)}, bf16[2,128,128]{2,1,0:T(8,128)(2,1)S(1)}, u32[]{:S(2)}, u32[]{:S(2)}) collective-permute-start(bf16[2,128,128]{2,1,0:T(8,128)(2,1)S(1)} %get-tuple-element.25), channel_id=1, source_target_pairs={{0,8},{1,9},{2,10},{3,11},{4,12},{5,13},{6,14},{7,15},{8,0},{9,1},... | collective-permute-start | bytes 196616 | tf_op jit(solution)/shard_map/ppermute | solution.py:300
  9.9 8.2 %collective-permute-start.3 = (bf16[2,128,128]{2,1,0:T(8,128)(2,1)S(1)}, bf16[2,128,128]{2,1,0:T(8,128)(2,1)S(1)}, u32[]{:S(2)}, u32[]{:S(2)}) collective-permute-start(bf16[2,128,128]{2,1,0:T(8,128)(2,1)S(1)} %get-tuple-element.26), channel_id=1, source_target_pairs={{0,12},{1,13},{2,14},{3,15},{4,8},{5,9},{6,10},{7,11},{8,4},{9,5},... | collective-permute-start | bytes 196616 | tf_op jit(solution)/shard_map/ppermute | solution.py:300
  11.3 6.9 %collective-permute-start.4 = (bf16[2,128,128]{2,1,0:T(8,128)(2,1)S(1)}, bf16[2,128,128]{2,1,0:T(8,128)(2,1)S(1)}, u32[]{:S(2)}, u32[]{:S(2)}) collective-permute-start(bf16[2,128,128]{2,1,0:T(8,128)(2,1)S(1)} %get-tuple-element.27), channel_id=1, source_target_pairs={{0,4},{1,5},{2,6},{3,7},{4,0},{5,1},{6,2},{7,3},{8,12},{9,13},{10,... | collective-permute-start | bytes 196616 | tf_op jit(solution)/shard_map/ppermute | solution.py:300
  13.0 8.9 %collective-permute-start.5 = (bf16[2,128,128]{2,1,0:T(8,128)(2,1)S(1)}, bf16[2,128,128]{2,1,0:T(8,128)(2,1)S(1)}, u32[]{:S(2)}, u32[]{:S(2)}) collective-permute-start(bf16[2,128,128]{2,1,0:T(8,128)(2,1)S(1)} %get-tuple-element.29), channel_id=1, source_target_pairs={{0,10},{1,11},{2,8},{3,9},{4,14},{5,15},{6,12},{7,13},{8,2},{9,3},... | collective-permute-start | bytes 196616 | tf_op jit(solution)/shard_map/ppermute | solution.py:300
  15.8 7.0 %collective-permute-start.6 = (bf16[2,128,128]{2,1,0:T(8,128)(2,1)S(1)}, bf16[2,128,128]{2,1,0:T(8,128)(2,1)S(1)}, u32[]{:S(2)}, u32[]{:S(2)}) collective-permute-start(bf16[2,128,128]{2,1,0:T(8,128)(2,1)S(1)} %get-tuple-element.30), channel_id=1, source_target_pairs={{0,14},{1,15},{2,12},{3,13},{4,10},{5,11},{6,8},{7,9},{8,6},{9,7},... | collective-permute-start | bytes 196616 | tf_op jit(solution)/shard_map/ppermute | solution.py:300
  18.1 5.4 %collective-permute-start.7 = (bf16[2,128,128]{2,1,0:T(8,128)(2,1)S(1)}, bf16[2,128,128]{2,1,0:T(8,128)(2,1)S(1)}, u32[]{:S(2)}, u32[]{:S(2)}) collective-permute-start(bf16[2,128,128]{2,1,0:T(8,128)(2,1)S(1)} %get-tuple-element.31), channel_id=1, source_target_pairs={{0,6},{1,7},{2,4},{3,5},{4,2},{5,3},{6,0},{7,1},{8,14},{9,15},{10,... | collective-permute-start | bytes 196616 | tf_op jit(solution)/shard_map/ppermute | solution.py:300
  27.4 4.0 %collective-permute-start.8 = (bf16[1,128,128]{2,1,0:T(8,128)(2,1)S(1)}, bf16[1,128,128]{2,1,0:T(8,128)(2,1)S(1)}, u32[]{:S(2)}, u32[]{:S(2)}) collective-permute-start(bf16[1,128,128]{2,1,0:T(8,128)(2,1)S(1)} %get-tuple-element.38), channel_id=1, source_target_pairs={{0,2},{1,3},{2,0},{3,1},{4,6},{5,7},{6,4},{7,5},{8,10},{9,11},{10,... | collective-permute-start | bytes 98312 | tf_op jit(solution)/shard_map/ppermute | solution.py:300
  31.4 5.0 %collective-permute-start.9 = (bf16[2,128,128]{2,1,0:T(8,128)(2,1)S(1)}, bf16[2,128,128]{2,1,0:T(8,128)(2,1)S(1)}, u32[]{:S(2)}, u32[]{:S(2)}) collective-permute-start(bf16[2,128,128]{2,1,0:T(8,128)(2,1)S(1)} %get-tuple-element.34), channel_id=1, source_target_pairs={{0,4},{1,5},{2,6},{3,7},{4,0},{5,1},{6,2},{7,3},{8,12},{9,13},{10,... | collective-permute-start | bytes 196616 | tf_op jit(solution)/shard_map/ppermute | solution.py:300
  31.5 7.8 %collective-permute-start.11 = (bf16[2,128,128]{2,1,0:T(8,128)(2,1)S(1)}, bf16[2,128,128]{2,1,0:T(8,128)(2,1)S(1)}, u32[]{:S(2)}, u32[]{:S(2)}) collective-permute-start(bf16[2,128,128]{2,1,0:T(8,128)(2,1)S(1)} %get-tuple-element.34), channel_id=1, source_target_pairs={{0,12},{1,13},{2,14},{3,15},{4,8},{5,9},{6,10},{7,11},{8,4},{9,5},... | collective-permute-start | bytes 196616 | tf_op jit(solution)/shard_map/ppermute | solution.py:300
  33.0 6.3 %collective-permute-start.10 = (bf16[2,128,128]{2,1,0:T(8,128)(2,1)S(1)}, bf16[2,128,128]{2,1,0:T(8,128)(2,1)S(1)}, u32[]{:S(2)}, u32[]{:S(2)}) collective-permute-start(bf16[2,128,128]{2,1,0:T(8,128)(2,1)S(1)} %get-tuple-element.34), channel_id=1, source_target_pairs={{0,8},{1,9},{2,10},{3,11},{4,12},{5,13},{6,14},{7,15},{8,0},{9,1},... | collective-permute-start | bytes 196616 | tf_op jit(solution)/shard_map/ppermute | solution.py:300
  39.3 1.6 %collective-permute-start.12 = (bf16[8,128,128]{2,1,0:T(8,128)(2,1)S(1)}, bf16[8,128,128]{2,1,0:T(8,128)(2,1)S(1)}, u32[]{:S(2)}, u32[]{:S(2)}) collective-permute-start(bf16[8,128,128]{2,1,0:T(8,128)(2,1)S(1)} %constant_dynamic-update-slice_fusion.2.refs_0_), channel_id=1, source_target_pairs={{0,1},{1,0},{2,3},{3,2},{4,5},{5,4},{6,7},{7,6},{8,9},{9,8},{10,11... | collective-permute-start | bytes 786440 | tf_op jit(solution)/shard_map/ppermute | solution.py:300

commit v4 on v3

--- a/solution.py
+++ b/solution.py
@@ -27,7 +27,7 @@
     return lax.dot_general(left, right, (((1,), (1,)), ((), ())), preferred_element_type=F32)
 
 
-def rotate_slabs(pick_hbm, source_hbm, peram_hbm, pick_ref, source_ref, peram_ref, rotated_ref, sems):
+def rotate_slabs(pick_hbm, source_hbm, peram_hbm, pick_ref, source_ref, peram_ref, rotated_ref, sems, later=()):
     per_device, evecs, _ = source_ref.shape
     timeslice = lax.axis_index("had") * per_device // evecs
     copies = [
@@ -35,7 +35,7 @@
         pltpu.make_async_copy(source_hbm, source_ref, sems.at[1]),
         pltpu.make_async_copy(pick_hbm, pick_ref, sems.at[2]),
     ]
-    for copy in copies:
+    for copy in [*copies, *later]:
         copy.start()
     for copy in copies:
         copy.wait()
@@ -71,9 +71,7 @@
         pltpu.make_async_copy(hbm, ref, later_sems.at[i])
         for i, (hbm, ref) in enumerate(zip(later_hbm, later_refs))
     ]
-    for copy in later:
-        copy.start()
-    rotate_slabs(pick_hbm, source_hbm, peram_hbm, *scratch)
+    rotate_slabs(pick_hbm, source_hbm, peram_hbm, *scratch, later=later)
     me = lax.axis_index("had")
     for i in range(mine_ref.shape[0]):
         other_ref[i] = rotated_ref[pick_ref[0, me ^ (2 * i + 1)]]
@@ -82,7 +80,7 @@
         copy.wait()
 
 
-def zip_kernel(mine_ref, got_ref, *out_refs):
+def zip_kernel(mine_ref, got_ref, _, *out_refs):
     for i, out_ref in enumerate(out_refs):
         out_ref[0] = mine_ref[i]
         out_ref[1] = got_ref[i]
@@ -375,21 +373,9 @@
             ],
         )
         got = xor_permute(other, readers, 1)
-        pairs_for = pl.pallas_call(
-            zip_kernel,
-            out_shape=[pltpu.VMEM((2,) + slab, BF16)] * half,
-            in_specs=[VMEM] * 2,
-            out_specs=[VMEM] * half,
-            compiler_params=params(16),
-            name="zip",
-        )(mine, got)
         order = [i for i in ORDER if i < half]
-        arrived = {0: pairs_for[0]}
-        for i in order:
-            arrived[i] = xor_permute(pairs_for[i], readers, 2 * i)
         early = [0] + order[:EARLY]
         late = order[EARLY:]
-        rows = readers * sinks + 1
         table = pl.pallas_call(
             functools.partial(plan_kernel, STEP, readers, sinks, early),
             out_shape=pltpu.VMEM((8, graphs + LANES), jnp.int32),
@@ -399,6 +385,18 @@
             cost_estimate=pl.CostEstimate(flops=10**8, bytes_accessed=0, transcendentals=0),
             name="plan",
         )(graph_count, slot_table, sink_table)
+        pairs_for = pl.pallas_call(
+            zip_kernel,
+            out_shape=[pltpu.VMEM((2,) + slab, BF16)] * half,
+            in_specs=[VMEM] * 3,
+            out_specs=[VMEM] * half,
+            compiler_params=params(16),
+            name="zip",
+        )(mine, got, table)
+        arrived = {0: pairs_for[0]}
+        for i in order:
+            arrived[i] = xor_permute(pairs_for[i], readers, 2 * i)
+        rows = readers * sinks + 1
         factors, early_sum = pl.pallas_call(
             functools.partial(early_kernel, STEP, root_scale, early),
             out_shape=[

time: 42.2 us -> 43.2 us (1.024)
  starting transfers between devices: 16.4 us -> 20.8 us
  Pallas kernels: 12 us -> 8.44 us
    ppermute x13, starting transfers between devices: 16.4 us -> 20.8 us  [xor_permute(): return lax.ppermute(array, 'had', [(d, d ^ mask) for d in range(readers)])]
    pallas_call x1, Pallas kernels: 3.9 us -> 1.75 us  [shards(): pl.pallas_call(functools.partial(late_kernel, STEP, root_scale, edge_scal...]
    pallas_call x1, Pallas kernels: 3.73 us -> 2.3 us  [shards(): pl.pallas_call(functools.partial(early_kernel, STEP, root_scale, early),...]
  transfers between devices with their start and end apart: 13 -> 13, of which waited for: 7 -> 7; matrix products, arithmetic and copies ran while one was open for 2% -> 2% of each run, Pallas kernels for 11% -> 7%
where the time goes in v4:
time: 43.2 us; the launch traced here: 43.1 us
  starting transfers between devices  20.8 us (48%)
  waiting for transfers between devices  11.8 us (27%)
  Pallas kernels  8.44 us (20%)
  between operations  1.37 us (3%)
  local copies, waits for them, and re-layouts  0.68 us (2%)
    ppermute x13, starting transfers between devices, xor_permute(): return lax.ppermute(array, 'had', [(d, d ^ mask) for d in range(readers)])  20.8 us
    ppermute x13, waiting for transfers between devices, xor_permute(): return lax.ppermute(array, 'had', [(d, d ^ mask) for d in range(readers)])  11.8 us
    pallas_call x1, Pallas kernels, shards(): pl.pallas_call(functools.partial(early_kernel, STEP, root_scale, early),...  2.3 us
    pallas_call x1, Pallas kernels, shards(): pl.pallas_call(rotate_pairs_kernel, out_shape=[pltpu.VMEM((half,) + slab,...  2.02 us
    pallas_call x1, Pallas kernels, shards(): pl.pallas_call(functools.partial(late_kernel, STEP, root_scale, edge_scal...  1.75 us
    pallas_call x1, Pallas kernels, shards(): pl.pallas_call(functools.partial(pair_kernel, root_scale, place), out_sha...  1.51 us
  transfers between devices with their start and end apart: 13, of which 7 were waited for; matrix products, arithmetic and copies ran while one was open for 2% of the time, Pallas kernels for 7%

profile of v4, /device:TPU:0, one launch (start us, length us, event | category | flops | bytes accessed | tf_op | source)
XLA Modules:
  0.0 43.1 jit_solution(9126577504507233058)
XLA Ops:
  0.6 2.0 %rotate.1 = (bf16[8,128,128]{2,1,0:T(8,128)(2,1)S(1)}, bf16[8,128,128]{2,1,0:T(8,128)(2,1)S(1)}, bf16[16,128,128]{2,1,0:T(8,128)(2,1)S(1)}, s32[2,512]{1,0:T(2,128)S(1)}, s32[2,512]{1,0:T(2,128)S(1)}) custom-call(s32[1,16]{1,0:T(1,128)} %pick_hbm.1, bf16[16,128,128]{2,1,0:T(8,128)(2,1)} %source_hbm.1, bf16[2,2,128,128]{3,2,1,0:T(8,128)(2,1)} %peram_hbm.1, ...), custom_call_target="tpu_custom_call" | custom-call | tf_op jit(solution)/shard_map/rotate/pallas_call | solution.py:354
  2.7 0.5 %collective-permute-start = (bf16[8,128,128]{2,1,0:T(8,128)(2,1)S(1)}, bf16[8,128,128]{2,1,0:T(8,128)(2,1)S(1)}, u32[]{:S(2)}, u32[]{:S(2)}) collective-permute-start(bf16[8,128,128]{2,1,0:T(8,128)(2,1)S(1)} %get-tuple-element.22), channel_id=1, source_target_pairs={{0,1},{1,0},{2,3},{3,2},{4,5},{5,4},{6,7},{7,6},{8,9},{9,8},{10,11... | collective-permute-start | bytes 786440 | tf_op jit(solution)/shard_map/ppermute | solution.py:298
  3.8 0.8 %plan.1._.table_ref = s32[8,640]{1,0:T(8,128)S(1)} custom-call(s32[1]{0:T(128)S(6)} %copy.18.count_ref, s32[2,512]{1,0:T(2,128)S(1)} %get-tuple-element.18.slot_ref, s32[2,512]{1,0:T(2,128)S(1)} %get-tuple-element.19.sink_ref), custom_call_target="tpu_custom_call" | custom-call | flops 100000000 | tf_op jit(solution)/shard_map/plan/pallas_call | solution.py:379
  4.7 2.6 %collective-permute-start.1 = (bf16[2,128,128]{2,1,0:T(8,128)(2,1)S(1)}, bf16[2,128,128]{2,1,0:T(8,128)(2,1)S(1)}, u32[]{:S(2)}, u32[]{:S(2)}) collective-permute-start(bf16[2,128,128]{2,1,0:T(8,128)(2,1)S(1)} %get-tuple-element.24), channel_id=1, source_target_pairs={{0,2},{1,3},{2,0},{3,1},{4,6},{5,7},{6,4},{7,5},{8,10},{9,11},{10,... | collective-permute-start | bytes 196616 | tf_op jit(solution)/shard_map/ppermute | solution.py:298
  7.4 2.6 %collective-permute-start.2 = (bf16[2,128,128]{2,1,0:T(8,128)(2,1)S(1)}, bf16[2,128,128]{2,1,0:T(8,128)(2,1)S(1)}, u32[]{:S(2)}, u32[]{:S(2)}) collective-permute-start(bf16[2,128,128]{2,1,0:T(8,128)(2,1)S(1)} %get-tuple-element.25), channel_id=1, source_target_pairs={{0,8},{1,9},{2,10},{3,11},{4,12},{5,13},{6,14},{7,15},{8,0},{9,1},... | collective-permute-start | bytes 196616 | tf_op jit(solution)/shard_map/ppermute | solution.py:298
  9.9 1.4 %collective-permute-start.3 = (bf16[2,128,128]{2,1,0:T(8,128)(2,1)S(1)}, bf16[2,128,128]{2,1,0:T(8,128)(2,1)S(1)}, u32[]{:S(2)}, u32[]{:S(2)}) collective-permute-start(bf16[2,128,128]{2,1,0:T(8,128)(2,1)S(1)} %get-tuple-element.26), channel_id=1, source_target_pairs={{0,12},{1,13},{2,14},{3,15},{4,8},{5,9},{6,10},{7,11},{8,4},{9,5},... | collective-permute-start | bytes 196616 | tf_op jit(solution)/shard_map/ppermute | solution.py:298
  11.3 0.2 collective-permute-start.4
  11.5 2.8 %collective-permute-start.5 = (bf16[2,128,128]{2,1,0:T(8,128)(2,1)S(1)}, bf16[2,128,128]{2,1,0:T(8,128)(2,1)S(1)}, u32[]{:S(2)}, u32[]{:S(2)}) collective-permute-start(bf16[2,128,128]{2,1,0:T(8,128)(2,1)S(1)} %get-tuple-element.29), channel_id=1, source_target_pairs={{0,10},{1,11},{2,8},{3,9},{4,14},{5,15},{6,12},{7,13},{8,2},{9,3},... | collective-permute-start | bytes 196616 | tf_op jit(solution)/shard_map/ppermute | solution.py:298
  14.3 2.3 %collective-permute-start.6 = (bf16[2,128,128]{2,1,0:T(8,128)(2,1)S(1)}, bf16[2,128,128]{2,1,0:T(8,128)(2,1)S(1)}, u32[]{:S(2)}, u32[]{:S(2)}) collective-permute-start(bf16[2,128,128]{2,1,0:T(8,128)(2,1)S(1)} %get-tuple-element.30), channel_id=1, source_target_pairs={{0,14},{1,15},{2,12},{3,13},{4,10},{5,11},{6,8},{7,9},{8,6},{9,7},... | collective-permute-start | bytes 196616 | tf_op jit(solution)/shard_map/ppermute | solution.py:298
  16.6 0.1 collective-permute-done.3.refs_3_
  16.7 2.3 %early.1 = (bf16[257,128,128]{2,1,0:T(8,128)(2,1)S(1)}, f32[128,256]{1,0:T(8,128)S(1)}) custom-call(s32[8,640]{1,0:T(8,128)S(1)} %plan.1._.table_ref, bf16[16,128,128]{2,1,0:T(8,128)(2,1)S(1)} %get-tuple-element.20.resident_ref, bf16[2,128,128]{2,1,0:T(8,128)(2,1)S(1)} %get-tuple-element.23.refs_0_, bf16[2,128,128]{2,1,0:T(8,128)(2,1)S(1)} %collective-permute-done.1.refs_1_, ...), custom_call_target="tpu_custom_call" | custom-call | flops 1342177280 | tf_op jit(solution)/shard_map/early/pallas_call | solution.py:400
  19.0 1.5 %collective-permute-done.5.refs_0_ = bf16[2,128,128]{2,1,0:T(8,128)(2,1)S(1)} collective-permute-done((bf16[2,128,128]{2,1,0:T(8,128)(2,1)S(1)}, bf16[2,128,128]{2,1,0:T(8,128)(2,1)S(1)}, u32[]{:S(2)}, u32[]{:S(2)}) %collective-permute-start.5) | collective-permute-done | bytes 65568 | tf_op jit(solution)/shard_map/ppermute | solution.py:298
  20.5 0.8 %collective-permute-done.6.refs_1_ = bf16[2,128,128]{2,1,0:T(8,128)(2,1)S(1)} collective-permute-done((bf16[2,128,128]{2,1,0:T(8,128)(2,1)S(1)}, bf16[2,128,128]{2,1,0:T(8,128)(2,1)S(1)}, u32[]{:S(2)}, u32[]{:S(2)}) %collective-permute-start.6) | collective-permute-done | bytes 65568 | tf_op jit(solution)/shard_map/ppermute | solution.py:298
  21.3 0.7 %collective-permute-done.7.refs_2_ = bf16[2,128,128]{2,1,0:T(8,128)(2,1)S(1)} collective-permute-done((bf16[2,128,128]{2,1,0:T(8,128)(2,1)S(1)}, bf16[2,128,128]{2,1,0:T(8,128)(2,1)S(1)}, u32[]{:S(2)}, u32[]{:S(2)}) %collective-permute-start.7) | collective-permute-done | bytes 65568 | tf_op jit(solution)/shard_map/ppermute | solution.py:298
  22.0 1.7 %edge.1 = (bf16[1,128,128]{2,1,0:T(8,128)(2,1)S(1)}, bf16[257,128,128]{2,1,0:T(8,128)(2,1)S(1)}) custom-call(s32[8,640]{1,0:T(8,128)S(1)} %plan.1._.table_ref, f32[128,256]{1,0:T(8,128)S(1)} %get-tuple-element.28.sum_ref, bf16[16,128,128]{2,1,0:T(8,128)(2,1)S(1)} %get-tuple-element.20.resident_ref, ...), custom_call_target="tpu_custom_call", output_to_operand_aliasing={{1}: (6, {})} | custom-call | tf_op jit(solution)/shard_map/edge/pallas_call | solution.py:418
  23.8 2.0 %collective-permute-start.8 = (bf16[1,128,128]{2,1,0:T(8,128)(2,1)S(1)}, bf16[1,128,128]{2,1,0:T(8,128)(2,1)S(1)}, u32[]{:S(2)}, u32[]{:S(2)}) collective-permute-start(bf16[1,128,128]{2,1,0:T(8,128)(2,1)S(1)} %get-tuple-element.38), channel_id=1, source_target_pairs={{0,2},{1,3},{2,0},{3,1},{4,6},{5,7},{6,4},{7,5},{8,10},{9,11},{10,... | collective-permute-start | bytes 98312 | tf_op jit(solution)/shard_map/ppermute | solution.py:298
  25.8 2.0 %collective-permute-done.8 = bf16[1,128,128]{2,1,0:T(8,128)(2,1)S(1)} collective-permute-done((bf16[1,128,128]{2,1,0:T(8,128)(2,1)S(1)}, bf16[1,128,128]{2,1,0:T(8,128)(2,1)S(1)}, u32[]{:S(2)}, u32[]{:S(2)}) %collective-permute-start.8) | collective-permute-done | bytes 32800 | tf_op jit(solution)/shard_map/ppermute | solution.py:298
  27.8 2.0 %collective-permute-start.9 = (bf16[2,128,128]{2,1,0:T(8,128)(2,1)S(1)}, bf16[2,128,128]{2,1,0:T(8,128)(2,1)S(1)}, u32[]{:S(2)}, u32[]{:S(2)}) collective-permute-start(bf16[2,128,128]{2,1,0:T(8,128)(2,1)S(1)} %get-tuple-element.34), channel_id=1, source_target_pairs={{0,4},{1,5},{2,6},{3,7},{4,0},{5,1},{6,2},{7,3},{8,12},{9,13},{10,... | collective-permute-start | bytes 196616 | tf_op jit(solution)/shard_map/ppermute | solution.py:298
  29.8 3.9 %collective-permute-start.11 = (bf16[2,128,128]{2,1,0:T(8,128)(2,1)S(1)}, bf16[2,128,128]{2,1,0:T(8,128)(2,1)S(1)}, u32[]{:S(2)}, u32[]{:S(2)}) collective-permute-start(bf16[2,128,128]{2,1,0:T(8,128)(2,1)S(1)} %get-tuple-element.34), channel_id=1, source_target_pairs={{0,12},{1,13},{2,14},{3,15},{4,8},{5,9},{6,10},{7,11},{8,4},{9,5},... | collective-permute-start | bytes 196616 | tf_op jit(solution)/shard_map/ppermute | solution.py:298
  33.7 0.5 %collective-permute-start.10 = (bf16[2,128,128]{2,1,0:T(8,128)(2,1)S(1)}, bf16[2,128,128]{2,1,0:T(8,128)(2,1)S(1)}, u32[]{:S(2)}, u32[]{:S(2)}) collective-permute-start(bf16[2,128,128]{2,1,0:T(8,128)(2,1)S(1)} %get-tuple-element.34), channel_id=1, source_target_pairs={{0,8},{1,9},{2,10},{3,11},{4,12},{5,13},{6,14},{7,15},{8,0},{9,1},... | collective-permute-start | bytes 196616 | tf_op jit(solution)/shard_map/ppermute | solution.py:298
  34.2 5.7 %collective-permute-done.10 = bf16[2,128,128]{2,1,0:T(8,128)(2,1)S(1)} collective-permute-done((bf16[2,128,128]{2,1,0:T(8,128)(2,1)S(1)}, bf16[2,128,128]{2,1,0:T(8,128)(2,1)S(1)}, u32[]{:S(2)}, u32[]{:S(2)}) %collective-permute-start.10) | collective-permute-done | bytes 65568 | tf_op jit(solution)/shard_map/ppermute | solution.py:298
  40.0 0.6 %copy.17 = bf16[1,128,128]{2,1,0:T(8,128)(2,1)} copy(bf16[1,128,128]{2,1,0:T(8,128)(2,1)S(1)} %get-tuple-element.38) | data formatting | bytes 65536
  40.7 0.9 %collective-permute-done.12.refs_1_ = bf16[8,128,128]{2,1,0:T(8,128)(2,1)S(1)} collective-permute-done((bf16[8,128,128]{2,1,0:T(8,128)(2,1)S(1)}, bf16[8,128,128]{2,1,0:T(8,128)(2,1)S(1)}, u32[]{:S(2)}, u32[]{:S(2)}) %collective-permute-start.12) | collective-permute-done | bytes 262176 | tf_op jit(solution)/shard_map/ppermute | solution.py:298
  41.6 1.5 %pairs.1 = bf16[8,128,128]{2,1,0:T(8,128)(2,1)} custom-call(s32[2,8]{1,0:T(2,128)S(1)} %bitcast.7, bf16[8,128,128]{2,1,0:T(8,128)(2,1)S(1)} %constant_dynamic-update-slice_fusion.2.refs_0_, bf16[8,128,128]{2,1,0:T(8,128)(2,1)S(1)} %collective-permute-done.12.refs_1_), custom_call_target="tpu_custom_call" | custom-call | tf_op jit(solution)/shard_map/pairs/pallas_call | solution.py:456
  (16 shorter events, 0.2 us)
Async XLA Ops:
  0.6 40.9 %copy-start = (s32[8,2]{0,1:T(2,128)S(1)}, s32[8,2]{0,1:T(2,128)}, u32[]{:S(2)}) copy-start(s32[8,2]{0,1:T(2,128)} %param.15) | copy-start | bytes 196
  2.7 2.0 %collective-permute-start = (bf16[8,128,128]{2,1,0:T(8,128)(2,1)S(1)}, bf16[8,128,128]{2,1,0:T(8,128)(2,1)S(1)}, u32[]{:S(2)}, u32[]{:S(2)}) collective-permute-start(bf16[8,128,128]{2,1,0:T(8,128)(2,1)S(1)} %get-tuple-element.22), channel_id=1, source_target_pairs={{0,1},{1,0},{2,3},{3,2},{4,5},{5,4},{6,7},{7,6},{8,9},{9,8},{10,11... | collective-permute-start | bytes 786440 | tf_op jit(solution)/shard_map/ppermute | solution.py:298
  4.7 9.5 %collective-permute-start.1 = (bf16[2,128,128]{2,1,0:T(8,128)(2,1)S(1)}, bf16[2,128,128]{2,1,0:T(8,128)(2,1)S(1)}, u32[]{:S(2)}, u32[]{:S(2)}) collective-permute-start(bf16[2,128,128]{2,1,0:T(8,128)(2,1)S(1)} %get-tuple-element.24), channel_id=1, source_target_pairs={{0,2},{1,3},{2,0},{3,1},{4,6},{5,7},{6,4},{7,5},{8,10},{9,11},{10,... | collective-permute-start | bytes 196616 | tf_op jit(solution)/shard_map/ppermute | solution.py:298
  7.4 9.2 %collective-permute-start.2 = (bf16[2,128,128]{2,1,0:T(8,128)(2,1)S(1)}, bf16[2,128,128]{2,1,0:T(8,128)(2,1)S(1)}, u32[]{:S(2)}, u32[]{:S(2)}) collective-permute-start(bf16[2,128,128]{2,1,0:T(8,128)(2,1)S(1)} %get-tuple-element.25), channel_id=1, source_target_pairs={{0,8},{1,9},{2,10},{3,11},{4,12},{5,13},{6,14},{7,15},{8,0},{9,1},... | collective-permute-start | bytes 196616 | tf_op jit(solution)/shard_map/ppermute | solution.py:298
  9.9 6.8 %collective-permute-start.3 = (bf16[2,128,128]{2,1,0:T(8,128)(2,1)S(1)}, bf16[2,128,128]{2,1,0:T(8,128)(2,1)S(1)}, u32[]{:S(2)}, u32[]{:S(2)}) collective-permute-start(bf16[2,128,128]{2,1,0:T(8,128)(2,1)S(1)} %get-tuple-element.26), channel_id=1, source_target_pairs={{0,12},{1,13},{2,14},{3,15},{4,8},{5,9},{6,10},{7,11},{8,4},{9,5},... | collective-permute-start | bytes 196616 | tf_op jit(solution)/shard_map/ppermute | solution.py:298
  11.3 5.4 %collective-permute-start.4 = (bf16[2,128,128]{2,1,0:T(8,128)(2,1)S(1)}, bf16[2,128,128]{2,1,0:T(8,128)(2,1)S(1)}, u32[]{:S(2)}, u32[]{:S(2)}) collective-permute-start(bf16[2,128,128]{2,1,0:T(8,128)(2,1)S(1)} %get-tuple-element.27), channel_id=1, source_target_pairs={{0,4},{1,5},{2,6},{3,7},{4,0},{5,1},{6,2},{7,3},{8,12},{9,13},{10,... | collective-permute-start | bytes 196616 | tf_op jit(solution)/shard_map/ppermute | solution.py:298
  11.5 9.0 %collective-permute-start.5 = (bf16[2,128,128]{2,1,0:T(8,128)(2,1)S(1)}, bf16[2,128,128]{2,1,0:T(8,128)(2,1)S(1)}, u32[]{:S(2)}, u32[]{:S(2)}) collective-permute-start(bf16[2,128,128]{2,1,0:T(8,128)(2,1)S(1)} %get-tuple-element.29), channel_id=1, source_target_pairs={{0,10},{1,11},{2,8},{3,9},{4,14},{5,15},{6,12},{7,13},{8,2},{9,3},... | collective-permute-start | bytes 196616 | tf_op jit(solution)/shard_map/ppermute | solution.py:298
  14.3 7.1 %collective-permute-start.6 = (bf16[2,128,128]{2,1,0:T(8,128)(2,1)S(1)}, bf16[2,128,128]{2,1,0:T(8,128)(2,1)S(1)}, u32[]{:S(2)}, u32[]{:S(2)}) collective-permute-start(bf16[2,128,128]{2,1,0:T(8,128)(2,1)S(1)} %get-tuple-element.30), channel_id=1, source_target_pairs={{0,14},{1,15},{2,12},{3,13},{4,10},{5,11},{6,8},{7,9},{8,6},{9,7},... | collective-permute-start | bytes 196616 | tf_op jit(solution)/shard_map/ppermute | solution.py:298
  16.6 5.5 %collective-permute-start.7 = (bf16[2,128,128]{2,1,0:T(8,128)(2,1)S(1)}, bf16[2,128,128]{2,1,0:T(8,128)(2,1)S(1)}, u32[]{:S(2)}, u32[]{:S(2)}) collective-permute-start(bf16[2,128,128]{2,1,0:T(8,128)(2,1)S(1)} %get-tuple-element.31), channel_id=1, source_target_pairs={{0,6},{1,7},{2,4},{3,5},{4,2},{5,3},{6,0},{7,1},{8,14},{9,15},{10,... | collective-permute-start | bytes 196616 | tf_op jit(solution)/shard_map/ppermute | solution.py:298
  23.8 4.0 %collective-permute-start.8 = (bf16[1,128,128]{2,1,0:T(8,128)(2,1)S(1)}, bf16[1,128,128]{2,1,0:T(8,128)(2,1)S(1)}, u32[]{:S(2)}, u32[]{:S(2)}) collective-permute-start(bf16[1,128,128]{2,1,0:T(8,128)(2,1)S(1)} %get-tuple-element.38), channel_id=1, source_target_pairs={{0,2},{1,3},{2,0},{3,1},{4,6},{5,7},{6,4},{7,5},{8,10},{9,11},{10,... | collective-permute-start | bytes 98312 | tf_op jit(solution)/shard_map/ppermute | solution.py:298
  27.8 6.4 %collective-permute-start.9 = (bf16[2,128,128]{2,1,0:T(8,128)(2,1)S(1)}, bf16[2,128,128]{2,1,0:T(8,128)(2,1)S(1)}, u32[]{:S(2)}, u32[]{:S(2)}) collective-permute-start(bf16[2,128,128]{2,1,0:T(8,128)(2,1)S(1)} %get-tuple-element.34), channel_id=1, source_target_pairs={{0,4},{1,5},{2,6},{3,7},{4,0},{5,1},{6,2},{7,3},{8,12},{9,13},{10,... | collective-permute-start | bytes 196616 | tf_op jit(solution)/shard_map/ppermute | solution.py:298
  29.8 10.2 %collective-permute-start.11 = (bf16[2,128,128]{2,1,0:T(8,128)(2,1)S(1)}, bf16[2,128,128]{2,1,0:T(8,128)(2,1)S(1)}, u32[]{:S(2)}, u32[]{:S(2)}) collective-permute-start(bf16[2,128,128]{2,1,0:T(8,128)(2,1)S(1)} %get-tuple-element.34), channel_id=1, source_target_pairs={{0,12},{1,13},{2,14},{3,15},{4,8},{5,9},{6,10},{7,11},{8,4},{9,5},... | collective-permute-start | bytes 196616 | tf_op jit(solution)/shard_map/ppermute | solution.py:298
  33.7 6.2 %collective-permute-start.10 = (bf16[2,128,128]{2,1,0:T(8,128)(2,1)S(1)}, bf16[2,128,128]{2,1,0:T(8,128)(2,1)S(1)}, u32[]{:S(2)}, u32[]{:S(2)}) collective-permute-start(bf16[2,128,128]{2,1,0:T(8,128)(2,1)S(1)} %get-tuple-element.34), channel_id=1, source_target_pairs={{0,8},{1,9},{2,10},{3,11},{4,12},{5,13},{6,14},{7,15},{8,0},{9,1},... | collective-permute-start | bytes 196616 | tf_op jit(solution)/shard_map/ppermute | solution.py:298
  40.0 1.6 %collective-permute-start.12 = (bf16[8,128,128]{2,1,0:T(8,128)(2,1)S(1)}, bf16[8,128,128]{2,1,0:T(8,128)(2,1)S(1)}, u32[]{:S(2)}, u32[]{:S(2)}) collective-permute-start(bf16[8,128,128]{2,1,0:T(8,128)(2,1)S(1)} %constant_dynamic-update-slice_fusion.2.refs_0_), channel_id=1, source_target_pairs={{0,1},{1,0},{2,3},{3,2},{4,5},{5,4},{6,7},{7,6},{8,9},{9,8},{10,11... | collective-permute-start | bytes 786440 | tf_op jit(solution)/shard_map/ppermute | solution.py:298

commit v5 on v4

--- a/solution.py
+++ b/solution.py
@@ -286,8 +286,8 @@
 
 
 def xor_phases(readers):
-    far = list(range(readers - 4, 0, -4))
-    return [phase for phase in ([2] if readers > 2 else [], far, [1]) if phase]
+    far = [4 * z + 1 for z in range(readers // 4 - 1, 0, -1)]
+    return [phase for phase in (far, [3] if readers > 2 else [], [1]) if phase]
 
 
 def by_xor(readers):
@@ -303,14 +303,17 @@
         return [lax.all_gather(edge, "had", axis=0, tiled=True)], lambda r: r
     held = edge
     for phase in xor_phases(readers):
-        arrived = [xor_permute(held, readers, mask) for mask in phase]
-        parts = [held] + arrived[::-1]
+        arrived = {mask: xor_permute(held, readers, mask) for mask in phase}
+        parts = [held] + [arrived[mask] for mask in sorted(phase)]
         if phase != [1]:
             held = jnp.concatenate(parts, axis=0)
 
     def place(reader):
         mask = reader ^ lax.axis_index("had")
-        return (mask >> 1) + (mask & 1) * (readers // 2)
+        other_core = mask ^ (mask >> 1) ^ jnp.where(mask >= 4, 1, 0)
+        return (
+            (mask >> 2) + ((mask >> 1) & 1) * (readers // 4) + (other_core & 1) * (readers // 2)
+        )
 
     return parts, place
 

time: 43.2 us -> 41.4 us (0.958); the launches traced: 43.1 us -> 41.7 us
  starting transfers between devices: 20.8 us -> 16.8 us
  Pallas kernels: 8.44 us -> 12 us
  waiting for transfers between devices: 11.8 us -> 10.9 us
    ppermute x13, starting transfers between devices: 20.8 us -> 16.8 us  [xor_permute(): return lax.ppermute(array, 'had', [(d, d ^ mask) for d in range(readers)])]
    pallas_call x1, Pallas kernels: 1.75 us -> 3.89 us  [shards(): pl.pallas_call(functools.partial(late_kernel, STEP, root_scale, edge_scal...]
    pallas_call x1, Pallas kernels: 2.3 us -> 3.73 us  [shards(): pl.pallas_call(functools.partial(early_kernel, STEP, root_scale, early),...]
    ppermute x13, waiting for transfers between devices: 11.8 us -> 10.9 us  [xor_permute(): return lax.ppermute(array, 'had', [(d, d ^ mask) for d in range(readers)])]
  transfers between devices with their start and end apart: 13 -> 13, of which waited for: 7 -> 7; matrix products, arithmetic and copies ran while one was open for 2% -> 2% of each run, Pallas kernels for 7% -> 11%
where the time goes in v5:
time: 41.4 us; the launch traced here: 41.7 us
  starting transfers between devices  16.8 us (41%)
  Pallas kernels  12 us (29%)
  waiting for transfers between devices  10.9 us (26%)
  between operations  1.37 us (3%)
  local copies, waits for them, and re-layouts  0.67 us (2%)
    ppermute x13, starting transfers between devices, xor_permute(): return lax.ppermute(array, 'had', [(d, d ^ mask) for d in range(readers)])  16.8 us
    ppermute x13, waiting for transfers between devices, xor_permute(): return lax.ppermute(array, 'had', [(d, d ^ mask) for d in range(readers)])  10.9 us
    pallas_call x1, Pallas kernels, shards(): pl.pallas_call(functools.partial(late_kernel, STEP, root_scale, edge_scal...  3.89 us
    pallas_call x1, Pallas kernels, shards(): pl.pallas_call(functools.partial(early_kernel, STEP, root_scale, early),...  3.73 us
    pallas_call x1, Pallas kernels, shards(): pl.pallas_call(rotate_pairs_kernel, out_shape=[pltpu.VMEM((half,) + slab,...  2.02 us
    pallas_call x1, Pallas kernels, shards(): pl.pallas_call(functools.partial(pair_kernel, root_scale, place), out_sha...  1.51 us
  transfers between devices with their start and end apart: 13, of which 7 were waited for; matrix products, arithmetic and copies ran while one was open for 2% of the time, Pallas kernels for 11%

profile of v5, /device:TPU:0, one launch (start us, length us, event | category | flops | bytes accessed | tf_op | source)
XLA Modules:
  0.0 41.7 jit_solution(16015150715946237498)
XLA Ops:
  0.6 2.0 %rotate.1 = (bf16[8,128,128]{2,1,0:T(8,128)(2,1)S(1)}, bf16[8,128,128]{2,1,0:T(8,128)(2,1)S(1)}, bf16[16,128,128]{2,1,0:T(8,128)(2,1)S(1)}, s32[2,512]{1,0:T(2,128)S(1)}, s32[2,512]{1,0:T(2,128)S(1)}) custom-call(s32[1,16]{1,0:T(1,128)} %pick_hbm.1, bf16[16,128,128]{2,1,0:T(8,128)(2,1)} %source_hbm.1, bf16[2,2,128,128]{3,2,1,0:T(8,128)(2,1)} %peram_hbm.1, ...), custom_call_target="tpu_custom_call" | custom-call | tf_op jit(solution)/shard_map/rotate/pallas_call | solution.py:357
  2.7 0.5 %collective-permute-start = (bf16[8,128,128]{2,1,0:T(8,128)(2,1)S(1)}, bf16[8,128,128]{2,1,0:T(8,128)(2,1)S(1)}, u32[]{:S(2)}, u32[]{:S(2)}) collective-permute-start(bf16[8,128,128]{2,1,0:T(8,128)(2,1)S(1)} %get-tuple-element.22), channel_id=1, source_target_pairs={{0,1},{1,0},{2,3},{3,2},{4,5},{5,4},{6,7},{7,6},{8,9},{9,8},{10,11... | collective-permute-start | bytes 786440 | tf_op jit(solution)/shard_map/ppermute | solution.py:298
  3.8 0.8 %plan.1._.table_ref = s32[8,640]{1,0:T(8,128)S(1)} custom-call(s32[1]{0:T(128)S(6)} %copy.17.count_ref, s32[2,512]{1,0:T(2,128)S(1)} %get-tuple-element.18.slot_ref, s32[2,512]{1,0:T(2,128)S(1)} %get-tuple-element.19.sink_ref), custom_call_target="tpu_custom_call" | custom-call | flops 100000000 | tf_op jit(solution)/shard_map/plan/pallas_call | solution.py:382
  4.7 2.6 %collective-permute-start.1 = (bf16[2,128,128]{2,1,0:T(8,128)(2,1)S(1)}, bf16[2,128,128]{2,1,0:T(8,128)(2,1)S(1)}, u32[]{:S(2)}, u32[]{:S(2)}) collective-permute-start(bf16[2,128,128]{2,1,0:T(8,128)(2,1)S(1)} %get-tuple-element.24), channel_id=1, source_target_pairs={{0,2},{1,3},{2,0},{3,1},{4,6},{5,7},{6,4},{7,5},{8,10},{9,11},{10,... | collective-permute-start | bytes 196616 | tf_op jit(solution)/shard_map/ppermute | solution.py:298
  7.3 2.6 %collective-permute-start.2 = (bf16[2,128,128]{2,1,0:T(8,128)(2,1)S(1)}, bf16[2,128,128]{2,1,0:T(8,128)(2,1)S(1)}, u32[]{:S(2)}, u32[]{:S(2)}) collective-permute-start(bf16[2,128,128]{2,1,0:T(8,128)(2,1)S(1)} %get-tuple-element.25), channel_id=1, source_target_pairs={{0,8},{1,9},{2,10},{3,11},{4,12},{5,13},{6,14},{7,15},{8,0},{9,1},... | collective-permute-start | bytes 196616 | tf_op jit(solution)/shard_map/ppermute | solution.py:298
  9.9 1.3 %collective-permute-start.3 = (bf16[2,128,128]{2,1,0:T(8,128)(2,1)S(1)}, bf16[2,128,128]{2,1,0:T(8,128)(2,1)S(1)}, u32[]{:S(2)}, u32[]{:S(2)}) collective-permute-start(bf16[2,128,128]{2,1,0:T(8,128)(2,1)S(1)} %get-tuple-element.26), channel_id=1, source_target_pairs={{0,12},{1,13},{2,14},{3,15},{4,8},{5,9},{6,10},{7,11},{8,4},{9,5},... | collective-permute-start | bytes 196616 | tf_op jit(solution)/shard_map/ppermute | solution.py:298
  11.3 0.2 collective-permute-start.4
  11.5 2.8 %collective-permute-start.5 = (bf16[2,128,128]{2,1,0:T(8,128)(2,1)S(1)}, bf16[2,128,128]{2,1,0:T(8,128)(2,1)S(1)}, u32[]{:S(2)}, u32[]{:S(2)}) collective-permute-start(bf16[2,128,128]{2,1,0:T(8,128)(2,1)S(1)} %get-tuple-element.29), channel_id=1, source_target_pairs={{0,10},{1,11},{2,8},{3,9},{4,14},{5,15},{6,12},{7,13},{8,2},{9,3},... | collective-permute-start | bytes 196616 | tf_op jit(solution)/shard_map/ppermute | solution.py:298
  14.3 2.3 %collective-permute-start.6 = (bf16[2,128,128]{2,1,0:T(8,128)(2,1)S(1)}, bf16[2,128,128]{2,1,0:T(8,128)(2,1)S(1)}, u32[]{:S(2)}, u32[]{:S(2)}) collective-permute-start(bf16[2,128,128]{2,1,0:T(8,128)(2,1)S(1)} %get-tuple-element.30), channel_id=1, source_target_pairs={{0,14},{1,15},{2,12},{3,13},{4,10},{5,11},{6,8},{7,9},{8,6},{9,7},... | collective-permute-start | bytes 196616 | tf_op jit(solution)/shard_map/ppermute | solution.py:298
  16.6 0.1 collective-permute-done.3.refs_3_
  16.7 3.7 %early.1 = (bf16[257,128,128]{2,1,0:T(8,128)(2,1)S(1)}, f32[128,256]{1,0:T(8,128)S(1)}) custom-call(s32[8,640]{1,0:T(8,128)S(1)} %plan.1._.table_ref, bf16[16,128,128]{2,1,0:T(8,128)(2,1)S(1)} %get-tuple-element.20.resident_ref, bf16[2,128,128]{2,1,0:T(8,128)(2,1)S(1)} %get-tuple-element.23.refs_0_, bf16[2,128,128]{2,1,0:T(8,128)(2,1)S(1)} %collective-permute-done.1.refs_1_, ...), custom_call_target="tpu_custom_call" | custom-call | flops 1342177280 | tf_op jit(solution)/shard_map/early/pallas_call | solution.py:403
  20.5 0.8 %collective-permute-done.6.refs_1_ = bf16[2,128,128]{2,1,0:T(8,128)(2,1)S(1)} collective-permute-done((bf16[2,128,128]{2,1,0:T(8,128)(2,1)S(1)}, bf16[2,128,128]{2,1,0:T(8,128)(2,1)S(1)}, u32[]{:S(2)}, u32[]{:S(2)}) %collective-permute-start.6) | collective-permute-done | bytes 65568 | tf_op jit(solution)/shard_map/ppermute | solution.py:298
  21.3 0.7 %collective-permute-done.7.refs_2_ = bf16[2,128,128]{2,1,0:T(8,128)(2,1)S(1)} collective-permute-done((bf16[2,128,128]{2,1,0:T(8,128)(2,1)S(1)}, bf16[2,128,128]{2,1,0:T(8,128)(2,1)S(1)}, u32[]{:S(2)}, u32[]{:S(2)}) %collective-permute-start.7) | collective-permute-done | bytes 65568 | tf_op jit(solution)/shard_map/ppermute | solution.py:298
  22.1 3.9 %edge.1 = (bf16[1,128,128]{2,1,0:T(8,128)(2,1)S(1)}, bf16[257,128,128]{2,1,0:T(8,128)(2,1)S(1)}) custom-call(s32[8,640]{1,0:T(8,128)S(1)} %plan.1._.table_ref, f32[128,256]{1,0:T(8,128)S(1)} %get-tuple-element.28.sum_ref, bf16[16,128,128]{2,1,0:T(8,128)(2,1)S(1)} %get-tuple-element.20.resident_ref, ...), custom_call_target="tpu_custom_call", output_to_operand_aliasing={{1}: (6, {})} | custom-call | tf_op jit(solution)/shard_map/edge/pallas_call | solution.py:421
  25.9 1.0 %collective-permute-start.10 = (bf16[1,128,128]{2,1,0:T(8,128)(2,1)S(1)}, bf16[1,128,128]{2,1,0:T(8,128)(2,1)S(1)}, u32[]{:S(2)}, u32[]{:S(2)}) collective-permute-start(bf16[1,128,128]{2,1,0:T(8,128)(2,1)S(1)} %get-tuple-element.34), channel_id=1, source_target_pairs={{0,13},{1,12},{2,15},{3,14},{4,9},{5,8},{6,11},{7,10},{8,5},{9,4},... | collective-permute-start | bytes 98312 | tf_op jit(solution)/shard_map/ppermute | solution.py:298
  27.0 1.1 %collective-permute-start.8 = (bf16[1,128,128]{2,1,0:T(8,128)(2,1)S(1)}, bf16[1,128,128]{2,1,0:T(8,128)(2,1)S(1)}, u32[]{:S(2)}, u32[]{:S(2)}) collective-permute-start(bf16[1,128,128]{2,1,0:T(8,128)(2,1)S(1)} %get-tuple-element.34), channel_id=1, source_target_pairs={{0,5},{1,4},{2,7},{3,6},{4,1},{5,0},{6,3},{7,2},{8,13},{9,12},{10,... | collective-permute-start | bytes 98312 | tf_op jit(solution)/shard_map/ppermute | solution.py:298
  28.0 3.1 %collective-permute-done.10 = bf16[1,128,128]{2,1,0:T(8,128)(2,1)S(1)} collective-permute-done((bf16[1,128,128]{2,1,0:T(8,128)(2,1)S(1)}, bf16[1,128,128]{2,1,0:T(8,128)(2,1)S(1)}, u32[]{:S(2)}, u32[]{:S(2)}) %collective-permute-start.10) | collective-permute-done | bytes 32800 | tf_op jit(solution)/shard_map/ppermute | solution.py:298
  31.2 1.2 %collective-permute-done.9 = bf16[1,128,128]{2,1,0:T(8,128)(2,1)S(1)} collective-permute-done((bf16[1,128,128]{2,1,0:T(8,128)(2,1)S(1)}, bf16[1,128,128]{2,1,0:T(8,128)(2,1)S(1)}, u32[]{:S(2)}, u32[]{:S(2)}) %collective-permute-start.9) | collective-permute-done | bytes 32800 | tf_op jit(solution)/shard_map/ppermute | solution.py:298
  32.4 2.2 %collective-permute-start.11 = (bf16[4,128,128]{2,1,0:T(8,128)(2,1)S(1)}, bf16[4,128,128]{2,1,0:T(8,128)(2,1)S(1)}, u32[]{:S(2)}, u32[]{:S(2)}) collective-permute-start(bf16[4,128,128]{2,1,0:T(8,128)(2,1)S(1)} %pad_maximum_fusion), channel_id=1, source_target_pairs={{0,3},{1,2},{2,1},{3,0},{4,7},{5,6},{6,5},{7,4},{8,11},{9,10},{10,... | collective-permute-start | bytes 393224 | tf_op jit(solution)/shard_map/ppermute | solution.py:298
  34.7 3.9 %collective-permute-done.11 = bf16[4,128,128]{2,1,0:T(8,128)(2,1)S(1)} collective-permute-done((bf16[4,128,128]{2,1,0:T(8,128)(2,1)S(1)}, bf16[4,128,128]{2,1,0:T(8,128)(2,1)S(1)}, u32[]{:S(2)}, u32[]{:S(2)}) %collective-permute-start.11) | collective-permute-done | bytes 131104 | tf_op jit(solution)/shard_map/ppermute | solution.py:298
  38.6 0.1 collective-permute-start.12
  38.7 0.6 %copy.16 = bf16[1,128,128]{2,1,0:T(8,128)(2,1)} copy(bf16[1,128,128]{2,1,0:T(8,128)(2,1)S(1)} %get-tuple-element.34) | data formatting | bytes 65536
  39.3 0.9 %collective-permute-done.12.refs_1_ = bf16[8,128,128]{2,1,0:T(8,128)(2,1)S(1)} collective-permute-done((bf16[8,128,128]{2,1,0:T(8,128)(2,1)S(1)}, bf16[8,128,128]{2,1,0:T(8,128)(2,1)S(1)}, u32[]{:S(2)}, u32[]{:S(2)}) %collective-permute-start.12) | collective-permute-done | bytes 262176 | tf_op jit(solution)/shard_map/ppermute | solution.py:298
  40.2 1.5 %pairs.1 = bf16[8,128,128]{2,1,0:T(8,128)(2,1)} custom-call(s32[2,8]{1,0:T(2,128)S(1)} %bitcast.7, bf16[8,128,128]{2,1,0:T(8,128)(2,1)S(1)} %constant_dynamic-update-slice_fusion.refs_0_, bf16[8,128,128]{2,1,0:T(8,128)(2,1)S(1)} %collective-permute-done.12.refs_1_), custom_call_target="tpu_custom_call" | custom-call | tf_op jit(solution)/shard_map/pairs/pallas_call | solution.py:459
  (17 shorter events, 0.2 us)
Async XLA Ops:
  0.6 39.6 %copy-start = (s32[8,2]{0,1:T(2,128)S(1)}, s32[8,2]{0,1:T(2,128)}, u32[]{:S(2)}) copy-start(s32[8,2]{0,1:T(2,128)} %param.15) | copy-start | bytes 196
  2.7 2.0 %collective-permute-start = (bf16[8,128,128]{2,1,0:T(8,128)(2,1)S(1)}, bf16[8,128,128]{2,1,0:T(8,128)(2,1)S(1)}, u32[]{:S(2)}, u32[]{:S(2)}) collective-permute-start(bf16[8,128,128]{2,1,0:T(8,128)(2,1)S(1)} %get-tuple-element.22), channel_id=1, source_target_pairs={{0,1},{1,0},{2,3},{3,2},{4,5},{5,4},{6,7},{7,6},{8,9},{9,8},{10,11... | collective-permute-start | bytes 786440 | tf_op jit(solution)/shard_map/ppermute | solution.py:298
  4.7 9.5 %collective-permute-start.1 = (bf16[2,128,128]{2,1,0:T(8,128)(2,1)S(1)}, bf16[2,128,128]{2,1,0:T(8,128)(2,1)S(1)}, u32[]{:S(2)}, u32[]{:S(2)}) collective-permute-start(bf16[2,128,128]{2,1,0:T(8,128)(2,1)S(1)} %get-tuple-element.24), channel_id=1, source_target_pairs={{0,2},{1,3},{2,0},{3,1},{4,6},{5,7},{6,4},{7,5},{8,10},{9,11},{10,... | collective-permute-start | bytes 196616 | tf_op jit(solution)/shard_map/ppermute | solution.py:298
  7.3 9.2 %collective-permute-start.2 = (bf16[2,128,128]{2,1,0:T(8,128)(2,1)S(1)}, bf16[2,128,128]{2,1,0:T(8,128)(2,1)S(1)}, u32[]{:S(2)}, u32[]{:S(2)}) collective-permute-start(bf16[2,128,128]{2,1,0:T(8,128)(2,1)S(1)} %get-tuple-element.25), channel_id=1, source_target_pairs={{0,8},{1,9},{2,10},{3,11},{4,12},{5,13},{6,14},{7,15},{8,0},{9,1},... | collective-permute-start | bytes 196616 | tf_op jit(solution)/shard_map/ppermute | solution.py:298
  9.9 6.8 %collective-permute-start.3 = (bf16[2,128,128]{2,1,0:T(8,128)(2,1)S(1)}, bf16[2,128,128]{2,1,0:T(8,128)(2,1)S(1)}, u32[]{:S(2)}, u32[]{:S(2)}) collective-permute-start(bf16[2,128,128]{2,1,0:T(8,128)(2,1)S(1)} %get-tuple-element.26), channel_id=1, source_target_pairs={{0,12},{1,13},{2,14},{3,15},{4,8},{5,9},{6,10},{7,11},{8,4},{9,5},... | collective-permute-start | bytes 196616 | tf_op jit(solution)/shard_map/ppermute | solution.py:298
  11.3 5.4 %collective-permute-start.4 = (bf16[2,128,128]{2,1,0:T(8,128)(2,1)S(1)}, bf16[2,128,128]{2,1,0:T(8,128)(2,1)S(1)}, u32[]{:S(2)}, u32[]{:S(2)}) collective-permute-start(bf16[2,128,128]{2,1,0:T(8,128)(2,1)S(1)} %get-tuple-element.27), channel_id=1, source_target_pairs={{0,4},{1,5},{2,6},{3,7},{4,0},{5,1},{6,2},{7,3},{8,12},{9,13},{10,... | collective-permute-start | bytes 196616 | tf_op jit(solution)/shard_map/ppermute | solution.py:298
  11.5 9.0 %collective-permute-start.5 = (bf16[2,128,128]{2,1,0:T(8,128)(2,1)S(1)}, bf16[2,128,128]{2,1,0:T(8,128)(2,1)S(1)}, u32[]{:S(2)}, u32[]{:S(2)}) collective-permute-start(bf16[2,128,128]{2,1,0:T(8,128)(2,1)S(1)} %get-tuple-element.29), channel_id=1, source_target_pairs={{0,10},{1,11},{2,8},{3,9},{4,14},{5,15},{6,12},{7,13},{8,2},{9,3},... | collective-permute-start | bytes 196616 | tf_op jit(solution)/shard_map/ppermute | solution.py:298
  14.3 7.1 %collective-permute-start.6 = (bf16[2,128,128]{2,1,0:T(8,128)(2,1)S(1)}, bf16[2,128,128]{2,1,0:T(8,128)(2,1)S(1)}, u32[]{:S(2)}, u32[]{:S(2)}) collective-permute-start(bf16[2,128,128]{2,1,0:T(8,128)(2,1)S(1)} %get-tuple-element.30), channel_id=1, source_target_pairs={{0,14},{1,15},{2,12},{3,13},{4,10},{5,11},{6,8},{7,9},{8,6},{9,7},... | collective-permute-start | bytes 196616 | tf_op jit(solution)/shard_map/ppermute | solution.py:298
  16.6 5.5 %collective-permute-start.7 = (bf16[2,128,128]{2,1,0:T(8,128)(2,1)S(1)}, bf16[2,128,128]{2,1,0:T(8,128)(2,1)S(1)}, u32[]{:S(2)}, u32[]{:S(2)}) collective-permute-start(bf16[2,128,128]{2,1,0:T(8,128)(2,1)S(1)} %get-tuple-element.31), channel_id=1, source_target_pairs={{0,6},{1,7},{2,4},{3,5},{4,2},{5,3},{6,0},{7,1},{8,14},{9,15},{10,... | collective-permute-start | bytes 196616 | tf_op jit(solution)/shard_map/ppermute | solution.py:298
  25.9 5.2 %collective-permute-start.10 = (bf16[1,128,128]{2,1,0:T(8,128)(2,1)S(1)}, bf16[1,128,128]{2,1,0:T(8,128)(2,1)S(1)}, u32[]{:S(2)}, u32[]{:S(2)}) collective-permute-start(bf16[1,128,128]{2,1,0:T(8,128)(2,1)S(1)} %get-tuple-element.34), channel_id=1, source_target_pairs={{0,13},{1,12},{2,15},{3,14},{4,9},{5,8},{6,11},{7,10},{8,5},{9,4},... | collective-permute-start | bytes 98312 | tf_op jit(solution)/shard_map/ppermute | solution.py:298
  27.0 5.4 %collective-permute-start.9 = (bf16[1,128,128]{2,1,0:T(8,128)(2,1)S(1)}, bf16[1,128,128]{2,1,0:T(8,128)(2,1)S(1)}, u32[]{:S(2)}, u32[]{:S(2)}) collective-permute-start(bf16[1,128,128]{2,1,0:T(8,128)(2,1)S(1)} %get-tuple-element.34), channel_id=1, source_target_pairs={{0,9},{1,8},{2,11},{3,10},{4,13},{5,12},{6,15},{7,14},{8,1},{9,0},... | collective-permute-start | bytes 98312 | tf_op jit(solution)/shard_map/ppermute | solution.py:298
  27.0 5.4 %collective-permute-start.8 = (bf16[1,128,128]{2,1,0:T(8,128)(2,1)S(1)}, bf16[1,128,128]{2,1,0:T(8,128)(2,1)S(1)}, u32[]{:S(2)}, u32[]{:S(2)}) collective-permute-start(bf16[1,128,128]{2,1,0:T(8,128)(2,1)S(1)} %get-tuple-element.34), channel_id=1, source_target_pairs={{0,5},{1,4},{2,7},{3,6},{4,1},{5,0},{6,3},{7,2},{8,13},{9,12},{10,... | collective-permute-start | bytes 98312 | tf_op jit(solution)/shard_map/ppermute | solution.py:298
  32.4 6.2 %collective-permute-start.11 = (bf16[4,128,128]{2,1,0:T(8,128)(2,1)S(1)}, bf16[4,128,128]{2,1,0:T(8,128)(2,1)S(1)}, u32[]{:S(2)}, u32[]{:S(2)}) collective-permute-start(bf16[4,128,128]{2,1,0:T(8,128)(2,1)S(1)} %pad_maximum_fusion), channel_id=1, source_target_pairs={{0,3},{1,2},{2,1},{3,0},{4,7},{5,6},{6,5},{7,4},{8,11},{9,10},{10,... | collective-permute-start | bytes 393224 | tf_op jit(solution)/shard_map/ppermute | solution.py:298
  38.6 1.6 %collective-permute-start.12 = (bf16[8,128,128]{2,1,0:T(8,128)(2,1)S(1)}, bf16[8,128,128]{2,1,0:T(8,128)(2,1)S(1)}, u32[]{:S(2)}, u32[]{:S(2)}) collective-permute-start(bf16[8,128,128]{2,1,0:T(8,128)(2,1)S(1)} %constant_dynamic-update-slice_fusion.refs_0_), channel_id=1, source_target_pairs={{0,1},{1,0},{2,3},{3,2},{4,5},{5,4},{6,7},{7,6},{8,9},{9,8},{10,11... | collective-permute-start | bytes 786440 | tf_op jit(solution)/shard_map/ppermute | solution.py:298

commit v6 on v5

--- a/solution.py
+++ b/solution.py
@@ -15,7 +15,8 @@
 HBM = pl.BlockSpec(memory_space=pltpu.HBM)
 ORDER = (1, 4, 6, 2, 5, 7, 3)
 EARLY = 4
-STEP = 64
+STEP = 32
+WIDE = 2
 LANES = 128
 
 
@@ -165,21 +166,26 @@
 
 
 def add_blocks(total_sum, table_ref, factor_ref, start, stop, step):
-    def body(b, total_sum):
-        base = b * step
-        left = jnp.concatenate([factor_ref[table_ref[0, base + i]] for i in range(step)], axis=1)
+    def add(total_sum, base, blocks):
+        left = jnp.concatenate([factor_ref[table_ref[0, base + i]] for i in range(blocks)], axis=1)
         right = jnp.concatenate(
             [
                 jnp.concatenate(
                     [factor_ref[table_ref[1, base + i]], factor_ref[table_ref[2, base + i]]], axis=1
                 )
-                for i in range(step)
+                for i in range(blocks)
             ],
             axis=0,
         )
         return total_sum + jnp.dot(left, right, preferred_element_type=F32)
 
-    return lax.fori_loop(start, stop, body, total_sum)
+    wide = (stop - start) // WIDE
+    total_sum = lax.fori_loop(
+        0, wide, lambda b, t: add(t, (start + b * WIDE) * step, WIDE * step), total_sum
+    )
+    return lax.fori_loop(
+        start + wide * WIDE, stop, lambda b, t: add(t, b * step, step), total_sum
+    )
 
 
 def steps_of(count, step):

time: 41.4 us -> 41 us (level)
  starting transfers between devices: 16.8 us -> 22 us
  Pallas kernels: 12 us -> 8.18 us
  waiting for transfers between devices: 10.9 us -> 9.12 us
    ppermute x13, starting transfers between devices: 16.8 us -> 22 us  [xor_permute(): return lax.ppermute(array, 'had', [(d, d ^ mask) for d in range(readers)])]
    pallas_call x1, Pallas kernels: 3.89 us -> 1.75 us  [shards(): pl.pallas_call(functools.partial(late_kernel, STEP, root_scale, edge_scal...]
    ppermute x13, waiting for transfers between devices: 10.9 us -> 9.12 us  [xor_permute(): return lax.ppermute(array, 'had', [(d, d ^ mask) for d in range(readers)])]
    pallas_call x1, Pallas kernels: 3.73 us -> 2.03 us  [shards(): pl.pallas_call(functools.partial(early_kernel, STEP, root_scale, early),...]
  transfers between devices with their start and end apart: 13 -> 13, of which waited for: 7 -> 7; matrix products, arithmetic and copies ran while one was open for 2% -> 2% of each run, Pallas kernels for 11% -> 7%
where the time goes in v6:
time: 41 us; the launch traced here: 41.3 us
  starting transfers between devices  22 us (54%)
  waiting for transfers between devices  9.12 us (22%)
  Pallas kernels  8.18 us (20%)
  between operations  1.36 us (3%)
  local copies, waits for them, and re-layouts  0.67 us (2%)
    ppermute x13, starting transfers between devices, xor_permute(): return lax.ppermute(array, 'had', [(d, d ^ mask) for d in range(readers)])  22 us
    ppermute x13, waiting for transfers between devices, xor_permute(): return lax.ppermute(array, 'had', [(d, d ^ mask) for d in range(readers)])  9.12 us
    pallas_call x1, Pallas kernels, shards(): pl.pallas_call(functools.partial(early_kernel, STEP, root_scale, early),...  2.03 us
    pallas_call x1, Pallas kernels, shards(): pl.pallas_call(rotate_pairs_kernel, out_shape=[pltpu.VMEM((half,) + slab,...  2.02 us
    pallas_call x1, Pallas kernels, shards(): pl.pallas_call(functools.partial(late_kernel, STEP, root_scale, edge_scal...  1.75 us
    pallas_call x1, Pallas kernels, shards(): pl.pallas_call(functools.partial(pair_kernel, root_scale, place), out_sha...  1.51 us
    pallas_call x1, Pallas kernels, shards(): pl.pallas_call(functools.partial(plan_kernel, STEP, readers, sinks, early...  0.82 us
  transfers between devices with their start and end apart: 13, of which 7 were waited for; matrix products, arithmetic and copies ran while one was open for 2% of the time, Pallas kernels for 7%

profile of v6, /device:TPU:0, one launch (start us, length us, event | category | flops | bytes accessed | tf_op | source)
XLA Modules:
  0.0 41.3 jit_solution(5949946227471315667)
XLA Ops:
  0.6 2.0 %rotate.1 = (bf16[8,128,128]{2,1,0:T(8,128)(2,1)S(1)}, bf16[8,128,128]{2,1,0:T(8,128)(2,1)S(1)}, bf16[16,128,128]{2,1,0:T(8,128)(2,1)S(1)}, s32[2,512]{1,0:T(2,128)S(1)}, s32[2,512]{1,0:T(2,128)S(1)}) custom-call(s32[1,16]{1,0:T(1,128)} %pick_hbm.1, bf16[16,128,128]{2,1,0:T(8,128)(2,1)} %source_hbm.1, bf16[2,2,128,128]{3,2,1,0:T(8,128)(2,1)} %peram_hbm.1, ...), custom_call_target="tpu_custom_call" | custom-call | tf_op jit(solution)/shard_map/rotate/pallas_call | solution.py:363
  2.7 0.5 %collective-permute-start = (bf16[8,128,128]{2,1,0:T(8,128)(2,1)S(1)}, bf16[8,128,128]{2,1,0:T(8,128)(2,1)S(1)}, u32[]{:S(2)}, u32[]{:S(2)}) collective-permute-start(bf16[8,128,128]{2,1,0:T(8,128)(2,1)S(1)} %get-tuple-element.22), channel_id=1, source_target_pairs={{0,1},{1,0},{2,3},{3,2},{4,5},{5,4},{6,7},{7,6},{8,9},{9,8},{10,11... | collective-permute-start | bytes 786440 | tf_op jit(solution)/shard_map/ppermute | solution.py:304
  3.8 0.8 %plan.1._.table_ref = s32[8,640]{1,0:T(8,128)S(1)} custom-call(s32[1]{0:T(128)S(6)} %copy.17.count_ref, s32[2,512]{1,0:T(2,128)S(1)} %get-tuple-element.18.slot_ref, s32[2,512]{1,0:T(2,128)S(1)} %get-tuple-element.19.sink_ref), custom_call_target="tpu_custom_call" | custom-call | flops 100000000 | tf_op jit(solution)/shard_map/plan/pallas_call | solution.py:388
  4.7 2.6 %collective-permute-start.1 = (bf16[2,128,128]{2,1,0:T(8,128)(2,1)S(1)}, bf16[2,128,128]{2,1,0:T(8,128)(2,1)S(1)}, u32[]{:S(2)}, u32[]{:S(2)}) collective-permute-start(bf16[2,128,128]{2,1,0:T(8,128)(2,1)S(1)} %get-tuple-element.24), channel_id=1, source_target_pairs={{0,2},{1,3},{2,0},{3,1},{4,6},{5,7},{6,4},{7,5},{8,10},{9,11},{10,... | collective-permute-start | bytes 196616 | tf_op jit(solution)/shard_map/ppermute | solution.py:304
  7.3 2.6 %collective-permute-start.2 = (bf16[2,128,128]{2,1,0:T(8,128)(2,1)S(1)}, bf16[2,128,128]{2,1,0:T(8,128)(2,1)S(1)}, u32[]{:S(2)}, u32[]{:S(2)}) collective-permute-start(bf16[2,128,128]{2,1,0:T(8,128)(2,1)S(1)} %get-tuple-element.25), channel_id=1, source_target_pairs={{0,8},{1,9},{2,10},{3,11},{4,12},{5,13},{6,14},{7,15},{8,0},{9,1},... | collective-permute-start | bytes 196616 | tf_op jit(solution)/shard_map/ppermute | solution.py:304
  9.9 1.3 %collective-permute-start.3 = (bf16[2,128,128]{2,1,0:T(8,128)(2,1)S(1)}, bf16[2,128,128]{2,1,0:T(8,128)(2,1)S(1)}, u32[]{:S(2)}, u32[]{:S(2)}) collective-permute-start(bf16[2,128,128]{2,1,0:T(8,128)(2,1)S(1)} %get-tuple-element.26), channel_id=1, source_target_pairs={{0,12},{1,13},{2,14},{3,15},{4,8},{5,9},{6,10},{7,11},{8,4},{9,5},... | collective-permute-start | bytes 196616 | tf_op jit(solution)/shard_map/ppermute | solution.py:304
  11.3 0.2 collective-permute-start.4
  11.5 2.8 %collective-permute-start.5 = (bf16[2,128,128]{2,1,0:T(8,128)(2,1)S(1)}, bf16[2,128,128]{2,1,0:T(8,128)(2,1)S(1)}, u32[]{:S(2)}, u32[]{:S(2)}) collective-permute-start(bf16[2,128,128]{2,1,0:T(8,128)(2,1)S(1)} %get-tuple-element.29), channel_id=1, source_target_pairs={{0,10},{1,11},{2,8},{3,9},{4,14},{5,15},{6,12},{7,13},{8,2},{9,3},... | collective-permute-start | bytes 196616 | tf_op jit(solution)/shard_map/ppermute | solution.py:304
  14.3 2.3 %collective-permute-start.6 = (bf16[2,128,128]{2,1,0:T(8,128)(2,1)S(1)}, bf16[2,128,128]{2,1,0:T(8,128)(2,1)S(1)}, u32[]{:S(2)}, u32[]{:S(2)}) collective-permute-start(bf16[2,128,128]{2,1,0:T(8,128)(2,1)S(1)} %get-tuple-element.30), channel_id=1, source_target_pairs={{0,14},{1,15},{2,12},{3,13},{4,10},{5,11},{6,8},{7,9},{8,6},{9,7},... | collective-permute-start | bytes 196616 | tf_op jit(solution)/shard_map/ppermute | solution.py:304
  16.6 0.1 collective-permute-done.3.refs_3_
  16.7 2.0 %early.1 = (bf16[257,128,128]{2,1,0:T(8,128)(2,1)S(1)}, f32[128,256]{1,0:T(8,128)S(1)}) custom-call(s32[8,640]{1,0:T(8,128)S(1)} %plan.1._.table_ref, bf16[16,128,128]{2,1,0:T(8,128)(2,1)S(1)} %get-tuple-element.20.resident_ref, bf16[2,128,128]{2,1,0:T(8,128)(2,1)S(1)} %get-tuple-element.23.refs_0_, bf16[2,128,128]{2,1,0:T(8,128)(2,1)S(1)} %collective-permute-done.1.refs_1_, ...), custom_call_target="tpu_custom_call" | custom-call | flops 1342177280 | tf_op jit(solution)/shard_map/early/pallas_call | solution.py:409
  18.8 1.7 %collective-permute-done.5.refs_0_ = bf16[2,128,128]{2,1,0:T(8,128)(2,1)S(1)} collective-permute-done((bf16[2,128,128]{2,1,0:T(8,128)(2,1)S(1)}, bf16[2,128,128]{2,1,0:T(8,128)(2,1)S(1)}, u32[]{:S(2)}, u32[]{:S(2)}) %collective-permute-start.5) | collective-permute-done | bytes 65568 | tf_op jit(solution)/shard_map/ppermute | solution.py:304
  20.5 0.8 %collective-permute-done.6.refs_1_ = bf16[2,128,128]{2,1,0:T(8,128)(2,1)S(1)} collective-permute-done((bf16[2,128,128]{2,1,0:T(8,128)(2,1)S(1)}, bf16[2,128,128]{2,1,0:T(8,128)(2,1)S(1)}, u32[]{:S(2)}, u32[]{:S(2)}) %collective-permute-start.6) | collective-permute-done | bytes 65568 | tf_op jit(solution)/shard_map/ppermute | solution.py:304
  21.3 0.7 %collective-permute-done.7.refs_2_ = bf16[2,128,128]{2,1,0:T(8,128)(2,1)S(1)} collective-permute-done((bf16[2,128,128]{2,1,0:T(8,128)(2,1)S(1)}, bf16[2,128,128]{2,1,0:T(8,128)(2,1)S(1)}, u32[]{:S(2)}, u32[]{:S(2)}) %collective-permute-start.7) | collective-permute-done | bytes 65568 | tf_op jit(solution)/shard_map/ppermute | solution.py:304
  22.1 1.8 %edge.1 = (bf16[1,128,128]{2,1,0:T(8,128)(2,1)S(1)}, bf16[257,128,128]{2,1,0:T(8,128)(2,1)S(1)}) custom-call(s32[8,640]{1,0:T(8,128)S(1)} %plan.1._.table_ref, f32[128,256]{1,0:T(8,128)S(1)} %get-tuple-element.28.sum_ref, bf16[16,128,128]{2,1,0:T(8,128)(2,1)S(1)} %get-tuple-element.20.resident_ref, ...), custom_call_target="tpu_custom_call", output_to_operand_aliasing={{1}: (6, {})} | custom-call | tf_op jit(solution)/shard_map/edge/pallas_call | solution.py:427
  23.8 3.6 %collective-permute-start.10 = (bf16[1,128,128]{2,1,0:T(8,128)(2,1)S(1)}, bf16[1,128,128]{2,1,0:T(8,128)(2,1)S(1)}, u32[]{:S(2)}, u32[]{:S(2)}) collective-permute-start(bf16[1,128,128]{2,1,0:T(8,128)(2,1)S(1)} %get-tuple-element.34), channel_id=1, source_target_pairs={{0,13},{1,12},{2,15},{3,14},{4,9},{5,8},{6,11},{7,10},{8,5},{9,4},... | collective-permute-start | bytes 98312 | tf_op jit(solution)/shard_map/ppermute | solution.py:304
  27.5 2.3 %collective-permute-start.8 = (bf16[1,128,128]{2,1,0:T(8,128)(2,1)S(1)}, bf16[1,128,128]{2,1,0:T(8,128)(2,1)S(1)}, u32[]{:S(2)}, u32[]{:S(2)}) collective-permute-start(bf16[1,128,128]{2,1,0:T(8,128)(2,1)S(1)} %get-tuple-element.34), channel_id=1, source_target_pairs={{0,5},{1,4},{2,7},{3,6},{4,1},{5,0},{6,3},{7,2},{8,13},{9,12},{10,... | collective-permute-start | bytes 98312 | tf_op jit(solution)/shard_map/ppermute | solution.py:304
  29.7 2.2 %collective-permute-done.9 = bf16[1,128,128]{2,1,0:T(8,128)(2,1)S(1)} collective-permute-done((bf16[1,128,128]{2,1,0:T(8,128)(2,1)S(1)}, bf16[1,128,128]{2,1,0:T(8,128)(2,1)S(1)}, u32[]{:S(2)}, u32[]{:S(2)}) %collective-permute-start.9) | collective-permute-done | bytes 32800 | tf_op jit(solution)/shard_map/ppermute | solution.py:304
  32.0 2.4 %collective-permute-start.11 = (bf16[4,128,128]{2,1,0:T(8,128)(2,1)S(1)}, bf16[4,128,128]{2,1,0:T(8,128)(2,1)S(1)}, u32[]{:S(2)}, u32[]{:S(2)}) collective-permute-start(bf16[4,128,128]{2,1,0:T(8,128)(2,1)S(1)} %pad_maximum_fusion), channel_id=1, source_target_pairs={{0,3},{1,2},{2,1},{3,0},{4,7},{5,6},{6,5},{7,4},{8,11},{9,10},{10,... | collective-permute-start | bytes 393224 | tf_op jit(solution)/shard_map/ppermute | solution.py:304
  34.5 2.9 %collective-permute-done.11 = bf16[4,128,128]{2,1,0:T(8,128)(2,1)S(1)} collective-permute-done((bf16[4,128,128]{2,1,0:T(8,128)(2,1)S(1)}, bf16[4,128,128]{2,1,0:T(8,128)(2,1)S(1)}, u32[]{:S(2)}, u32[]{:S(2)}) %collective-permute-start.11) | collective-permute-done | bytes 131104 | tf_op jit(solution)/shard_map/ppermute | solution.py:304
  37.4 1.3 %collective-permute-start.12 = (bf16[8,128,128]{2,1,0:T(8,128)(2,1)S(1)}, bf16[8,128,128]{2,1,0:T(8,128)(2,1)S(1)}, u32[]{:S(2)}, u32[]{:S(2)}) collective-permute-start(bf16[8,128,128]{2,1,0:T(8,128)(2,1)S(1)} %constant_dynamic-update-slice_fusion.refs_0_), channel_id=1, source_target_pairs={{0,1},{1,0},{2,3},{3,2},{4,5},{5,4},{6,7},{7,6},{8,9},{9,8},{10,11... | collective-permute-start | bytes 786440 | tf_op jit(solution)/shard_map/ppermute | solution.py:304
  38.6 0.6 %copy.16 = bf16[1,128,128]{2,1,0:T(8,128)(2,1)} copy(bf16[1,128,128]{2,1,0:T(8,128)(2,1)S(1)} %get-tuple-element.34) | data formatting | bytes 65536
  39.3 0.5 %collective-permute-done.12.refs_1_ = bf16[8,128,128]{2,1,0:T(8,128)(2,1)S(1)} collective-permute-done((bf16[8,128,128]{2,1,0:T(8,128)(2,1)S(1)}, bf16[8,128,128]{2,1,0:T(8,128)(2,1)S(1)}, u32[]{:S(2)}, u32[]{:S(2)}) %collective-permute-start.12) | collective-permute-done | bytes 262176 | tf_op jit(solution)/shard_map/ppermute | solution.py:304
  39.8 1.5 %pairs.1 = bf16[8,128,128]{2,1,0:T(8,128)(2,1)} custom-call(s32[2,8]{1,0:T(2,128)S(1)} %bitcast.7, bf16[8,128,128]{2,1,0:T(8,128)(2,1)S(1)} %constant_dynamic-update-slice_fusion.refs_0_, bf16[8,128,128]{2,1,0:T(8,128)(2,1)S(1)} %collective-permute-done.12.refs_1_), custom_call_target="tpu_custom_call" | custom-call | tf_op jit(solution)/shard_map/pairs/pallas_call | solution.py:465
  (17 shorter events, 0.1 us)
Async XLA Ops:
  0.6 39.2 %copy-start = (s32[8,2]{0,1:T(2,128)S(1)}, s32[8,2]{0,1:T(2,128)}, u32[]{:S(2)}) copy-start(s32[8,2]{0,1:T(2,128)} %param.15) | copy-start | bytes 196
  2.7 2.0 %collective-permute-start = (bf16[8,128,128]{2,1,0:T(8,128)(2,1)S(1)}, bf16[8,128,128]{2,1,0:T(8,128)(2,1)S(1)}, u32[]{:S(2)}, u32[]{:S(2)}) collective-permute-start(bf16[8,128,128]{2,1,0:T(8,128)(2,1)S(1)} %get-tuple-element.22), channel_id=1, source_target_pairs={{0,1},{1,0},{2,3},{3,2},{4,5},{5,4},{6,7},{7,6},{8,9},{9,8},{10,11... | collective-permute-start | bytes 786440 | tf_op jit(solution)/shard_map/ppermute | solution.py:304
  4.7 9.5 %collective-permute-start.1 = (bf16[2,128,128]{2,1,0:T(8,128)(2,1)S(1)}, bf16[2,128,128]{2,1,0:T(8,128)(2,1)S(1)}, u32[]{:S(2)}, u32[]{:S(2)}) collective-permute-start(bf16[2,128,128]{2,1,0:T(8,128)(2,1)S(1)} %get-tuple-element.24), channel_id=1, source_target_pairs={{0,2},{1,3},{2,0},{3,1},{4,6},{5,7},{6,4},{7,5},{8,10},{9,11},{10,... | collective-permute-start | bytes 196616 | tf_op jit(solution)/shard_map/ppermute | solution.py:304
  7.3 9.2 %collective-permute-start.2 = (bf16[2,128,128]{2,1,0:T(8,128)(2,1)S(1)}, bf16[2,128,128]{2,1,0:T(8,128)(2,1)S(1)}, u32[]{:S(2)}, u32[]{:S(2)}) collective-permute-start(bf16[2,128,128]{2,1,0:T(8,128)(2,1)S(1)} %get-tuple-element.25), channel_id=1, source_target_pairs={{0,8},{1,9},{2,10},{3,11},{4,12},{5,13},{6,14},{7,15},{8,0},{9,1},... | collective-permute-start | bytes 196616 | tf_op jit(solution)/shard_map/ppermute | solution.py:304
  9.9 6.8 %collective-permute-start.3 = (bf16[2,128,128]{2,1,0:T(8,128)(2,1)S(1)}, bf16[2,128,128]{2,1,0:T(8,128)(2,1)S(1)}, u32[]{:S(2)}, u32[]{:S(2)}) collective-permute-start(bf16[2,128,128]{2,1,0:T(8,128)(2,1)S(1)} %get-tuple-element.26), channel_id=1, source_target_pairs={{0,12},{1,13},{2,14},{3,15},{4,8},{5,9},{6,10},{7,11},{8,4},{9,5},... | collective-permute-start | bytes 196616 | tf_op jit(solution)/shard_map/ppermute | solution.py:304
  11.3 5.4 %collective-permute-start.4 = (bf16[2,128,128]{2,1,0:T(8,128)(2,1)S(1)}, bf16[2,128,128]{2,1,0:T(8,128)(2,1)S(1)}, u32[]{:S(2)}, u32[]{:S(2)}) collective-permute-start(bf16[2,128,128]{2,1,0:T(8,128)(2,1)S(1)} %get-tuple-element.27), channel_id=1, source_target_pairs={{0,4},{1,5},{2,6},{3,7},{4,0},{5,1},{6,2},{7,3},{8,12},{9,13},{10,... | collective-permute-start | bytes 196616 | tf_op jit(solution)/shard_map/ppermute | solution.py:304
  11.5 9.0 %collective-permute-start.5 = (bf16[2,128,128]{2,1,0:T(8,128)(2,1)S(1)}, bf16[2,128,128]{2,1,0:T(8,128)(2,1)S(1)}, u32[]{:S(2)}, u32[]{:S(2)}) collective-permute-start(bf16[2,128,128]{2,1,0:T(8,128)(2,1)S(1)} %get-tuple-element.29), channel_id=1, source_target_pairs={{0,10},{1,11},{2,8},{3,9},{4,14},{5,15},{6,12},{7,13},{8,2},{9,3},... | collective-permute-start | bytes 196616 | tf_op jit(solution)/shard_map/ppermute | solution.py:304
  14.3 7.1 %collective-permute-start.6 = (bf16[2,128,128]{2,1,0:T(8,128)(2,1)S(1)}, bf16[2,128,128]{2,1,0:T(8,128)(2,1)S(1)}, u32[]{:S(2)}, u32[]{:S(2)}) collective-permute-start(bf16[2,128,128]{2,1,0:T(8,128)(2,1)S(1)} %get-tuple-element.30), channel_id=1, source_target_pairs={{0,14},{1,15},{2,12},{3,13},{4,10},{5,11},{6,8},{7,9},{8,6},{9,7},... | collective-permute-start | bytes 196616 | tf_op jit(solution)/shard_map/ppermute | solution.py:304
  16.6 5.5 %collective-permute-start.7 = (bf16[2,128,128]{2,1,0:T(8,128)(2,1)S(1)}, bf16[2,128,128]{2,1,0:T(8,128)(2,1)S(1)}, u32[]{:S(2)}, u32[]{:S(2)}) collective-permute-start(bf16[2,128,128]{2,1,0:T(8,128)(2,1)S(1)} %get-tuple-element.31), channel_id=1, source_target_pairs={{0,6},{1,7},{2,4},{3,5},{4,2},{5,3},{6,0},{7,1},{8,14},{9,15},{10,... | collective-permute-start | bytes 196616 | tf_op jit(solution)/shard_map/ppermute | solution.py:304
  23.8 5.9 %collective-permute-start.10 = (bf16[1,128,128]{2,1,0:T(8,128)(2,1)S(1)}, bf16[1,128,128]{2,1,0:T(8,128)(2,1)S(1)}, u32[]{:S(2)}, u32[]{:S(2)}) collective-permute-start(bf16[1,128,128]{2,1,0:T(8,128)(2,1)S(1)} %get-tuple-element.34), channel_id=1, source_target_pairs={{0,13},{1,12},{2,15},{3,14},{4,9},{5,8},{6,11},{7,10},{8,5},{9,4},... | collective-permute-start | bytes 98312 | tf_op jit(solution)/shard_map/ppermute | solution.py:304
  27.5 4.5 %collective-permute-start.9 = (bf16[1,128,128]{2,1,0:T(8,128)(2,1)S(1)}, bf16[1,128,128]{2,1,0:T(8,128)(2,1)S(1)}, u32[]{:S(2)}, u32[]{:S(2)}) collective-permute-start(bf16[1,128,128]{2,1,0:T(8,128)(2,1)S(1)} %get-tuple-element.34), channel_id=1, source_target_pairs={{0,9},{1,8},{2,11},{3,10},{4,13},{5,12},{6,15},{7,14},{8,1},{9,0},... | collective-permute-start | bytes 98312 | tf_op jit(solution)/shard_map/ppermute | solution.py:304
  27.5 4.5 %collective-permute-start.8 = (bf16[1,128,128]{2,1,0:T(8,128)(2,1)S(1)}, bf16[1,128,128]{2,1,0:T(8,128)(2,1)S(1)}, u32[]{:S(2)}, u32[]{:S(2)}) collective-permute-start(bf16[1,128,128]{2,1,0:T(8,128)(2,1)S(1)} %get-tuple-element.34), channel_id=1, source_target_pairs={{0,5},{1,4},{2,7},{3,6},{4,1},{5,0},{6,3},{7,2},{8,13},{9,12},{10,... | collective-permute-start | bytes 98312 | tf_op jit(solution)/shard_map/ppermute | solution.py:304
  32.0 5.4 %collective-permute-start.11 = (bf16[4,128,128]{2,1,0:T(8,128)(2,1)S(1)}, bf16[4,128,128]{2,1,0:T(8,128)(2,1)S(1)}, u32[]{:S(2)}, u32[]{:S(2)}) collective-permute-start(bf16[4,128,128]{2,1,0:T(8,128)(2,1)S(1)} %pad_maximum_fusion), channel_id=1, source_target_pairs={{0,3},{1,2},{2,1},{3,0},{4,7},{5,6},{6,5},{7,4},{8,11},{9,10},{10,... | collective-permute-start | bytes 393224 | tf_op jit(solution)/shard_map/ppermute | solution.py:304
  37.4 2.4 %collective-permute-start.12 = (bf16[8,128,128]{2,1,0:T(8,128)(2,1)S(1)}, bf16[8,128,128]{2,1,0:T(8,128)(2,1)S(1)}, u32[]{:S(2)}, u32[]{:S(2)}) collective-permute-start(bf16[8,128,128]{2,1,0:T(8,128)(2,1)S(1)} %constant_dynamic-update-slice_fusion.refs_0_), channel_id=1, source_target_pairs={{0,1},{1,0},{2,3},{3,2},{4,5},{5,4},{6,7},{7,6},{8,9},{9,8},{10,11... | collective-permute-start | bytes 786440 | tf_op jit(solution)/shard_map/ppermute | solution.py:304
